TPU v7x, 512 devices: a whole 4x8x8 slice. The times are simulated.
512 devices in a mesh: seq: 32 (over z, x), hidden: 16 (over y, core).
Axes of the slice: x: 4, y: 8, z: 8, core: 2. Of those that a mesh axis runs over, the one named last changes fastest.
Arguments:
- tokens: bfloat16 [8192, 8192], P('seq', 'hidden'), may hold values from -6 to 6
- w_first: bfloat16 [64, 128, 128], P('hidden'), may hold values from -0.5 to 0.5
- w_second: bfloat16 [64, 128, 512], P('hidden'), may hold values from -0.5 to 0.5
- w_third: bfloat16 [64, 512, 128], P('hidden'), may hold values from -0.25 to 0.25
- w_fourth: bfloat16 [64, 128, 128], P('hidden'), may hold values from -0.5 to 0.5
- upstream: bfloat16 [8192, 8192], P('seq', 'hidden'), may hold values from -6 to 6
Outputs:
- output: bfloat16 [8192, 8192], P('seq', 'hidden')
- grad_tokens: bfloat16 [8192, 8192], P('seq', 'hidden')
- grad_first: bfloat16 [64, 128, 128], P('hidden')
- grad_second: bfloat16 [64, 128, 512], P('hidden')
- grad_third: bfloat16 [64, 512, 128], P('hidden')
- grad_fourth: bfloat16 [64, 128, 128], P('hidden')
All inputs are finite; a program needn't handle non-finite values.
Results may differ from a plain program's by a relative error of at most 0.007.
Values may be sent and summed in bfloat16 or wider, within the bound.
No kernel may reach another device: no remote copies, remote signals or barrier semaphores. Data moves between devices by JAX's collectives and lax.ppermute only.
A program may use at most 64 MiB of HBM per device.

v0:
```python
import math

import jax
import jax.numpy as jnp
from jax import lax
from jax.sharding import PartitionSpec as P

ROOT = 0.7978845608
CUBIC = 0.044715


def gelu_value(h):
    inner = ROOT * (h + CUBIC * h * h * h)
    return 0.5 * h * (1.0 + jnp.tanh(inner))


def gelu_slope(h):
    slope = jnp.tanh(ROOT * (h + CUBIC * h * h * h))
    return 0.5 * (1.0 + slope) + 0.5 * h * (1.0 - slope * slope) * ROOT * (
        1.0 + 3.0 * CUBIC * h * h
    )


def deliver(outgoing):
    return lax.all_to_all(outgoing, "hidden", split_axis=0, concat_axis=0, tiled=True)


def permute(z):
    rows, local, width = z.shape
    groups = lax.axis_size("hidden")
    pair = width // (local * groups)
    outgoing = z.reshape(rows, local, groups, local, pair).transpose(2, 0, 3, 1, 4)
    flat_out = outgoing.reshape(groups, rows * local * local * pair)
    incoming = deliver(flat_out).reshape(groups, rows, local, local, pair)
    return incoming.transpose(1, 2, 0, 3, 4).reshape(rows, local, width)


def apply(z, w):
    return jnp.einsum("tbi,bio->tbo", z, w, preferred_element_type=jnp.float32)


def apply_t(z, w):
    return jnp.einsum("tbo,bio->tbi", z, w, preferred_element_type=jnp.float32)


def outer(left, right):
    return jnp.einsum("tbi,tbo->bio", left, right, preferred_element_type=jnp.float32)


def body(tokens, w_first, w_second, w_third, w_fourth, upstream):
    rows = tokens.shape[0]
    local = w_first.shape[0]
    width = w_first.shape[1]
    scale = 1.0 / math.sqrt(rows * lax.axis_size("seq"))
    x = tokens.reshape(rows, local, width)
    first = apply(x, w_first).astype(jnp.bfloat16)
    mixed = permute(first)
    pre = apply(mixed, w_second)
    act = gelu_value(pre).astype(jnp.bfloat16)
    down = apply(act, w_third).astype(jnp.bfloat16)
    back = permute(down)
    output = apply(back, w_fourth).astype(jnp.bfloat16).reshape(rows, local * width)
    upper = upstream.reshape(rows, local, width)
    d_back = apply_t(upper, w_fourth).astype(jnp.bfloat16)
    grad_fourth = outer(back, upper)
    d_down = permute(d_back)
    d_act = apply_t(d_down, w_third)
    grad_third = outer(act, d_down)
    d_pre = (d_act * gelu_slope(pre)).astype(jnp.bfloat16)
    d_mixed = apply_t(d_pre, w_second).astype(jnp.bfloat16)
    grad_second = outer(mixed, d_pre)
    d_first = permute(d_mixed)
    grad_tokens = apply_t(d_first, w_first).astype(jnp.bfloat16).reshape(rows, local * width)
    grad_first = outer(x, d_first)
    summed = lax.psum((grad_first, grad_second, grad_third, grad_fourth), "seq")
    grad_first, grad_second, grad_third, grad_fourth = [
        (item * scale).astype(jnp.bfloat16) for item in summed
    ]
    return (output, grad_tokens, grad_first, grad_second, grad_third, grad_fourth)


def solution(mesh):
    placed = (
        P("seq", "hidden"),
        P("hidden", None, None),
        P("hidden", None, None),
        P("hidden", None, None),
        P("hidden", None, None),
        P("seq", "hidden"),
    )
    return jax.shard_map(
        body,
        mesh=mesh,
        in_specs=placed,
        out_specs=(
            P("seq", "hidden"),
            P("seq", "hidden"),
            P("hidden", None, None),
            P("hidden", None, None),
            P("hidden", None, None),
            P("hidden", None, None),
        ),
        check_vma=False,
    )
```

profile of v0, /device:TPU:56, one launch (start us, length us, event | category | flops | bytes accessed | tf_op | source)
XLA Modules:
  0.0 301.7 jit_solution(17008954510926609318)
XLA Ops:
  8.6 2.0 copy.72
  11.1 3.2 %reduce.2 = bf16[16,8192]{0,1:T(8,128)(2,1)} reduce(bf16[16,1,8192]{0,2,1:T(8,128)(2,1)S(1)} %bitcast.108, bf16[]{:T(256)} %broadcast.30), dimensions={1}, to_apply=%copy.73.reduce_sub_computation | reduce | bytes 524290 | tf_op jit(solution)/shard_map/all_to_all | solution.py:25
  17.2 8.6 %all-to-all-start.2 = ((bf16[16,2,4096]{2,1,0:T(2,128)(2,1)}), bf16[16,2,4096]{2,1,0:T(2,128)(2,1)S(1)}, u32[]{:S(2)}, u32[]{:S(2)}) async-start(bf16[16,2,4096]{2,1,0:T(2,128)(2,1)} %reshape.100), calls=%async_computation.2 | async-start | bytes 524288 | tf_op jit(solution)/shard_map/all_to_all | solution.py:25
  26.1 2.0 copy.59
  28.1 3.2 %reduce = bf16[16,8192]{0,1:T(8,128)(2,1)} reduce(bf16[16,1,8192]{0,2,1:T(8,128)(2,1)S(1)} %bitcast.110, bf16[]{:T(256)} %broadcast.30), dimensions={1}, to_apply=%copy.60.reduce_sub_computation | reduce | bytes 524290 | tf_op jit(solution)/shard_map/all_to_all | solution.py:25
  34.1 7.2 %all-to-all-start = ((bf16[16,2,4096]{2,1,0:T(2,128)(2,1)}), bf16[16,2,4096]{2,1,0:T(2,128)(2,1)}, u32[]{:S(2)}, u32[]{:S(2)}) async-start(bf16[16,2,4096]{2,1,0:T(2,128)(2,1)} %reshape.96), calls=%async_computation | async-start | bytes 524288 | tf_op jit(solution)/shard_map/all_to_all | solution.py:25
  43.5 2.9 copy.75
  46.6 2.8 all-to-all-done
  49.4 2.2 reshape.97
  53.4 2.9 copy.62
  56.4 2.1 multiply_convert_fusion
  62.1 3.2 %reduce.1 = bf16[16,8192]{0,1:T(8,128)(2,1)} reduce(bf16[16,1,8192]{0,2,1:T(8,128)(2,1)S(1)} %bitcast.111, bf16[]{:T(256)} %broadcast.30), dimensions={1}, to_apply=%copy.66.reduce_sub_computation | reduce | bytes 524290 | tf_op jit(solution)/shard_map/all_to_all | solution.py:25
  68.2 6.8 %all-to-all-start.1 = ((bf16[16,2,4096]{2,1,0:T(2,128)(2,1)}), bf16[16,2,4096]{2,1,0:T(2,128)(2,1)S(1)}, u32[]{:S(2)}, u32[]{:S(2)}) async-start(bf16[16,2,4096]{2,1,0:T(2,128)(2,1)} %reshape.98), calls=%async_computation.1 | async-start | bytes 524288 | tf_op jit(solution)/shard_map/all_to_all | solution.py:25
  75.0 3.0 fusion.6
  80.2 4.4 %copy.77 = bf16[256,4,16,4,2]{2,4,1,3,0:T(2,128)(2,1)S(1)} copy(bf16[256,4,16,4,2]{0,4,3,2,1:T(2,128)(2,1)} %reshape.92) | data formatting | bytes 524288 | tf_op jit(solution)/shard_map/reshape | solution.py:32
  84.7 3.2 %reduce.3 = bf16[16,8192]{0,1:T(8,128)(2,1)} reduce(bf16[16,1,8192]{0,2,1:T(8,128)(2,1)S(1)} %bitcast.109, bf16[]{:T(256)} %broadcast.30), dimensions={1}, to_apply=%copy.78.reduce_sub_computation | reduce | bytes 524290 | tf_op jit(solution)/shard_map/all_to_all | solution.py:25
  87.9 2.6 copy.134
  93.8 7.2 %all-to-all-start.3 = ((bf16[16,2,4096]{2,1,0:T(2,128)(2,1)}), bf16[16,2,4096]{2,1,0:T(2,128)(2,1)}, u32[]{:S(2)}, u32[]{:S(2)}) async-start(bf16[16,2,4096]{2,1,0:T(2,128)(2,1)} %reshape.102), calls=%async_computation.3 | async-start | bytes 524288 | tf_op jit(solution)/shard_map/all_to_all | solution.py:25
  102.6 2.2 reshape.99
  106.6 2.9 copy.68
  110.5 2.2 reshape.103
  114.6 2.9 copy.80
  120.7 168.4 %all-reduce.3.cloned.1.call-done = (f32[4,128,128]{1,2,0:T(8,128)}, f32[4,128,512]{2,1,0:T(8,128)}, f32[4,512,128]{2,1,0:T(8,128)}, f32[4,128,128]{1,2,0:T(8,128)}) async-done(((f32[4,128,128]{1,2,0:T(8,128)}, f32[4,128,512]{2,1,0:T(8,128)}, f32[4,512,128]{2,1,0:T(8,128)}, f32[4,128,128]{1,2,0:T(8,128)}), (f32[4,128,128]{1,2,0:T(8,128)}, f32[4,128,512]{2,1,0:T(8,128)}, f32[4,512,128]{2,1,0:T(8,128)}, ...) | async-done | bytes 2621456 | tf_op jit(solution)/shard_map/psum | solution.py:75
  291.8 2.1 multiply_convert_fusion.2
  (68 shorter events, 36.9 us)
Async XLA Ops:
  7.2 49.2 %copy-start = (bf16[4,128,512]{2,1,0:T(8,128)(2,1)S(1)}, bf16[4,128,512]{2,1,0:T(8,128)(2,1)}, u32[]{:S(2)}) copy-start(bf16[4,128,512]{2,1,0:T(8,128)(2,1)} %param.8) | copy-start | bytes 1572868
  14.4 11.3 %copy-start.6 = (bf16[256,512]{1,0:T(8,128)(2,1)S(1)}, bf16[256,512]{1,0:T(8,128)(2,1)}, u32[]{:S(2)}) copy-start(bf16[256,512]{1,0:T(8,128)(2,1)} %param.6) | copy-start | bytes 786436
  14.4 11.4 %copy-start.13 = (bf16[4,128,128]{2,1,0:T(8,128)(2,1)S(1)}, bf16[4,128,128]{2,1,0:T(8,128)(2,1)}, u32[]{:S(2)}) copy-start(bf16[4,128,128]{2,1,0:T(8,128)(2,1)} %param.7) | copy-start | bytes 393220
  17.2 17.0 %all-to-all-start.2 = ((bf16[16,2,4096]{2,1,0:T(2,128)(2,1)}), bf16[16,2,4096]{2,1,0:T(2,128)(2,1)S(1)}, u32[]{:S(2)}, u32[]{:S(2)}) async-start(bf16[16,2,4096]{2,1,0:T(2,128)(2,1)} %reshape.100), calls=%async_computation.2 | async-start | bytes 524288 | tf_op jit(solution)/shard_map/all_to_all | solution.py:25
  34.1 15.2 %all-to-all-start = ((bf16[16,2,4096]{2,1,0:T(2,128)(2,1)}), bf16[16,2,4096]{2,1,0:T(2,128)(2,1)}, u32[]{:S(2)}, u32[]{:S(2)}) async-start(bf16[16,2,4096]{2,1,0:T(2,128)(2,1)} %reshape.96), calls=%async_computation | async-start | bytes 524288 | tf_op jit(solution)/shard_map/all_to_all | solution.py:25
  56.4 3.1 %copy-start.10 = (bf16[4,512,128]{2,1,0:T(8,128)(2,1)S(1)}, bf16[4,512,128]{2,1,0:T(8,128)(2,1)}, u32[]{:S(2)}) copy-start(bf16[4,512,128]{2,1,0:T(8,128)(2,1)} %param.9) | copy-start | bytes 1572868
  58.5 1.0 copy-start.1
  65.3 9.6 %copy-start.11 = (bf16[4,512,128]{2,1,0:T(8,128)(2,1)S(1)}, bf16[4,512,128]{2,1,0:T(8,128)(2,1)}, u32[]{:S(2)}) copy-start(bf16[4,512,128]{2,1,0:T(8,128)(2,1)} %param.9) | copy-start | bytes 1572868
  68.2 25.6 %all-to-all-start.1 = ((bf16[16,2,4096]{2,1,0:T(2,128)(2,1)}), bf16[16,2,4096]{2,1,0:T(2,128)(2,1)S(1)}, u32[]{:S(2)}, u32[]{:S(2)}) async-start(bf16[16,2,4096]{2,1,0:T(2,128)(2,1)} %reshape.98), calls=%async_computation.1 | async-start | bytes 524288 | tf_op jit(solution)/shard_map/all_to_all | solution.py:25
  78.0 1.0 copy-start.3
  87.9 4.5 %copy-start.4 = (bf16[256,4,512]{2,0,1:T(8,128)(2,1)S(1)}, bf16[256,4,512]{2,0,1:T(8,128)(2,1)}, u32[]{:S(2)}) copy-start(bf16[256,4,512]{2,0,1:T(8,128)(2,1)} %copy-done.3) | copy-start | bytes 3145732
  90.5 10.5 %copy-start.2 = (bf16[256,4,512]{2,0,1:T(8,128)(2,1)S(1)}, bf16[256,4,512]{2,0,1:T(8,128)(2,1)}, u32[]{:S(2)}) copy-start(bf16[256,4,512]{2,0,1:T(8,128)(2,1)} %copy-done.1) | copy-start | bytes 3145732
  93.8 7.2 %copy-start.8 = (bf16[16,2,4096]{2,1,0:T(2,128)(2,1)}, bf16[16,2,4096]{2,1,0:T(2,128)(2,1)S(1)}, u32[]{:S(2)}) copy-start(bf16[16,2,4096]{2,1,0:T(2,128)(2,1)S(1)} %all-to-all-done.1) | copy-start | bytes 786436
  93.8 16.8 %all-to-all-start.3 = ((bf16[16,2,4096]{2,1,0:T(2,128)(2,1)}), bf16[16,2,4096]{2,1,0:T(2,128)(2,1)}, u32[]{:S(2)}, u32[]{:S(2)}) async-start(bf16[16,2,4096]{2,1,0:T(2,128)(2,1)} %reshape.102), calls=%async_computation.3 | async-start | bytes 524288 | tf_op jit(solution)/shard_map/all_to_all | solution.py:25
  101.0 188.1 %all-reduce.3.cloned.1.call-start = ((), (), s32[]{:S(2)}) async-start(), calls=%async_computation.4 | async-start | bytes 5242880 | tf_op jit(solution)/shard_map/psum | solution.py:75
  104.7 4.8 %copy-start.5 = (bf16[256,512]{1,0:T(8,128)(2,1)S(1)}, bf16[256,512]{1,0:T(8,128)(2,1)}, u32[]{:S(2)}) copy-start(bf16[256,512]{1,0:T(8,128)(2,1)} %param.11) | copy-start | bytes 786436
  114.6 3.0 copy-start.7
  117.5 1.0 copy-start.12
  289.1 4.9 %copy-start.9 = (f32[4,512,128]{2,1,0:T(8,128)S(1)}, f32[4,512,128]{2,1,0:T(8,128)}, u32[]{:S(2)}) copy-start(f32[4,512,128]{2,1,0:T(8,128)} %get-tuple-element.26) | copy-start | bytes 3145732
Sparse Core Ops, SparseCore 0:
  118.6 170.4 all-reduce.2
where the time goes:
time: 303 us; the launch traced here: 302 us
  waiting for transfers between devices  171 us (56%)
  local copies, waits for them, and re-layouts  56.3 us (19%)
  starting transfers between devices  29.8 us (10%)
  other arithmetic  17.2 us (6%)
  between operations  14.4 us (5%)
  matrix products  12.9 us (4%)
    psum x1, waiting for transfers between devices, body(): summed = lax.psum((grad_first, grad_second, grad_third, grad_fourth), 'seq')  168 us
    all_to_all x4, starting transfers between devices, deliver(): lax.all_to_all(outgoing, 'hidden', split_axis=0, concat_axis=0, tiled=True)  29.8 us
    unnamed x44, local copies, waits for them, and re-layouts  24.8 us
    all_to_all x4, other arithmetic, deliver(): lax.all_to_all(outgoing, 'hidden', split_axis=0, concat_axis=0, tiled=True)  12.9 us
    transpose x4, local copies, waits for them, and re-layouts, permute(): return incoming.transpose(1, 2, 0, 3, 4).reshape(rows, local, width)  11.7 us
    reshape x8, local copies, waits for them, and re-layouts, permute(): z.reshape(rows, local, groups, local, pair).transpose(2, 0, 3, 1, 4)  11.6 us
    all_to_all x5, local copies, waits for them, and re-layouts, deliver(): lax.all_to_all(outgoing, 'hidden', split_axis=0, concat_axis=0, tiled=True)  7.91 us
  transfers between devices with their start and end apart: 5, of which 2 were waited for; matrix products, arithmetic and copies ran while one was open for 14% of the time, Pallas kernels for 0%

commit v1 on v0

v1 whole, which is shorter than its diff:
```python
import functools

import jax
import jax.numpy as jnp
from jax import lax
from jax.experimental import pallas as pl
from jax.experimental.pallas import tpu as pltpu
from jax.sharding import Mesh, PartitionSpec as P

ROOT = 0.7978845608
CUBIC = 0.044715
BF = jnp.bfloat16
F32 = jnp.float32
PAIR = 2
NN = (((1,), (0,)), ((), ()))
NT = (((1,), (1,)), ((), ()))
TN = (((0,), (0,)), ((), ()))
TT = (((0,), (1,)), ((), ()))


def dot(a, b, dims):
    return lax.dot_general(a, b, dims, preferred_element_type=F32)


def call(kernel, outs, *args, flops=0, transcendentals=0):
    moved = sum(a.size * a.dtype.itemsize for a in (*args, *outs))
    return pl.pallas_call(
        kernel,
        out_shape=outs,
        compiler_params=pltpu.CompilerParams(vmem_limit_bytes=24 * 1024 * 1024),
        cost_estimate=pl.CostEstimate(
            flops=int(flops), bytes_accessed=int(moved), transcendentals=int(transcendentals)
        ),
    )(*args)


def shape(*dims, dtype=BF):
    return jax.ShapeDtypeStruct(dims, dtype)


def place(send, slot, low, high, groups):
    width, tokens = low.shape
    per = width // groups
    both = jnp.concatenate(
        [low.reshape(groups, per, tokens), high.reshape(groups, per, tokens)], axis=1
    )
    send[:, slot * 2 * per : (slot + 1) * 2 * per, :] = both.astype(BF)


def enter_kernel(groups, x, dy, w1, w4, send):
    local, width, _ = w1.shape
    half = local // 2
    for k in range(half):
        pair = []
        for b in (2 * k, 2 * k + 1):
            cols = pl.ds(b * width, width)
            pair.append(dot(w1[b], x[:, cols], TT))
        place(send, k, *pair, groups)
    for k in range(half):
        pair = []
        for b in (2 * k, 2 * k + 1):
            cols = pl.ds(b * width, width)
            pair.append(dot(w4[b], dy[:, cols], NT))
        place(send, half + k, *pair, groups)


def source_row(r, local, groups):
    per = local * PAIR
    own, rest = r // (groups * per), r % (groups * per)
    group, rest = rest // per, rest % per
    theirs, one = rest // PAIR, rest % PAIR
    return group * (local * per) + theirs * per + own * PAIR + one


def ready_kernel(groups, w2, w3, order, order_t, w2t, w3t):
    local = w2.shape[0]
    n = order.shape[0]
    source = source_row(lax.broadcasted_iota(jnp.int32, (n, 1), 0), local, groups)
    order[...] = (lax.broadcasted_iota(jnp.int32, (n, n), 1) == source).astype(F32).astype(BF)
    source = source_row(lax.broadcasted_iota(jnp.int32, (1, n), 1), local, groups)
    order_t[...] = (lax.broadcasted_iota(jnp.int32, (n, n), 0) == source).astype(F32).astype(BF)
    for b in range(local):
        w2t[b] = w2[b].T
        w3t[b] = w3[b].T


def middle_kernel(groups, got, order, w2, w3, w2t, w3t, send, mixed, d_down, act, d_pre):
    local, width, _ = w2.shape
    rows = got.shape[1] // 2
    n, tokens = order.shape[0], got.shape[2]
    mixed[...] = dot(order[...], got[:, :rows, :].reshape(n, tokens), NN).astype(BF)
    d_down[...] = dot(order[...], got[:, rows:, :].reshape(n, tokens), NN).astype(BF)
    downs, d_mixeds = [], []
    for b in range(local):
        part = pl.ds(b * width, width)
        h = dot(w2t[b], mixed[part, :], NN)
        squared = h * h
        slope = jnp.tanh(ROOT * (h + CUBIC * (squared * h)))
        act[b] = (0.5 * h * (1.0 + slope)).astype(BF)
        downs.append(dot(w3t[b], act[b], NN))
        d_act = dot(w3[b], d_down[part, :], NN)
        gain = 0.5 * (1.0 + slope) + 0.5 * h * (1.0 - slope * slope) * ROOT * (
            1.0 + 3.0 * CUBIC * squared
        )
        d_pre[b] = (d_act * gain).astype(BF)
        d_mixeds.append(dot(w2[b], d_pre[b], NN))
        if b % 2 == 1:
            place(send, b // 2, *downs, groups)
            place(send, (local + b) // 2, *d_mixeds, groups)
            downs, d_mixeds = [], []


def wide_grads_kernel(mixed, d_down, act, d_pre, grads):
    local, hidden, _ = act.shape
    width = mixed.shape[0] // local
    parts = hidden // width
    for b in range(local):
        rows = pl.ds(b * width, width)
        second = dot(mixed[rows, :], d_pre[b], NT).astype(BF)
        third = dot(act[b], d_down[rows, :], NT).astype(BF)
        for j in range(parts):
            part = slice(j * width, (j + 1) * width)
            grads[j, b * width : (b + 1) * width, :] = second[:, part]
            grads[parts + j, b * width : (b + 1) * width, :] = third[part, :]


def leave_kernel(got, order_t, x, dy, wide, back, d_first, grads):
    rows = got.shape[1] // 2
    n, tokens = order_t.shape[0], got.shape[2]
    parts, high, width = wide.shape
    grads[:, :high, :] = wide[...]
    local = n // width
    back[...] = dot(got[:, :rows, :].reshape(n, tokens), order_t[...], TN).astype(BF)
    d_first[...] = dot(got[:, rows:, :].reshape(n, tokens), order_t[...], TN).astype(BF)
    for b in range(local):
        cols = pl.ds(b * width, width)
        grads[b, high:, :] = dot(x[:, cols], d_first[:, cols], TN).astype(BF)
        grads[local + b, high:, :] = dot(back[:, cols], dy[:, cols], TN).astype(BF)


def outputs_kernel(back, d_first, w1, w4, output, grad_tokens):
    local, width, _ = w1.shape
    for b in range(local):
        cols = pl.ds(b * width, width)
        output[:, cols] = dot(back[:, cols], w4[b], NN).astype(BF)
        grad_tokens[:, cols] = dot(d_first[:, cols], w1[b], NT).astype(BF)


def add_kernel(got, total):
    acc = got[0].astype(F32)
    for k in range(1, got.shape[0]):
        acc = acc + got[k].astype(F32)
    total[...] = acc.astype(BF)


def add_copy_kernel(scale, got, copies):
    acc = got[0].astype(F32)
    for k in range(1, got.shape[0]):
        acc = acc + got[k].astype(F32)
    total = (acc * scale).astype(BF)
    for k in range(copies.shape[0]):
        copies[k] = total


def unpack_kernel(got, first, second, third, fourth):
    local, width, hidden = second.shape
    parts = hidden // width
    for b in range(local):
        rows = slice(b * width, (b + 1) * width)
        for j in range(parts):
            part = slice(j * width, (j + 1) * width)
            second[b, :, part] = got[j, rows, :]
            third[b, part, :] = got[parts + j, rows, :]
        first[b] = got[b, local * width :, :]
        fourth[b] = got[local + b, local * width :, :]


def exchange(value, axes):
    return lax.all_to_all(value, axes, split_axis=0, concat_axis=0, tiled=True)


def body(near, far, all_tokens, tokens, w_first, w_second, w_third, w_fourth, upstream):
    count, wide = tokens.shape
    local, width, hidden = w_second.shape
    groups = lax.axis_size("hidden")
    parts = 2 * hidden // width
    scale = float(all_tokens) ** -0.5
    rows = 2 * local * local * PAIR
    send = call(
        functools.partial(enter_kernel, groups),
        [shape(groups, rows, count)],
        tokens, upstream, w_first, w_fourth,
        flops=4 * count * wide * width,
    )[0]
    got = exchange(send, "hidden")
    order, order_t, w2t, w3t = call(
        functools.partial(ready_kernel, groups),
        [shape(wide, wide), shape(wide, wide), shape(local, hidden, width), shape(local, width, hidden)],
        w_second, w_third,
        flops=2e8,
    )
    send, mixed, d_down, act, d_pre = call(
        functools.partial(middle_kernel, groups),
        [
            shape(groups, rows, count), shape(wide, count), shape(wide, count),
            shape(local, hidden, count), shape(local, hidden, count),
        ],
        got, order, w_second, w_third, w2t, w3t,
        flops=8 * count * wide * hidden, transcendentals=count * local * hidden,
    )
    got = exchange(send, "hidden")
    (grads,) = call(
        wide_grads_kernel, [shape(parts, local * width, width)],
        mixed, d_down, act, d_pre,
        flops=4 * count * wide * hidden,
    )
    back, d_first, grads = call(
        leave_kernel,
        [shape(count, wide), shape(count, wide), shape(parts, (local + 1) * width, width)],
        got, order_t, tokens, upstream, grads,
        flops=4 * count * wide * (wide + width),
    )
    got = exchange(grads, near)
    output, grad_tokens = call(
        outputs_kernel, [shape(count, wide), shape(count, wide)],
        back, d_first, w_first, w_fourth,
        flops=4 * count * wide * width,
    )
    (total,) = call(add_kernel, [shape((local + 1) * width, width)], got, flops=got.size)
    got = lax.all_gather(total, far, axis=0, tiled=False)
    (copies,) = call(
        functools.partial(add_copy_kernel, scale),
        [shape(parts, (local + 1) * width, width)], got, flops=got.size,
    )
    got = exchange(copies, near)
    first, second, third, fourth = call(
        unpack_kernel,
        [shape(*w.shape) for w in (w_first, w_second, w_third, w_fourth)],
        got,
    )
    return output, grad_tokens, first, second, third, fourth


def solution(mesh):
    seq, groups = mesh.shape["seq"], mesh.shape["hidden"]
    near_size = 8
    fine = Mesh(
        mesh.devices.reshape(seq // near_size, near_size, groups), ("far", "near", "hidden")
    )
    rows = P(("far", "near"), "hidden")
    weight = P("hidden", None, None)

    def run(tokens, w_first, w_second, w_third, w_fourth, upstream):
        return jax.shard_map(
            functools.partial(body, "near", "far", tokens.shape[0]),
            mesh=fine,
            in_specs=(rows, weight, weight, weight, weight, rows),
            out_specs=(rows, rows, weight, weight, weight, weight),
            check_vma=False,
        )(tokens, w_first, w_second, w_third, w_fourth, upstream)

    return run
```

time: 303 us -> 133 us (0.44)
  the two profiles are of different devices: /device:TPU:56 before, /device:TPU:1 now
where the time goes in v1:
time: 133 us; the launch traced here: 132 us
  waiting for transfers between devices  44.4 us (33%)
  blocking collectives  43.5 us (33%)
  starting transfers between devices  18.9 us (14%)
  local copies, waits for them, and re-layouts  13.2 us (10%)
  Pallas kernels  11.1 us (8%)
    all_to_all x3, waiting for transfers between devices, exchange(): return lax.all_to_all(value, axes, split_axis=0, concat_axis=0, tiled=True)  44.4 us
    all_to_all x1, blocking collectives, exchange(): return lax.all_to_all(value, axes, split_axis=0, concat_axis=0, tiled=True)  22.1 us
    all_gather x1, blocking collectives, body(): got = lax.all_gather(total, far, axis=0, tiled=False)  21.4 us
    all_to_all x3, starting transfers between devices, exchange(): return lax.all_to_all(value, axes, split_axis=0, concat_axis=0, tiled=True)  18.9 us
    unnamed x40, local copies, waits for them, and re-layouts  13.2 us
    pallas_call x9, Pallas kernels, call(): pl.pallas_call(kernel, out_shape=outs, compiler_params=pltpu.CompilerPara...  11.1 us
  transfers between devices with their start and end apart: 3, of which 3 were waited for; matrix products, arithmetic and copies ran while one was open for 0% of the time, Pallas kernels for 2%

profile of v1, /device:TPU:1, one launch (start us, length us, event | category | flops | bytes accessed | tf_op | source)
XLA Modules:
  0.0 131.9 jit_solution(13922287553074097252)
XLA Ops:
  0.7 1.0 copy-done.4
  1.7 0.9 copy-done.6
  2.6 0.9 copy-done.10
  3.5 0.9 copy-done.12
  4.4 1.1 shard_map.109
  5.5 10.2 %all-to-all-start = ((bf16[16,64,256]{2,1,0:T(8,128)(2,1)}), bf16[16,64,256]{2,1,0:T(8,128)(2,1)S(1)}, u32[]{:S(2)}, u32[]{:S(2)}) async-start(bf16[16,64,256]{2,1,0:T(8,128)(2,1)} %shard_map.109), calls=%async_computation | async-start | bytes 1048576 | tf_op jit(solution)/shard_map/all_to_all | solution.py:179
  15.8 1.0 shard_map.110
  19.2 13.9 %all-to-all-done.got = bf16[16,64,256]{2,1,0:T(8,128)(2,1)S(1)} async-done(((bf16[16,64,256]{2,1,0:T(8,128)(2,1)}), bf16[16,64,256]{2,1,0:T(8,128)(2,1)S(1)}, u32[]{:S(2)}, u32[]{:S(2)}) %all-to-all-start) | async-done | bytes 524320 | tf_op jit(solution)/shard_map/all_to_all | solution.py:179
  33.1 1.0 copy-done.15
  34.2 1.0 copy-done.17
  35.2 3.9 %shard_map.111 = (bf16[16,64,256]{2,1,0:T(8,128)(2,1)}, bf16[512,256]{1,0:T(8,128)(2,1)S(1)}, bf16[512,256]{1,0:T(8,128)(2,1)S(1)}, bf16[4,512,256]{2,1,0:T(8,128)(2,1)S(1)}, bf16[4,512,256]{2,1,0:T(8,128)(2,1)S(1)}) custom-call(bf16[16,64,256]{2,1,0:T(8,128)(2,1)S(1)} %all-to-all-done.got, bf16[512,512]{1,0:T(8,128)(2,1)S(1)} %get-tuple-element.24.order, ...), custom_call_target="tpu_custom_call" | custom-call | flops 536870912 | bytes 6291456 | tf_op jit(solution)/shard_map/pallas_call | solution.py:27
  39.1 1.0 copy-done.2
  40.8 3.5 %all-to-all-start.1 = ((bf16[16,64,256]{2,1,0:T(8,128)(2,1)}), bf16[16,64,256]{2,1,0:T(8,128)(2,1)S(1)}, u32[]{:S(2)}, u32[]{:S(2)}) async-start(bf16[16,64,256]{2,1,0:T(8,128)(2,1)} %get-tuple-element.27), calls=%async_computation.1 | async-start | bytes 1048576 | tf_op jit(solution)/shard_map/all_to_all | solution.py:179
  44.3 1.2 copy-done.3
  45.5 0.9 copy-done.19
  47.1 13.8 %all-to-all-done.1.got = bf16[16,64,256]{2,1,0:T(8,128)(2,1)S(1)} async-done(((bf16[16,64,256]{2,1,0:T(8,128)(2,1)}), bf16[16,64,256]{2,1,0:T(8,128)(2,1)S(1)}, u32[]{:S(2)}, u32[]{:S(2)}) %all-to-all-start.1) | async-done | bytes 524320 | tf_op jit(solution)/shard_map/all_to_all | solution.py:179
  61.0 1.0 copy-done.9
  62.9 22.1 %all_to_all.20.got = bf16[8,640,128]{2,1,0:T(8,128)(2,1)S(1)} all-to-all(bf16[8,640,128]{2,1,0:T(8,128)(2,1)S(1)} %get-tuple-element.37), channel_id=1, replica_groups=mesh['far'=4,'near'=8,'hidden'=16] {'near'}, dimensions={0} | all-to-all | bytes 2621440 | tf_op jit(solution)/shard_map/all_to_all | solution.py:179
  85.1 21.4 %all-gather = bf16[2560,128]{1,0:T(8,128)(2,1)S(1)} all-gather(bf16[640,128]{1,0:T(8,128)(2,1)S(1)} %shard_map.115), channel_id=2, replica_groups=mesh['far'=4,'near'=8,'hidden'=16] {'far'}, dimensions={0}, use_global_device_ids=true | all-gather | bytes 819200 | tf_op jit(solution)/shard_map/all_gather | solution.py:230
  106.5 1.2 shard_map.116
  107.7 5.2 %all-to-all-start.3 = ((bf16[8,640,128]{2,1,0:T(8,128)(2,1)}), bf16[8,640,128]{2,1,0:T(8,128)(2,1)S(1)}, u32[]{:S(2)}, u32[]{:S(2)}) async-start(bf16[8,640,128]{2,1,0:T(8,128)(2,1)} %shard_map.116), calls=%async_computation.3 | async-start | bytes 2621440 | tf_op jit(solution)/shard_map/all_to_all | solution.py:179
  113.0 1.1 shard_map.114
  114.0 16.7 %all-to-all-done.3.got = bf16[8,640,128]{2,1,0:T(8,128)(2,1)S(1)} async-done(((bf16[8,640,128]{2,1,0:T(8,128)(2,1)}), bf16[8,640,128]{2,1,0:T(8,128)(2,1)S(1)}, u32[]{:S(2)}, u32[]{:S(2)}) %all-to-all-start.3) | async-done | bytes 1310752 | tf_op jit(solution)/shard_map/all_to_all | solution.py:179
  130.7 1.2 shard_map.117
  (33 shorter events, 4.9 us)
Async XLA Ops:
  0.6 15.1 %copy-start.1 = (bf16[4,512,128]{2,1,0:T(8,128)(2,1)S(1)}, bf16[4,512,128]{2,1,0:T(8,128)(2,1)}, u32[]{:S(2)}) copy-start(bf16[4,512,128]{2,1,0:T(8,128)(2,1)} %w3.3) | copy-start | bytes 1572868
  0.6 1.0 copy-start.4
  1.7 0.9 copy-start.6
  2.6 0.9 copy-start.10
  3.5 0.9 copy-start.12
  4.4 11.4 %copy-start = (bf16[4,128,512]{2,1,0:T(8,128)(2,1)S(1)}, bf16[4,128,512]{2,1,0:T(8,128)(2,1)}, u32[]{:S(2)}) copy-start(bf16[4,128,512]{2,1,0:T(8,128)(2,1)} %w2.3) | copy-start | bytes 1572868
  5.5 27.6 %all-to-all-start = ((bf16[16,64,256]{2,1,0:T(8,128)(2,1)}), bf16[16,64,256]{2,1,0:T(8,128)(2,1)S(1)}, u32[]{:S(2)}, u32[]{:S(2)}) async-start(bf16[16,64,256]{2,1,0:T(8,128)(2,1)} %shard_map.109), calls=%async_computation | async-start | bytes 1048576 | tf_op jit(solution)/shard_map/all_to_all | solution.py:179
  16.8 0.8 copy-start.8
  17.6 0.8 copy-start.14
  18.4 0.8 copy-start.16
  33.1 1.0 copy-start.15
  34.2 1.0 copy-start.17
  39.1 1.0 copy-start.2
  40.1 0.7 copy-start.18
  40.8 20.2 %all-to-all-start.1 = ((bf16[16,64,256]{2,1,0:T(8,128)(2,1)}), bf16[16,64,256]{2,1,0:T(8,128)(2,1)S(1)}, u32[]{:S(2)}, u32[]{:S(2)}) async-start(bf16[16,64,256]{2,1,0:T(8,128)(2,1)} %get-tuple-element.27), calls=%async_computation.1 | async-start | bytes 1048576 | tf_op jit(solution)/shard_map/all_to_all | solution.py:179
  44.2 1.2 copy-start.3
  45.5 0.9 copy-start.19
  46.4 14.5 %copy-start.5 = (bf16[256,512]{1,0:T(8,128)(2,1)S(1)}, bf16[256,512]{1,0:T(8,128)(2,1)}, u32[]{:S(2)}) copy-start(bf16[256,512]{1,0:T(8,128)(2,1)} %x.3) | copy-start | bytes 786436
  46.4 14.5 %copy-start.7 = (bf16[256,512]{1,0:T(8,128)(2,1)S(1)}, bf16[256,512]{1,0:T(8,128)(2,1)}, u32[]{:S(2)}) copy-start(bf16[256,512]{1,0:T(8,128)(2,1)} %dy.3) | copy-start | bytes 786436
  61.0 1.0 copy-start.9
  107.7 5.2 %copy-start.11 = (bf16[4,128,128]{2,1,0:T(8,128)(2,1)S(1)}, bf16[4,128,128]{2,1,0:T(8,128)(2,1)}, u32[]{:S(2)}) copy-start(bf16[4,128,128]{2,1,0:T(8,128)(2,1)} %w1.3) | copy-start | bytes 393220
  107.7 5.2 %copy-start.13 = (bf16[4,128,128]{2,1,0:T(8,128)(2,1)S(1)}, bf16[4,128,128]{2,1,0:T(8,128)(2,1)}, u32[]{:S(2)}) copy-start(bf16[4,128,128]{2,1,0:T(8,128)(2,1)} %w4.3) | copy-start | bytes 393220
  107.7 23.0 %all-to-all-start.3 = ((bf16[8,640,128]{2,1,0:T(8,128)(2,1)}), bf16[8,640,128]{2,1,0:T(8,128)(2,1)S(1)}, u32[]{:S(2)}, u32[]{:S(2)}) async-start(bf16[8,640,128]{2,1,0:T(8,128)(2,1)} %shard_map.116), calls=%async_computation.3 | async-start | bytes 2621440 | tf_op jit(solution)/shard_map/all_to_all | solution.py:179

commit v2 on v1

v2 whole, which is shorter than its diff:
```python
import functools

import jax
import jax.numpy as jnp
from jax import lax
from jax.experimental import pallas as pl
from jax.experimental.pallas import tpu as pltpu
from jax.sharding import Mesh, PartitionSpec as P

ROOT = 0.7978845608
CUBIC = 0.044715
BF = jnp.bfloat16
F32 = jnp.float32
PAIR = 2
NN = (((1,), (0,)), ((), ()))
NT = (((1,), (1,)), ((), ()))
TN = (((0,), (0,)), ((), ()))
TT = (((0,), (1,)), ((), ()))


def dot(a, b, dims):
    return lax.dot_general(a, b, dims, preferred_element_type=F32)


def call(kernel, outs, *args, flops=0, transcendentals=0, vmem=24 << 20, **more):
    moved = sum(a.size * a.dtype.itemsize for a in (*args, *outs))
    return pl.pallas_call(
        kernel,
        out_shape=outs,
        compiler_params=pltpu.CompilerParams(vmem_limit_bytes=vmem),
        cost_estimate=pl.CostEstimate(
            flops=int(flops), bytes_accessed=int(moved), transcendentals=int(transcendentals)
        ),
        **more,
    )(*args)


def shape(*dims, dtype=BF):
    return jax.ShapeDtypeStruct(dims, dtype)


def place(send, slot, low, high, groups):
    width, tokens = low.shape
    per = width // groups
    both = jnp.concatenate(
        [low.reshape(groups, per, tokens), high.reshape(groups, per, tokens)], axis=1
    )
    send[:, slot * 2 * per : (slot + 1) * 2 * per, :] = both.astype(BF)


def enter_kernel(groups, x_in, w1_in, dy_in, w4_in, send, x, w1, dy, w4, arrived):
    copies = [
        pltpu.make_async_copy(source, target, arrived.at[k])
        for k, (source, target) in enumerate(((x_in, x), (w1_in, w1), (dy_in, dy), (w4_in, w4)))
    ]
    for copy in copies:
        copy.start()
    local, width, _ = w1.shape
    half = local // 2
    copies[0].wait()
    copies[1].wait()
    for k in range(half):
        pair = []
        for b in (2 * k, 2 * k + 1):
            cols = pl.ds(b * width, width)
            pair.append(dot(w1[b], x[:, cols], TT))
        place(send, k, *pair, groups)
    copies[2].wait()
    copies[3].wait()
    for k in range(half):
        pair = []
        for b in (2 * k, 2 * k + 1):
            cols = pl.ds(b * width, width)
            pair.append(dot(w4[b], dy[:, cols], NT))
        place(send, half + k, *pair, groups)


def gather_blocks(got, low, local, out):
    groups, _, tokens = got.shape
    per = local * PAIR
    held = local * per
    n = out.shape[0] // local
    some = n // held
    r = lax.broadcasted_iota(jnp.int32, (n, 1), 0)
    own, group = r // (some * per), (r // per) % some
    theirs, one = (r // PAIR) % local, r % PAIR
    source = group * held + theirs * per + own * PAIR + one
    order = (lax.broadcasted_iota(jnp.int32, (n, n), 1) == source).astype(F32).astype(BF)
    for k in range(groups // some):
        rows = got[k * some : (k + 1) * some, low : low + held, :].reshape(n, tokens)
        moved = dot(order, rows, NN).astype(BF)
        for b in range(local):
            at = b * n + k * some * per
            out[at : at + some * per, :] = moved[b * some * per : (b + 1) * some * per, :]


def middle_kernel(groups, got, w2, w3, send, grads, mixed, d_down):
    local, width, hidden = w2.shape
    parts = hidden // width
    gather_blocks(got, 0, local, mixed)
    gather_blocks(got, got.shape[1] // 2, local, d_down)
    downs, d_mixeds = [], []
    for b in range(local):
        rows = pl.ds(b * width, width)
        h = dot(w2[b], mixed[rows, :], TN)
        squared = h * h
        half = 0.5 + 0.5 * jnp.tanh(h * (ROOT + (ROOT * CUBIC) * squared))
        act = (h * half).astype(BF)
        gain = half + h * (half - half * half) * (2.0 * ROOT + (6.0 * ROOT * CUBIC) * squared)
        d_act = dot(w3[b], d_down[rows, :], NN)
        d_pre = (d_act * gain).astype(BF)
        downs.append(dot(w3[b], act, TN))
        d_mixeds.append(dot(w2[b], d_pre, NN))
        if b % 2 == 1:
            place(send, b // 2, *downs, groups)
            place(send, (local + b) // 2, *d_mixeds, groups)
            downs, d_mixeds = [], []
        second = dot(mixed[rows, :], d_pre, NT).astype(BF)
        third = dot(act, d_down[rows, :], NT).astype(BF)
        for j in range(parts):
            part = slice(j * width, (j + 1) * width)
            grads[j, b * width : (b + 1) * width, :] = second[:, part]
            grads[parts + j, b * width : (b + 1) * width, :] = third[part, :]


def leave_kernel(got, x, dy, wide, back, d_first, grads):
    parts, high, width = wide.shape
    local = high // width
    grads[:, :high, :] = wide[...]
    gather_blocks(got, 0, local, back)
    gather_blocks(got, got.shape[1] // 2, local, d_first)
    for b in range(local):
        rows = pl.ds(b * width, width)
        grads[b, high:, :] = dot(x[:, rows], d_first[rows, :], TT).astype(BF)
        grads[local + b, high:, :] = dot(back[rows, :], dy[:, rows], NN).astype(BF)


def outputs_kernel(back, d_first, w1, w4, output, grad_tokens):
    local, width, _ = w1.shape
    for b in range(local):
        cols = pl.ds(b * width, width)
        output[:, cols] = dot(back[cols, :], w4[b], TN).astype(BF)
        grad_tokens[:, cols] = dot(d_first[cols, :], w1[b], TT).astype(BF)


def add_kernel(got, total):
    acc = got[0].astype(F32)
    for k in range(1, got.shape[0]):
        acc = acc + got[k].astype(F32)
    total[...] = acc.astype(BF)


def add_copy_kernel(scale, got, copies):
    acc = got[0].astype(F32)
    for k in range(1, got.shape[0]):
        acc = acc + got[k].astype(F32)
    total = (acc * scale).astype(BF)
    for k in range(copies.shape[0]):
        copies[k] = total


def unpack_kernel(got, first, second, third, fourth):
    local, width, hidden = second.shape
    parts = hidden // width
    for b in range(local):
        rows = slice(b * width, (b + 1) * width)
        for j in range(parts):
            part = slice(j * width, (j + 1) * width)
            second[b, :, part] = got[j, rows, :]
            third[b, part, :] = got[parts + j, rows, :]
        first[b] = got[b, local * width :, :]
        fourth[b] = got[local + b, local * width :, :]


def exchange(value, axes):
    return lax.all_to_all(value, axes, split_axis=0, concat_axis=0, tiled=True)


def body(near, far, all_tokens, tokens, w_first, w_second, w_third, w_fourth, upstream):
    count, wide = tokens.shape
    local, width, hidden = w_second.shape
    groups = lax.axis_size("hidden")
    parts = 2 * hidden // width
    scale = float(all_tokens) ** -0.5
    rows = 2 * local * local * PAIR
    entering = (tokens, w_first, upstream, w_fourth)
    (send,) = call(
        functools.partial(enter_kernel, groups),
        [shape(groups, rows, count)],
        *entering,
        flops=4 * count * wide * width, vmem=60 << 20,
        in_specs=[pl.BlockSpec(memory_space=pltpu.HBM)] * 4,
        scratch_shapes=[pltpu.VMEM(a.shape, BF) for a in entering]
        + [pltpu.SemaphoreType.DMA((4,))],
    )
    got = exchange(send, "hidden")
    send, grads = call(
        functools.partial(middle_kernel, groups),
        [shape(groups, rows, count), shape(parts, local * width, width)],
        got, w_second, w_third,
        flops=12 * count * wide * hidden, transcendentals=count * local * hidden,
        scratch_shapes=[pltpu.VMEM((wide, count), BF)] * 2,
    )
    got = exchange(send, "hidden")
    back, d_first, grads = call(
        leave_kernel,
        [shape(wide, count), shape(wide, count), shape(parts, (local + 1) * width, width)],
        got, tokens, upstream, grads,
        flops=8 * count * wide * width,
    )
    got = exchange(grads, near)
    output, grad_tokens = call(
        outputs_kernel, [shape(count, wide), shape(count, wide)],
        back, d_first, w_first, w_fourth,
        flops=4 * count * wide * width,
    )
    (total,) = call(add_kernel, [shape((local + 1) * width, width)], got, flops=got.size)
    got = lax.all_gather(total, far, axis=0, tiled=False)
    (copies,) = call(
        functools.partial(add_copy_kernel, scale),
        [shape(parts, (local + 1) * width, width)], got, flops=got.size,
    )
    got = exchange(copies, near)
    first, second, third, fourth = call(
        unpack_kernel,
        [shape(*w.shape) for w in (w_first, w_second, w_third, w_fourth)],
        got,
    )
    return output, grad_tokens, first, second, third, fourth


def solution(mesh):
    seq, groups = mesh.shape["seq"], mesh.shape["hidden"]
    near_size = 8
    fine = Mesh(
        mesh.devices.reshape(seq // near_size, near_size, groups), ("far", "near", "hidden")
    )
    rows = P(("far", "near"), "hidden")
    weight = P("hidden", None, None)

    def run(tokens, w_first, w_second, w_third, w_fourth, upstream):
        return jax.shard_map(
            functools.partial(body, "near", "far", tokens.shape[0]),
            mesh=fine,
            in_specs=(rows, weight, weight, weight, weight, rows),
            out_specs=(rows, rows, weight, weight, weight, weight),
            check_vma=False,
        )(tokens, w_first, w_second, w_third, w_fourth, upstream)

    return run
```

time: 133 us -> 123 us (0.925)
  blocking collectives: 43.5 us -> 91.6 us
  waiting for transfers between devices: 44.4 us -> 16.6 us
  starting transfers between devices: 18.9 us -> 4.51 us
  local copies, waits for them, and re-layouts: 13.2 us -> 0.02 us
  Pallas kernels: 11.1 us -> 9.26 us
    all_to_all x1 -> x3, blocking collectives: 22.1 us -> 69.6 us  [exchange(): return lax.all_to_all(value, axes, split_axis=0, concat_axis=0, tiled=True)]
    all_to_all x3 -> x1, waiting for transfers between devices: 44.4 us -> 16.6 us  [exchange(): return lax.all_to_all(value, axes, split_axis=0, concat_axis=0, tiled=True)]
    all_to_all x3 -> x1, starting transfers between devices: 18.9 us -> 4.51 us  [exchange(): return lax.all_to_all(value, axes, split_axis=0, concat_axis=0, tiled=True)]
    unnamed x40 -> x12, local copies, waits for them, and re-layouts: 13.2 us -> 0.02 us
    pallas_call x9 -> x7, Pallas kernels: 11.1 us -> 9.26 us  [call(): pl.pallas_call(kernel, out_shape=outs, compiler_params=pltpu.CompilerPara...]
  transfers between devices with their start and end apart: 3 -> 1, of which waited for: 3 -> 1; matrix products, arithmetic and copies ran while one was open for 0% -> 0% of each run, Pallas kernels for 2% -> 1%
where the time goes in v2:
time: 123 us
  blocking collectives  91.6 us (74%)
  waiting for transfers between devices  16.6 us (13%)
  Pallas kernels  9.26 us (8%)
  starting transfers between devices  4.51 us (4%)
    all_to_all x3, blocking collectives, exchange(): return lax.all_to_all(value, axes, split_axis=0, concat_axis=0, tiled=True)  69.6 us
    all_gather x1, blocking collectives, body(): got = lax.all_gather(total, far, axis=0, tiled=False)  22 us
    all_to_all x1, waiting for transfers between devices, exchange(): return lax.all_to_all(value, axes, split_axis=0, concat_axis=0, tiled=True)  16.6 us
    pallas_call x7, Pallas kernels, call(): pl.pallas_call(kernel, out_shape=outs, compiler_params=pltpu.CompilerPara...  9.26 us
    all_to_all x1, starting transfers between devices, exchange(): return lax.all_to_all(value, axes, split_axis=0, concat_axis=0, tiled=True)  4.51 us
  transfers between devices with their start and end apart: 1, of which 1 were waited for; matrix products, arithmetic and copies ran while one was open for 0% of the time, Pallas kernels for 1%

profile of v2, /device:TPU:1, one launch (start us, length us, event | category | flops | bytes accessed | tf_op | source)
XLA Modules:
  0.0 122.7 jit_solution(16906243498237570377)
XLA Ops:
  0.6 0.0 copy-start.5
  0.6 0.0 copy-start.4
  0.7 2.4 %shard_map.109 = bf16[16,64,256]{2,1,0:T(8,128)(2,1)} custom-call(bf16[256,512]{1,0:T(8,128)(2,1)} %x.1, bf16[4,128,128]{2,1,0:T(8,128)(2,1)} %w1.1, bf16[256,512]{1,0:T(8,128)(2,1)} %dy.1, bf16[4,128,128]{2,1,0:T(8,128)(2,1)} %w4.1), custom_call_target="tpu_custom_call" | custom-call | flops 67108864 | bytes 1310720 | tf_op jit(solution)/shard_map/pallas_call | solution.py:27
  3.0 27.6 %all_to_all.20.got = bf16[16,64,256]{2,1,0:T(8,128)(2,1)S(1)} all-to-all(bf16[16,64,256]{2,1,0:T(8,128)(2,1)} %shard_map.109), channel_id=1, replica_groups=mesh['far'=4,'near'=8,'hidden'=16] {'hidden'}, dimensions={0} | all-to-all | bytes 1048576 | tf_op jit(solution)/shard_map/all_to_all | solution.py:176
  30.6 0.0 copy-done.5
  30.6 0.0 copy-done.4
  30.6 0.0 copy-start
  30.6 0.0 copy-start.1
  30.6 2.6 %shard_map.110 = (bf16[16,64,256]{2,1,0:T(8,128)(2,1)S(1)}, bf16[8,512,128]{2,1,0:T(8,128)(2,1)S(1)}) custom-call(bf16[16,64,256]{2,1,0:T(8,128)(2,1)S(1)} %all_to_all.20.got, bf16[4,128,512]{2,1,0:T(8,128)(2,1)S(1)} %copy-done.4, bf16[4,512,128]{2,1,0:T(8,128)(2,1)S(1)} %copy-done.5), custom_call_target="tpu_custom_call" | custom-call | flops 805306368 | bytes 3145728 | tf_op jit(solution)/shard_map/pallas_call | solution.py:27
  33.2 20.0 %all_to_all.21.got = bf16[16,64,256]{2,1,0:T(8,128)(2,1)S(1)} all-to-all(bf16[16,64,256]{2,1,0:T(8,128)(2,1)S(1)} %get-tuple-element.17), channel_id=1, replica_groups=mesh['far'=4,'near'=8,'hidden'=16] {'hidden'}, dimensions={0} | all-to-all | bytes 1048576 | tf_op jit(solution)/shard_map/all_to_all | solution.py:176
  53.3 0.0 copy-done
  53.3 0.0 copy-done.1
  53.3 0.6 shard_map.111
  53.9 22.0 %all_to_all.22.got = bf16[8,640,128]{2,1,0:T(8,128)(2,1)S(1)} all-to-all(bf16[8,640,128]{2,1,0:T(8,128)(2,1)S(1)} %get-tuple-element.23), channel_id=1, replica_groups=mesh['far'=4,'near'=8,'hidden'=16] {'near'}, dimensions={0} | all-to-all | bytes 2621440 | tf_op jit(solution)/shard_map/all_to_all | solution.py:176
  75.9 0.2 shard_map.113
  76.1 22.0 %all-gather = bf16[2560,128]{1,0:T(8,128)(2,1)S(1)} all-gather(bf16[640,128]{1,0:T(8,128)(2,1)S(1)} %shard_map.113), channel_id=2, replica_groups=mesh['far'=4,'near'=8,'hidden'=16] {'far'}, dimensions={0}, use_global_device_ids=true | all-gather | bytes 819200 | tf_op jit(solution)/shard_map/all_gather | solution.py:218
  98.0 1.2 shard_map.114
  99.2 0.0 copy-start.2
  99.2 4.5 %all-to-all-start.3 = ((bf16[8,640,128]{2,1,0:T(8,128)(2,1)}), bf16[8,640,128]{2,1,0:T(8,128)(2,1)S(1)}, u32[]{:S(2)}, u32[]{:S(2)}) async-start(bf16[8,640,128]{2,1,0:T(8,128)(2,1)} %shard_map.114), calls=%async_computation.3 | async-start | bytes 2621440 | tf_op jit(solution)/shard_map/all_to_all | solution.py:176
  103.7 0.0 copy-done.2
  103.8 0.0 copy-done.3
  103.8 1.1 shard_map.112
  104.9 16.6 %all-to-all-done.3.got = bf16[8,640,128]{2,1,0:T(8,128)(2,1)S(1)} async-done(((bf16[8,640,128]{2,1,0:T(8,128)(2,1)}), bf16[8,640,128]{2,1,0:T(8,128)(2,1)S(1)}, u32[]{:S(2)}, u32[]{:S(2)}) %all-to-all-start.3) | async-done | bytes 1310752 | tf_op jit(solution)/shard_map/all_to_all | solution.py:176
  121.5 1.2 shard_map.115
  (1 shorter events, 0.0 us)
Async XLA Ops:
  0.6 30.0 %copy-start.5 = (bf16[4,512,128]{2,1,0:T(8,128)(2,1)S(1)}, bf16[4,512,128]{2,1,0:T(8,128)(2,1)}, u32[]{:S(2)}) copy-start(bf16[4,512,128]{2,1,0:T(8,128)(2,1)} %w3.1) | copy-start | bytes 1572868
  0.6 30.0 %copy-start.4 = (bf16[4,128,512]{2,1,0:T(8,128)(2,1)S(1)}, bf16[4,128,512]{2,1,0:T(8,128)(2,1)}, u32[]{:S(2)}) copy-start(bf16[4,128,512]{2,1,0:T(8,128)(2,1)} %w2.1) | copy-start | bytes 1572868
  30.6 22.6 %copy-start = (bf16[256,512]{1,0:T(8,128)(2,1)S(1)}, bf16[256,512]{1,0:T(8,128)(2,1)}, u32[]{:S(2)}) copy-start(bf16[256,512]{1,0:T(8,128)(2,1)} %x.1) | copy-start | bytes 786436
  30.6 22.6 %copy-start.1 = (bf16[256,512]{1,0:T(8,128)(2,1)S(1)}, bf16[256,512]{1,0:T(8,128)(2,1)}, u32[]{:S(2)}) copy-start(bf16[256,512]{1,0:T(8,128)(2,1)} %dy.1) | copy-start | bytes 786436
  99.2 4.5 %copy-start.2 = (bf16[4,128,128]{2,1,0:T(8,128)(2,1)S(1)}, bf16[4,128,128]{2,1,0:T(8,128)(2,1)}, u32[]{:S(2)}) copy-start(bf16[4,128,128]{2,1,0:T(8,128)(2,1)} %w1.1) | copy-start | bytes 393220
  99.2 4.5 %copy-start.3 = (bf16[4,128,128]{2,1,0:T(8,128)(2,1)S(1)}, bf16[4,128,128]{2,1,0:T(8,128)(2,1)}, u32[]{:S(2)}) copy-start(bf16[4,128,128]{2,1,0:T(8,128)(2,1)} %w4.1) | copy-start | bytes 393220
  99.2 22.3 %all-to-all-start.3 = ((bf16[8,640,128]{2,1,0:T(8,128)(2,1)}), bf16[8,640,128]{2,1,0:T(8,128)(2,1)S(1)}, u32[]{:S(2)}, u32[]{:S(2)}) async-start(bf16[8,640,128]{2,1,0:T(8,128)(2,1)} %shard_map.114), calls=%async_computation.3 | async-start | bytes 2621440 | tf_op jit(solution)/shard_map/all_to_all | solution.py:176

commit v3 on v2

--- a/solution.py
+++ b/solution.py
@@ -48,7 +48,7 @@
     send[:, slot * 2 * per : (slot + 1) * 2 * per, :] = both.astype(BF)
 
 
-def enter_kernel(groups, x_in, w1_in, dy_in, w4_in, send, x, w1, dy, w4, arrived):
+def enter_kernel(groups, x_in, w1_in, dy_in, w4_in, out, x, w1, dy, w4, send, arrived, left):
     copies = [
         pltpu.make_async_copy(source, target, arrived.at[k])
         for k, (source, target) in enumerate(((x_in, x), (w1_in, w1), (dy_in, dy), (w4_in, w4)))
@@ -56,23 +56,27 @@
     for copy in copies:
         copy.start()
     local, width, _ = w1.shape
-    half = local // 2
-    copies[0].wait()
-    copies[1].wait()
-    for k in range(half):
+    slots = local // 2
+    per = send.shape[1] // (2 * slots)
+    leaving = []
+    for k in range(2 * slots):
+        if k % slots == 0:
+            copies[k // slots * 2].wait()
+            copies[k // slots * 2 + 1].wait()
         pair = []
-        for b in (2 * k, 2 * k + 1):
+        for b in (2 * (k % slots), 2 * (k % slots) + 1):
             cols = pl.ds(b * width, width)
-            pair.append(dot(w1[b], x[:, cols], TT))
+            if k < slots:
+                pair.append(dot(w1[b], x[:, cols], TT))
+            else:
+                pair.append(dot(w4[b], dy[:, cols], NT))
         place(send, k, *pair, groups)
-    copies[2].wait()
-    copies[3].wait()
-    for k in range(half):
-        pair = []
-        for b in (2 * k, 2 * k + 1):
-            cols = pl.ds(b * width, width)
-            pair.append(dot(w4[b], dy[:, cols], NT))
-        place(send, half + k, *pair, groups)
+        rows = pl.ds(k * per, per)
+        copy = pltpu.make_async_copy(send.at[:, rows, :], out.at[:, rows, :], left.at[k])
+        copy.start()
+        leaving.append(copy)
+    for copy in leaving:
+        copy.wait()
 
 
 def gather_blocks(got, low, local, out):
@@ -150,26 +154,38 @@
     total[...] = acc.astype(BF)
 
 
-def add_copy_kernel(scale, got, copies):
+def add_copy_kernel(scale, got, copies, total, left):
     acc = got[0].astype(F32)
     for k in range(1, got.shape[0]):
         acc = acc + got[k].astype(F32)
-    total = (acc * scale).astype(BF)
-    for k in range(copies.shape[0]):
-        copies[k] = total
-
-
-def unpack_kernel(got, first, second, third, fourth):
+    total[...] = (acc * scale).astype(BF)
+    leaving = [
+        pltpu.make_async_copy(total, copies.at[k], left.at[k]) for k in range(copies.shape[0])
+    ]
+    for copy in leaving:
+        copy.start()
+    for copy in leaving:
+        copy.wait()
+
+
+def unpack_kernel(got, first, second, third, fourth, done):
     local, width, hidden = second.shape
     parts = hidden // width
-    for b in range(local):
-        rows = slice(b * width, (b + 1) * width)
-        for j in range(parts):
-            part = slice(j * width, (j + 1) * width)
-            second[b, :, part] = got[j, rows, :]
-            third[b, part, :] = got[parts + j, rows, :]
-        first[b] = got[b, local * width :, :]
-        fourth[b] = got[local + b, local * width :, :]
+    pairs = []
+    for j in range(parts):
+        part = pl.ds(j * width, width)
+        pairs.append((got.at[j, :local], second.at[:, :, part]))
+        pairs.append((got.at[parts + j, :local], third.at[:, part, :]))
+    pairs.append((got.at[:local, local], first))
+    pairs.append((got.at[local:, local], fourth))
+    copies = [
+        pltpu.make_async_copy(source, target, done.at[k])
+        for k, (source, target) in enumerate(pairs)
+    ]
+    for copy in copies:
+        copy.start()
+    for copy in copies:
+        copy.wait()
 
 
 def exchange(value, axes):
@@ -189,9 +205,11 @@
         [shape(groups, rows, count)],
         *entering,
         flops=4 * count * wide * width, vmem=60 << 20,
-        in_specs=[pl.BlockSpec(memory_space=pltpu.HBM)] * 4,
+        in_specs=[pl.BlockSpec(memory_space=pl.ANY)] * 4,
+        out_specs=[pl.BlockSpec(memory_space=pl.ANY)],
         scratch_shapes=[pltpu.VMEM(a.shape, BF) for a in entering]
-        + [pltpu.SemaphoreType.DMA((4,))],
+        + [pltpu.VMEM((groups, rows, count), BF)]
+        + [pltpu.SemaphoreType.DMA((4,)), pltpu.SemaphoreType.DMA((local,))],
     )
     got = exchange(send, "hidden")
     send, grads = call(
@@ -218,13 +236,22 @@
     got = lax.all_gather(total, far, axis=0, tiled=False)
     (copies,) = call(
         functools.partial(add_copy_kernel, scale),
-        [shape(parts, (local + 1) * width, width)], got, flops=got.size,
-    )
-    got = exchange(copies, near)
+        [shape(parts, (local + 1) * width, width)],
+        got,
+        flops=got.size,
+        out_specs=[pl.BlockSpec(memory_space=pl.ANY)],
+        scratch_shapes=[
+            pltpu.VMEM(((local + 1) * width, width), BF), pltpu.SemaphoreType.DMA((parts,)),
+        ],
+    )
+    got = exchange(copies, near).reshape(parts, local + 1, width, width)
     first, second, third, fourth = call(
         unpack_kernel,
         [shape(*w.shape) for w in (w_first, w_second, w_third, w_fourth)],
         got,
+        in_specs=[pl.BlockSpec(memory_space=pl.ANY)],
+        out_specs=[pl.BlockSpec(memory_space=pl.ANY)] * 4,
+        scratch_shapes=[pltpu.SemaphoreType.DMA((parts + 2,))],
     )
     return output, grad_tokens, first, second, third, fourth
 

time: 123 us -> 123 us (level)
  no operation moved by 1% of the time
where the time goes in v3:
time: 123 us
  blocking collectives  91.6 us (74%)
  waiting for transfers between devices  16.6 us (13%)
  Pallas kernels  9.16 us (7%)
  starting transfers between devices  4.5 us (4%)
    all_to_all x3, blocking collectives, exchange(): return lax.all_to_all(value, axes, split_axis=0, concat_axis=0, tiled=True)  69.6 us
    all_gather x1, blocking collectives, body(): got = lax.all_gather(total, far, axis=0, tiled=False)  22 us
    all_to_all x1, waiting for transfers between devices, exchange(): return lax.all_to_all(value, axes, split_axis=0, concat_axis=0, tiled=True)  16.6 us
    pallas_call x7, Pallas kernels, call(): pl.pallas_call(kernel, out_shape=outs, compiler_params=pltpu.CompilerPara...  9.16 us
    all_to_all x1, starting transfers between devices, exchange(): return lax.all_to_all(value, axes, split_axis=0, concat_axis=0, tiled=True)  4.5 us
  transfers between devices with their start and end apart: 1, of which 1 were waited for; matrix products, arithmetic and copies ran while one was open for 0% of the time, Pallas kernels for 1%

profile of v3, /device:TPU:1, one launch (start us, length us, event | category | flops | bytes accessed | tf_op | source)
XLA Modules:
  0.0 122.6 jit_solution(1876565620955175956)
XLA Ops:
  0.6 0.0 copy-start.5
  0.6 0.0 copy-start.4
  0.7 2.3 %shard_map.109 = bf16[16,64,256]{2,1,0:T(8,128)(2,1)} custom-call(bf16[256,512]{1,0:T(8,128)(2,1)} %x.1, bf16[4,128,128]{2,1,0:T(8,128)(2,1)} %w1.1, bf16[256,512]{1,0:T(8,128)(2,1)} %dy.1, bf16[4,128,128]{2,1,0:T(8,128)(2,1)} %w4.1), custom_call_target="tpu_custom_call" | custom-call | flops 67108864 | bytes 1310720 | tf_op jit(solution)/shard_map/pallas_call | solution.py:27
  2.9 27.6 %all_to_all.20.got = bf16[16,64,256]{2,1,0:T(8,128)(2,1)S(1)} all-to-all(bf16[16,64,256]{2,1,0:T(8,128)(2,1)} %shard_map.109), channel_id=1, replica_groups=mesh['far'=4,'near'=8,'hidden'=16] {'hidden'}, dimensions={0} | all-to-all | bytes 1048576 | tf_op jit(solution)/shard_map/all_to_all | solution.py:192
  30.5 0.0 copy-done.5
  30.5 0.0 copy-done.4
  30.5 0.0 copy-start
  30.5 2.6 %shard_map.110 = (bf16[16,64,256]{2,1,0:T(8,128)(2,1)S(1)}, bf16[8,512,128]{2,1,0:T(8,128)(2,1)S(1)}) custom-call(bf16[16,64,256]{2,1,0:T(8,128)(2,1)S(1)} %all_to_all.20.got, bf16[4,128,512]{2,1,0:T(8,128)(2,1)S(1)} %copy-done.4, bf16[4,512,128]{2,1,0:T(8,128)(2,1)S(1)} %copy-done.5), custom_call_target="tpu_custom_call" | custom-call | flops 805306368 | bytes 3145728 | tf_op jit(solution)/shard_map/pallas_call | solution.py:27
  33.1 20.0 %all_to_all.21.got = bf16[16,64,256]{2,1,0:T(8,128)(2,1)S(1)} all-to-all(bf16[16,64,256]{2,1,0:T(8,128)(2,1)S(1)} %get-tuple-element.17), channel_id=1, replica_groups=mesh['far'=4,'near'=8,'hidden'=16] {'hidden'}, dimensions={0} | all-to-all | bytes 1048576 | tf_op jit(solution)/shard_map/all_to_all | solution.py:192
  53.2 0.0 copy-done
  53.2 0.0 copy-done.1
  53.2 0.6 shard_map.111
  53.8 22.0 %all_to_all.22.got = bf16[8,640,128]{2,1,0:T(8,128)(2,1)S(1)} all-to-all(bf16[8,640,128]{2,1,0:T(8,128)(2,1)S(1)} %get-tuple-element.23), channel_id=1, replica_groups=mesh['far'=4,'near'=8,'hidden'=16] {'near'}, dimensions={0} | all-to-all | bytes 2621440 | tf_op jit(solution)/shard_map/all_to_all | solution.py:192
  75.8 0.2 shard_map.113
  76.0 22.0 %all-gather = bf16[2560,128]{1,0:T(8,128)(2,1)S(1)} all-gather(bf16[640,128]{1,0:T(8,128)(2,1)S(1)} %shard_map.113), channel_id=2, replica_groups=mesh['far'=4,'near'=8,'hidden'=16] {'far'}, dimensions={0}, use_global_device_ids=true | all-gather | bytes 819200 | tf_op jit(solution)/shard_map/all_gather | solution.py:236
  98.0 1.3 %shard_map.114 = bf16[8,640,128]{2,1,0:T(8,128)(2,1)} custom-call(bf16[4,640,128]{2,1,0:T(8,128)(2,1)S(1)} %bitcast.3), custom_call_target="tpu_custom_call" | custom-call | flops 327680 | bytes 1966080 | tf_op jit(solution)/shard_map/pallas_call | solution.py:27
  99.2 0.0 copy-start.2
  99.2 0.0 copy-start.3
  99.2 4.5 %all-to-all-start.3 = ((bf16[8,640,128]{2,1,0:T(8,128)(2,1)}), bf16[8,640,128]{2,1,0:T(8,128)(2,1)S(1)}, u32[]{:S(2)}, u32[]{:S(2)}) async-start(bf16[8,640,128]{2,1,0:T(8,128)(2,1)} %shard_map.114), calls=%async_computation.3 | async-start | bytes 2621440 | tf_op jit(solution)/shard_map/all_to_all | solution.py:192
  103.7 0.0 copy-done.2
  103.8 0.0 copy-done.3
  103.8 1.1 shard_map.112
  104.9 16.6 %all-to-all-done.3 = bf16[8,640,128]{2,1,0:T(8,128)(2,1)S(1)} async-done(((bf16[8,640,128]{2,1,0:T(8,128)(2,1)}), bf16[8,640,128]{2,1,0:T(8,128)(2,1)S(1)}, u32[]{:S(2)}, u32[]{:S(2)}) %all-to-all-start.3) | async-done | bytes 1310752 | tf_op jit(solution)/shard_map/all_to_all | solution.py:192
  121.5 1.1 shard_map.115
  (1 shorter events, 0.0 us)
Async XLA Ops:
  0.6 29.9 %copy-start.5 = (bf16[4,512,128]{2,1,0:T(8,128)(2,1)S(1)}, bf16[4,512,128]{2,1,0:T(8,128)(2,1)}, u32[]{:S(2)}) copy-start(bf16[4,512,128]{2,1,0:T(8,128)(2,1)} %w3.1) | copy-start | bytes 1572868
  0.6 29.9 %copy-start.4 = (bf16[4,128,512]{2,1,0:T(8,128)(2,1)S(1)}, bf16[4,128,512]{2,1,0:T(8,128)(2,1)}, u32[]{:S(2)}) copy-start(bf16[4,128,512]{2,1,0:T(8,128)(2,1)} %w2.1) | copy-start | bytes 1572868
  30.5 22.6 %copy-start = (bf16[256,512]{1,0:T(8,128)(2,1)S(1)}, bf16[256,512]{1,0:T(8,128)(2,1)}, u32[]{:S(2)}) copy-start(bf16[256,512]{1,0:T(8,128)(2,1)} %x.1) | copy-start | bytes 786436
  30.5 22.6 %copy-start.1 = (bf16[256,512]{1,0:T(8,128)(2,1)S(1)}, bf16[256,512]{1,0:T(8,128)(2,1)}, u32[]{:S(2)}) copy-start(bf16[256,512]{1,0:T(8,128)(2,1)} %dy.1) | copy-start | bytes 786436
  99.2 4.5 %copy-start.2 = (bf16[4,128,128]{2,1,0:T(8,128)(2,1)S(1)}, bf16[4,128,128]{2,1,0:T(8,128)(2,1)}, u32[]{:S(2)}) copy-start(bf16[4,128,128]{2,1,0:T(8,128)(2,1)} %w1.1) | copy-start | bytes 393220
  99.2 4.5 %copy-start.3 = (bf16[4,128,128]{2,1,0:T(8,128)(2,1)S(1)}, bf16[4,128,128]{2,1,0:T(8,128)(2,1)}, u32[]{:S(2)}) copy-start(bf16[4,128,128]{2,1,0:T(8,128)(2,1)} %w4.1) | copy-start | bytes 393220
  99.2 22.3 %all-to-all-start.3 = ((bf16[8,640,128]{2,1,0:T(8,128)(2,1)}), bf16[8,640,128]{2,1,0:T(8,128)(2,1)S(1)}, u32[]{:S(2)}, u32[]{:S(2)}) async-start(bf16[8,640,128]{2,1,0:T(8,128)(2,1)} %shard_map.114), calls=%async_computation.3 | async-start | bytes 2621440 | tf_op jit(solution)/shard_map/all_to_all | solution.py:192

commit v4 on v2

v4 whole, which is shorter than its diff:
```python
import functools

import jax
import jax.numpy as jnp
from jax import lax
from jax.experimental import pallas as pl
from jax.experimental.pallas import tpu as pltpu
from jax.sharding import Mesh, PartitionSpec as P

ROOT = 0.7978845608
CUBIC = 0.044715
BF = jnp.bfloat16
F32 = jnp.float32
PAIR = 2
Z_LOW = 2
X_SIZE = 4
NN = (((1,), (0,)), ((), ()))
NT = (((1,), (1,)), ((), ()))
TN = (((0,), (0,)), ((), ()))
TT = (((0,), (1,)), ((), ()))


def dot(a, b, dims):
    return lax.dot_general(a, b, dims, preferred_element_type=F32)


def call(kernel, outs, *args, flops=0, transcendentals=0, vmem=24 << 20, **more):
    moved = sum(a.size * a.dtype.itemsize for a in (*args, *outs))
    return pl.pallas_call(
        kernel,
        out_shape=outs,
        compiler_params=pltpu.CompilerParams(vmem_limit_bytes=vmem),
        cost_estimate=pl.CostEstimate(
            flops=int(flops), bytes_accessed=int(moved), transcendentals=int(transcendentals)
        ),
        **more,
    )(*args)


def shape(*dims, dtype=BF):
    return jax.ShapeDtypeStruct(dims, dtype)


def stack(low, high):
    width, tokens = low.shape
    per = 2 * PAIR * Z_LOW
    split = (width // per, per, tokens)
    return jnp.concatenate([low.reshape(split), high.reshape(split)], axis=1)


def enter_kernel(groups, x_in, w1_in, dy_in, w4_in, send, x, w1, dy, w4, arrived):
    copies = [
        pltpu.make_async_copy(source, target, arrived.at[k])
        for k, (source, target) in enumerate(((x_in, x), (w1_in, w1), (dy_in, dy), (w4_in, w4)))
    ]
    for copy in copies:
        copy.start()
    local, width, _ = w1.shape
    tokens = x.shape[0]
    per = width // groups
    rows = local * per // Z_LOW
    first_half = lax.broadcasted_iota(jnp.int32, (groups, per, tokens), 1) < per // 2
    for k in range(2):
        copies[2 * k].wait()
        copies[2 * k + 1].wait()
        to_zl = [[], []]
        for pair in range(local // 2):
            both = []
            for b in (2 * pair, 2 * pair + 1):
                cols = pl.ds(b * width, width)
                if k == 0:
                    z = dot(w1[b], x[:, cols], TT)
                else:
                    z = dot(w4[b], dy[:, cols], NT)
                both.append(z.reshape(groups, per, tokens))
            low, high = both
            to_zl[0].append(jnp.where(first_half, low, pltpu.roll(high, per // 2, 1)))
            to_zl[1].append(jnp.where(first_half, pltpu.roll(low, per // 2, 1), high))
        for zl in range(Z_LOW):
            filled = jnp.concatenate(to_zl[zl], axis=1).astype(BF)
            send[zl * groups : (zl + 1) * groups, k * rows : (k + 1) * rows, :] = filled


def one_hot(source):
    n = source.shape[0]
    return (lax.broadcasted_iota(jnp.int32, (n, n), 1) == source).astype(F32).astype(BF)


def collect(got, k, theirs, out):
    count, rows, tokens = got.shape
    groups, held = count // Z_LOW, rows // 2
    mine = held // (theirs * PAIR)
    n = out.shape[0] // mine
    some = n // held
    per = theirs * PAIR
    r = lax.broadcasted_iota(jnp.int32, (n, 1), 0)
    own, group = r // (some * per), (r // per) % some
    their, one = (r // PAIR) % theirs, r % PAIR
    order = one_hot(group * held + their * (mine * PAIR) + own * PAIR + one)
    for zl in range(Z_LOW):
        for g in range(groups // some):
            at = zl * groups + g * some
            taken = got[at : at + some, k * held : (k + 1) * held, :].reshape(n, tokens)
            moved = dot(order, taken, NN).astype(BF)
            for b in range(mine):
                to = b * n + g * some * per
                out[to : to + some * per, zl * tokens : (zl + 1) * tokens] = moved[
                    b * some * per : (b + 1) * some * per, :
                ]


def collect_back(got, k, local, out):
    count, rows, tokens = got.shape
    groups, held = count // Z_LOW, rows // 2
    theirs = held // (local * PAIR)
    n = out.shape[0] // local
    some = n // (Z_LOW * held)
    per = Z_LOW * theirs * PAIR
    r = lax.broadcasted_iota(jnp.int32, (n, 1), 0)
    own, group = r // (some * per), (r // per) % some
    zl, their, one = (r // (theirs * PAIR)) % Z_LOW, (r // PAIR) % theirs, r % PAIR
    order = one_hot((zl * some + group) * held + their * (local * PAIR) + own * PAIR + one)
    for g in range(groups // some):
        taken = jnp.concatenate(
            [
                got[z * groups + g * some : z * groups + (g + 1) * some, k * held : (k + 1) * held, :]
                .reshape(some * held, tokens)
                for z in range(Z_LOW)
            ],
            axis=0,
        )
        moved = dot(order, taken, NN).astype(BF)
        for b in range(local):
            to = b * n + g * some * per
            out[to : to + some * per, :] = moved[b * some * per : (b + 1) * some * per, :]


def middle_kernel(groups, at, got, w2, w3, send, *rest):
    shares, (mixed, d_down, act, d_pre, grads) = rest[:X_SIZE], rest[X_SIZE:]
    local, width, hidden = w2.shape
    mine = local // Z_LOW
    tokens = got.shape[2]
    rows = send.shape[1] // 2
    parts = hidden // width
    base = at[0] * mine
    collect(got, 0, local, mixed)
    collect(got, 1, local, d_down)
    for zl in range(Z_LOW):
        cols = pl.ds(zl * tokens, tokens)
        downs, d_mixeds = [], []
        for b in range(mine):
            held = pl.ds(b * width, width)
            h = dot(w2[base + b], mixed[held, cols], TN)
            squared = h * h
            half = 0.5 + 0.5 * jnp.tanh(h * (ROOT + (ROOT * CUBIC) * squared))
            acted = (h * half).astype(BF)
            gain = half + h * (half - half * half) * (2.0 * ROOT + (6.0 * ROOT * CUBIC) * squared)
            d_act = dot(w3[base + b], d_down[held, cols], NN)
            d_h = (d_act * gain).astype(BF)
            downs.append(dot(w3[base + b], acted, TN))
            d_mixeds.append(dot(w2[base + b], d_h, NN))
            act[b, :, cols] = acted
            d_pre[b, :, cols] = d_h
        send[zl * groups : (zl + 1) * groups, :rows, :] = stack(*downs).astype(BF)
        send[zl * groups : (zl + 1) * groups, rows:, :] = stack(*d_mixeds).astype(BF)
    for b in range(mine):
        held = pl.ds(b * width, width)
        second = dot(mixed[held, :], d_pre[b], NT).astype(BF)
        for j in range(parts):
            part = slice(j * width, (j + 1) * width)
            grads[b, part, :] = second[:, part]
        grads[mine + b] = dot(act[b], d_down[held, :], NT).astype(BF)
    for k in range(X_SIZE):
        shares[k][...] = grads[(at[1] + k) % X_SIZE]


def leave_kernel(got, x, dy, *rest):
    *shares, back, d_first, grads, wide_sum = rest
    acc = shares[0][...].astype(F32)
    for share in shares[1:]:
        acc = acc + share[...].astype(F32)
    wide_sum[...] = acc.astype(BF)
    parts, width, _ = grads.shape
    local = parts // 2
    collect_back(got, 0, local, back)
    collect_back(got, 1, local, d_first)
    for b in range(local):
        rows = pl.ds(b * width, width)
        grads[b] = dot(x[:, rows], d_first[rows, :], TT).astype(BF)
        grads[local + b] = dot(back[rows, :], dy[:, rows], NN).astype(BF)


def outputs_kernel(back, d_first, w1, w4, output, grad_tokens):
    local, width, _ = w1.shape
    for b in range(local):
        cols = pl.ds(b * width, width)
        output[:, cols] = dot(back[cols, :], w4[b], TN).astype(BF)
        grad_tokens[:, cols] = dot(d_first[cols, :], w1[b], TT).astype(BF)


def add_kernel(got, wide_sum, total):
    high = wide_sum.shape[0]
    total[:high, :] = wide_sum[...]
    acc = got[0].astype(F32)
    for k in range(1, got.shape[0]):
        acc = acc + got[k].astype(F32)
    total[high:, :] = acc.astype(BF)


def add_copy_kernel(scale, got, copies):
    acc = got[0].astype(F32)
    for k in range(1, got.shape[0]):
        acc = acc + got[k].astype(F32)
    total = (acc * scale).astype(BF)
    for k in range(copies.shape[0]):
        copies[k] = total


def unpack_kernel(got, first, second, third, fourth):
    local, width, hidden = second.shape
    parts = hidden // width
    mine = local // Z_LOW
    for b in range(local):
        k = b // mine * X_SIZE + b % mine
        for j in range(parts):
            part = slice(j * width, (j + 1) * width)
            second[b, :, part] = got[k, part, :]
        third[b] = got[k + mine, :hidden, :]
        first[b] = got[b, hidden:, :]
        fourth[b] = got[local + b, hidden:, :]


def exchange(value, axes):
    return lax.all_to_all(value, axes, split_axis=0, concat_axis=0, tiled=True)


def body(all_tokens, tokens, w_first, w_second, w_third, w_fourth, upstream):
    count, wide = tokens.shape
    local, width, hidden = w_second.shape
    groups = lax.axis_size("hidden")
    near, middle = ("zl", "x"), ("zl", "hidden")
    parts = Z_LOW * X_SIZE
    mine = local // Z_LOW
    scale = float(all_tokens) ** -0.5
    rows = 2 * local * mine * PAIR
    place = jnp.stack([lax.axis_index("zl"), lax.axis_index("x")]).astype(jnp.int32)
    entering = (tokens, w_first, upstream, w_fourth)
    (send,) = call(
        functools.partial(enter_kernel, groups),
        [shape(Z_LOW * groups, rows, count)],
        *entering,
        flops=4 * count * wide * width, vmem=60 << 20,
        in_specs=[pl.BlockSpec(memory_space=pltpu.HBM)] * 4,
        scratch_shapes=[pltpu.VMEM(a.shape, BF) for a in entering]
        + [pltpu.SemaphoreType.DMA((4,))],
    )
    got = exchange(send, middle)
    both = Z_LOW * count
    send, *shares = call(
        functools.partial(middle_kernel, groups),
        [shape(Z_LOW * groups, rows, count)] + [shape(hidden, width)] * X_SIZE,
        place, got, w_second, w_third,
        flops=12 * count * wide * hidden, transcendentals=count * local * hidden,
        in_specs=[pl.BlockSpec(memory_space=pltpu.SMEM)] + [pl.BlockSpec()] * 3,
        scratch_shapes=[pltpu.VMEM((mine * width, both), BF)] * 2
        + [pltpu.VMEM((mine, hidden, both), BF)] * 2
        + [pltpu.VMEM((X_SIZE, hidden, width), BF)],
    )
    got = exchange(send, middle)
    shares = [
        share if k == 0 else lax.ppermute(share, "x", [(i, (i + k) % X_SIZE) for i in range(X_SIZE)])
        for k, share in enumerate(shares)
    ]
    back, d_first, grads, wide_sum = call(
        leave_kernel,
        [
            shape(wide, count), shape(wide, count), shape(parts, width, width),
            shape(hidden, width),
        ],
        got, tokens, upstream, *shares,
        flops=8 * count * wide * width,
    )
    got = exchange(grads, near)
    output, grad_tokens = call(
        outputs_kernel, [shape(count, wide), shape(count, wide)],
        back, d_first, w_first, w_fourth,
        flops=4 * count * wide * width,
    )
    (total,) = call(
        add_kernel, [shape(hidden + width, width)], got, wide_sum, flops=4 * hidden * width
    )
    got = lax.all_gather(total, "far", axis=0, tiled=False)
    (copies,) = call(
        functools.partial(add_copy_kernel, scale),
        [shape(parts, hidden + width, width)], got, flops=got.size,
    )
    got = exchange(copies, near)
    first, second, third, fourth = call(
        unpack_kernel,
        [shape(*w.shape) for w in (w_first, w_second, w_third, w_fourth)],
        got,
    )
    return output, grad_tokens, first, second, third, fourth


def solution(mesh):
    seq, groups = mesh.shape["seq"], mesh.shape["hidden"]
    fine = Mesh(
        mesh.devices.reshape(seq // (Z_LOW * X_SIZE), Z_LOW, X_SIZE, groups),
        ("far", "zl", "x", "hidden"),
    )
    rows = P(("far", "zl", "x"), "hidden")
    weight = P("hidden", None, None)

    def run(tokens, w_first, w_second, w_third, w_fourth, upstream):
        return jax.shard_map(
            functools.partial(body, tokens.shape[0]),
            mesh=fine,
            in_specs=(rows, weight, weight, weight, weight, rows),
            out_specs=(rows, rows, weight, weight, weight, weight),
            check_vma=False,
        )(tokens, w_first, w_second, w_third, w_fourth, upstream)

    return run
```

time: 123 us -> 111 us (0.902)
  the two profiles are of different devices: /device:TPU:1 before, /device:TPU:8 now
where the time goes in v4:
time: 111 us; the launch traced here: 110 us
  waiting for transfers between devices  36.3 us (33%)
  blocking collectives  34.4 us (31%)
  starting transfers between devices  29.1 us (26%)
  Pallas kernels  9.73 us (9%)
    all_to_all x3, waiting for transfers between devices, exchange(): return lax.all_to_all(value, axes, split_axis=0, concat_axis=0, tiled=True)  32.8 us
    all_gather x1, blocking collectives, body(): got = lax.all_gather(total, 'far', axis=0, tiled=False)  23.1 us
    all_to_all x3, starting transfers between devices, exchange(): return lax.all_to_all(value, axes, split_axis=0, concat_axis=0, tiled=True)  17.7 us
    ppermute x3, starting transfers between devices, body(): lax.ppermute(share, 'x', [(i, (i + k) % X_SIZE) for i in range(X_SIZE)])  11.4 us
    all_to_all x1, blocking collectives, exchange(): return lax.all_to_all(value, axes, split_axis=0, concat_axis=0, tiled=True)  11.3 us
    pallas_call x7, Pallas kernels, call(): pl.pallas_call(kernel, out_shape=outs, compiler_params=pltpu.CompilerPara...  9.73 us
    ppermute x3, waiting for transfers between devices, body(): lax.ppermute(share, 'x', [(i, (i + k) % X_SIZE) for i in range(X_SIZE)])  3.53 us
  transfers between devices with their start and end apart: 6, of which 5 were waited for; matrix products, arithmetic and copies ran while one was open for 0% of the time, Pallas kernels for 1%

profile of v4, /device:TPU:8, one launch (start us, length us, event | category | flops | bytes accessed | tf_op | source)
XLA Modules:
  0.0 110.3 jit_solution(11449095583145391275)
XLA Ops:
  0.6 0.0 copy-start.5
  0.6 0.0 copy-start.4
  0.7 2.4 %shard_map.109 = bf16[32,32,256]{2,1,0:T(8,128)(2,1)} custom-call(bf16[256,512]{1,0:T(8,128)(2,1)} %x.1, bf16[4,128,128]{2,1,0:T(8,128)(2,1)} %w1.1, bf16[256,512]{1,0:T(8,128)(2,1)} %dy.1, bf16[4,128,128]{2,1,0:T(8,128)(2,1)} %w4.1), custom_call_target="tpu_custom_call" | custom-call | flops 67108864 | bytes 1310720 | tf_op jit(solution)/shard_map/pallas_call | solution.py:29
  3.1 9.5 %all-to-all-start = ((bf16[32,32,256]{2,1,0:T(8,128)(2,1)}), bf16[32,32,256]{2,1,0:T(8,128)(2,1)S(1)}, u32[]{:S(2)}, u32[]{:S(2)}) async-start(bf16[32,32,256]{2,1,0:T(8,128)(2,1)} %shard_map.109), calls=%async_computation | async-start | bytes 1048576 | tf_op jit(solution)/shard_map/all_to_all | solution.py:234
  12.6 0.1 pad_add_fusion.at
  12.7 17.7 %all-to-all-done.got = bf16[32,32,256]{2,1,0:T(8,128)(2,1)S(1)} async-done(((bf16[32,32,256]{2,1,0:T(8,128)(2,1)}), bf16[32,32,256]{2,1,0:T(8,128)(2,1)S(1)}, u32[]{:S(2)}, u32[]{:S(2)}) %all-to-all-start) | async-done | bytes 524320 | tf_op jit(solution)/shard_map/all_to_all | solution.py:234
  30.4 3.2 %shard_map.110 = (bf16[32,32,256]{2,1,0:T(8,128)(2,1)}, bf16[512,128]{1,0:T(8,128)(2,1)S(1)}, bf16[512,128]{1,0:T(8,128)(2,1)S(1)}, bf16[512,128]{1,0:T(8,128)(2,1)S(1)}, bf16[512,128]{1,0:T(8,128)(2,1)S(1)}) custom-call(s32[2]{0:T(128)S(1)} %pad_add_fusion.at, bf16[32,32,256]{2,1,0:T(8,128)(2,1)S(1)} %all-to-all-done.got, ...), custom_call_target="tpu_custom_call" | custom-call | flops 805306368 | bytes 2621448 | tf_op jit(solution)/shard_map/pallas_call | solution.py:29
  33.5 4.5 %all-to-all-start.1 = ((bf16[32,32,256]{2,1,0:T(8,128)(2,1)}), bf16[32,32,256]{2,1,0:T(8,128)(2,1)S(1)}, u32[]{:S(2)}, u32[]{:S(2)}) async-start(bf16[32,32,256]{2,1,0:T(8,128)(2,1)} %get-tuple-element.21), calls=%async_computation.1 | async-start | bytes 1048576 | tf_op jit(solution)/shard_map/all_to_all | solution.py:234
  38.0 3.4 %collective-permute-start = (bf16[512,128]{1,0:T(8,128)(2,1)S(1)}, bf16[512,128]{1,0:T(8,128)(2,1)S(1)}, u32[]{:S(2)}, u32[]{:S(2)}) collective-permute-start(bf16[512,128]{1,0:T(8,128)(2,1)S(1)} %get-tuple-element.23), channel_id=1, source_target_pairs={{0,16},{16,32},{32,48},{48,0},{1,17},{17,33},{33,49},{49,1},{2,18}... | collective-permute-start | bytes 393224 | tf_op jit(solution)/shard_map/ppermute | solution.py:271
  41.4 4.6 %collective-permute-start.1 = (bf16[512,128]{1,0:T(8,128)(2,1)S(1)}, bf16[512,128]{1,0:T(8,128)(2,1)S(1)}, u32[]{:S(2)}, u32[]{:S(2)}) collective-permute-start(bf16[512,128]{1,0:T(8,128)(2,1)S(1)} %get-tuple-element.24), channel_id=1, source_target_pairs={{0,32},{16,48},{32,0},{48,16},{1,33},{17,49},{33,1},{49,17},{2,34}... | collective-permute-start | bytes 393224 | tf_op jit(solution)/shard_map/ppermute | solution.py:271
  46.1 3.3 %collective-permute-start.2 = (bf16[512,128]{1,0:T(8,128)(2,1)S(1)}, bf16[512,128]{1,0:T(8,128)(2,1)S(1)}, u32[]{:S(2)}, u32[]{:S(2)}) collective-permute-start(bf16[512,128]{1,0:T(8,128)(2,1)S(1)} %get-tuple-element.25), channel_id=1, source_target_pairs={{0,48},{16,0},{32,16},{48,32},{1,49},{17,1},{33,17},{49,33},{2,50}... | collective-permute-start | bytes 393224 | tf_op jit(solution)/shard_map/ppermute | solution.py:271
  49.4 0.0 collective-permute-done.rest_1_
  49.4 1.0 collective-permute-done.1.rest_2_
  50.5 2.5 %collective-permute-done.2.rest_3_ = bf16[512,128]{1,0:T(8,128)(2,1)S(1)} collective-permute-done((bf16[512,128]{1,0:T(8,128)(2,1)S(1)}, bf16[512,128]{1,0:T(8,128)(2,1)S(1)}, u32[]{:S(2)}, u32[]{:S(2)}) %collective-permute-start.2) | collective-permute-done | bytes 131104 | tf_op jit(solution)/shard_map/ppermute | solution.py:271
  52.9 2.9 %all-to-all-done.1.got = bf16[32,32,256]{2,1,0:T(8,128)(2,1)S(1)} async-done(((bf16[32,32,256]{2,1,0:T(8,128)(2,1)}), bf16[32,32,256]{2,1,0:T(8,128)(2,1)S(1)}, u32[]{:S(2)}, u32[]{:S(2)}) %all-to-all-start.1) | async-done | bytes 524320 | tf_op jit(solution)/shard_map/all_to_all | solution.py:234
  55.9 0.0 copy-done.1
  55.9 0.6 shard_map.111
  56.5 11.3 %all_to_all.20.got = bf16[8,128,128]{2,1,0:T(8,128)(2,1)S(1)} all-to-all(bf16[8,128,128]{2,1,0:T(8,128)(2,1)S(1)} %get-tuple-element.30), channel_id=1, replica_groups=mesh['far'=4,'zl'=2,'x'=4,'hidden'=16] {'zl','x'}, dimensions={0} | all-to-all | bytes 524288 | tf_op jit(solution)/shard_map/all_to_all | solution.py:234
  67.9 23.1 %all-gather = bf16[2560,128]{1,0:T(8,128)(2,1)S(1)} all-gather(bf16[640,128]{1,0:T(8,128)(2,1)S(1)} %shard_map.113), channel_id=2, replica_groups=mesh['far'=4,'zl'=2,'x'=4,'hidden'=16] {'far'}, dimensions={0}, use_global_device_ids=true | all-gather | bytes 819200 | tf_op jit(solution)/shard_map/all_gather | solution.py:292
  90.9 1.2 %shard_map.114 = bf16[8,640,128]{2,1,0:T(8,128)(2,1)} custom-call(bf16[4,640,128]{2,1,0:T(8,128)(2,1)S(1)} %bitcast.3), custom_call_target="tpu_custom_call" | custom-call | flops 327680 | bytes 1966080 | tf_op jit(solution)/shard_map/pallas_call | solution.py:29
  92.1 3.7 %all-to-all-start.3 = ((bf16[8,640,128]{2,1,0:T(8,128)(2,1)}), bf16[8,640,128]{2,1,0:T(8,128)(2,1)S(1)}, u32[]{:S(2)}, u32[]{:S(2)}) async-start(bf16[8,640,128]{2,1,0:T(8,128)(2,1)} %shard_map.114), calls=%async_computation.3 | async-start | bytes 2621440 | tf_op jit(solution)/shard_map/all_to_all | solution.py:234
  95.9 1.1 %shard_map.112 = (bf16[256,512]{1,0:T(8,128)(2,1)}, bf16[256,512]{1,0:T(8,128)(2,1)}) custom-call(bf16[512,256]{1,0:T(8,128)(2,1)S(1)} %get-tuple-element.26.back, bf16[512,256]{1,0:T(8,128)(2,1)S(1)} %get-tuple-element.27.d_first, bf16[4,128,128]{2,1,0:T(8,128)(2,1)S(1)} %copy-done.2, bf16[4,128,128]{2,1,0:T(8,128)(2,1)S(1)} %copy-done.3), custom_call_target="tpu_custom_call" | custom-call | flops 67108864 | bytes 1310720 | tf_op jit(solution)/shard_map/pallas_call | solution.py:29
  97.0 12.2 %all-to-all-done.3.got = bf16[8,640,128]{2,1,0:T(8,128)(2,1)S(1)} async-done(((bf16[8,640,128]{2,1,0:T(8,128)(2,1)}), bf16[8,640,128]{2,1,0:T(8,128)(2,1)S(1)}, u32[]{:S(2)}, u32[]{:S(2)}) %all-to-all-start.3) | async-done | bytes 1310752 | tf_op jit(solution)/shard_map/all_to_all | solution.py:234
  109.1 1.2 %shard_map.115 = (bf16[4,128,128]{2,1,0:T(8,128)(2,1)}, bf16[4,128,512]{2,1,0:T(8,128)(2,1)}, bf16[4,512,128]{2,1,0:T(8,128)(2,1)}, bf16[4,128,128]{2,1,0:T(8,128)(2,1)}) custom-call(bf16[8,640,128]{2,1,0:T(8,128)(2,1)S(1)} %all-to-all-done.3.got), custom_call_target="tpu_custom_call" | custom-call | bytes 2621440 | tf_op jit(solution)/shard_map/pallas_call | solution.py:29
  (10 shorter events, 0.1 us)
Async XLA Ops:
  0.6 29.7 %copy-start.5 = (bf16[4,512,128]{2,1,0:T(8,128)(2,1)S(1)}, bf16[4,512,128]{2,1,0:T(8,128)(2,1)}, u32[]{:S(2)}) copy-start(bf16[4,512,128]{2,1,0:T(8,128)(2,1)} %w3.1) | copy-start | bytes 1572868
  0.6 29.7 %copy-start.4 = (bf16[4,128,512]{2,1,0:T(8,128)(2,1)S(1)}, bf16[4,128,512]{2,1,0:T(8,128)(2,1)}, u32[]{:S(2)}) copy-start(bf16[4,128,512]{2,1,0:T(8,128)(2,1)} %w2.1) | copy-start | bytes 1572868
  3.1 27.3 %all-to-all-start = ((bf16[32,32,256]{2,1,0:T(8,128)(2,1)}), bf16[32,32,256]{2,1,0:T(8,128)(2,1)S(1)}, u32[]{:S(2)}, u32[]{:S(2)}) async-start(bf16[32,32,256]{2,1,0:T(8,128)(2,1)} %shard_map.109), calls=%async_computation | async-start | bytes 1048576 | tf_op jit(solution)/shard_map/all_to_all | solution.py:234
  12.7 43.2 %copy-start = (bf16[256,512]{1,0:T(8,128)(2,1)S(1)}, bf16[256,512]{1,0:T(8,128)(2,1)}, u32[]{:S(2)}) copy-start(bf16[256,512]{1,0:T(8,128)(2,1)} %x.1) | copy-start | bytes 786436
  12.7 43.2 %copy-start.1 = (bf16[256,512]{1,0:T(8,128)(2,1)S(1)}, bf16[256,512]{1,0:T(8,128)(2,1)}, u32[]{:S(2)}) copy-start(bf16[256,512]{1,0:T(8,128)(2,1)} %dy.1) | copy-start | bytes 786436
  33.5 22.3 %all-to-all-start.1 = ((bf16[32,32,256]{2,1,0:T(8,128)(2,1)}), bf16[32,32,256]{2,1,0:T(8,128)(2,1)S(1)}, u32[]{:S(2)}, u32[]{:S(2)}) async-start(bf16[32,32,256]{2,1,0:T(8,128)(2,1)} %get-tuple-element.21), calls=%async_computation.1 | async-start | bytes 1048576 | tf_op jit(solution)/shard_map/all_to_all | solution.py:234
  38.0 11.4 %collective-permute-start = (bf16[512,128]{1,0:T(8,128)(2,1)S(1)}, bf16[512,128]{1,0:T(8,128)(2,1)S(1)}, u32[]{:S(2)}, u32[]{:S(2)}) collective-permute-start(bf16[512,128]{1,0:T(8,128)(2,1)S(1)} %get-tuple-element.23), channel_id=1, source_target_pairs={{0,16},{16,32},{32,48},{48,0},{1,17},{17,33},{33,49},{49,1},{2,18}... | collective-permute-start | bytes 393224 | tf_op jit(solution)/shard_map/ppermute | solution.py:271
  41.4 9.0 %collective-permute-start.1 = (bf16[512,128]{1,0:T(8,128)(2,1)S(1)}, bf16[512,128]{1,0:T(8,128)(2,1)S(1)}, u32[]{:S(2)}, u32[]{:S(2)}) collective-permute-start(bf16[512,128]{1,0:T(8,128)(2,1)S(1)} %get-tuple-element.24), channel_id=1, source_target_pairs={{0,32},{16,48},{32,0},{48,16},{1,33},{17,49},{33,1},{49,17},{2,34}... | collective-permute-start | bytes 393224 | tf_op jit(solution)/shard_map/ppermute | solution.py:271
  46.1 6.9 %collective-permute-start.2 = (bf16[512,128]{1,0:T(8,128)(2,1)S(1)}, bf16[512,128]{1,0:T(8,128)(2,1)S(1)}, u32[]{:S(2)}, u32[]{:S(2)}) collective-permute-start(bf16[512,128]{1,0:T(8,128)(2,1)S(1)} %get-tuple-element.25), channel_id=1, source_target_pairs={{0,48},{16,0},{32,16},{48,32},{1,49},{17,1},{33,17},{49,33},{2,50}... | collective-permute-start | bytes 393224 | tf_op jit(solution)/shard_map/ppermute | solution.py:271
  92.1 3.7 %copy-start.2 = (bf16[4,128,128]{2,1,0:T(8,128)(2,1)S(1)}, bf16[4,128,128]{2,1,0:T(8,128)(2,1)}, u32[]{:S(2)}) copy-start(bf16[4,128,128]{2,1,0:T(8,128)(2,1)} %w1.1) | copy-start | bytes 393220
  92.1 3.7 %copy-start.3 = (bf16[4,128,128]{2,1,0:T(8,128)(2,1)S(1)}, bf16[4,128,128]{2,1,0:T(8,128)(2,1)}, u32[]{:S(2)}) copy-start(bf16[4,128,128]{2,1,0:T(8,128)(2,1)} %w4.1) | copy-start | bytes 393220
  92.1 17.0 %all-to-all-start.3 = ((bf16[8,640,128]{2,1,0:T(8,128)(2,1)}), bf16[8,640,128]{2,1,0:T(8,128)(2,1)S(1)}, u32[]{:S(2)}, u32[]{:S(2)}) async-start(bf16[8,640,128]{2,1,0:T(8,128)(2,1)} %shard_map.114), calls=%async_computation.3 | async-start | bytes 2621440 | tf_op jit(solution)/shard_map/all_to_all | solution.py:234

commit v5 on v2

v5 whole, which is shorter than its diff:
```python
import functools

import jax
import jax.numpy as jnp
from jax import lax
from jax.experimental import pallas as pl
from jax.experimental.pallas import tpu as pltpu
from jax.sharding import Mesh, PartitionSpec as P

ROOT = 0.7978845608
CUBIC = 0.044715
BF = jnp.bfloat16
F32 = jnp.float32
PAIR = 2
Z_LOW = 2
X_SIZE = 4
NN = (((1,), (0,)), ((), ()))
NT = (((1,), (1,)), ((), ()))
TN = (((0,), (0,)), ((), ()))
TT = (((0,), (1,)), ((), ()))


def dot(a, b, dims):
    return lax.dot_general(a, b, dims, preferred_element_type=F32)


def call(kernel, outs, *args, flops=0, transcendentals=0, vmem=24 << 20, **more):
    moved = sum(a.size * a.dtype.itemsize for a in (*args, *outs))
    return pl.pallas_call(
        kernel,
        out_shape=outs,
        compiler_params=pltpu.CompilerParams(vmem_limit_bytes=vmem),
        cost_estimate=pl.CostEstimate(
            flops=int(flops), bytes_accessed=int(moved), transcendentals=int(transcendentals)
        ),
        **more,
    )(*args)


def shape(*dims, dtype=BF):
    return jax.ShapeDtypeStruct(dims, dtype)


def swap_units(tiles):
    row = lax.broadcasted_iota(jnp.int32, tiles[0].shape, 1)
    tiles = list(tiles)
    per = tiles[0].shape[1]
    for step in (len(tiles) // 2, len(tiles) // 4):
        shift = step * PAIR
        stay = (row // shift) % 2 == 0
        for k in range(len(tiles)):
            if k // step % 2 == 0:
                low, high = tiles[k], tiles[k + step]
                tiles[k] = jnp.where(stay, low, pltpu.roll(high, shift, 1))
                tiles[k + step] = jnp.where(stay, pltpu.roll(low, per - shift, 1), high)
    return tiles


def enter_kernel(groups, x_in, w1_in, dy_in, w4_in, send, x, w1, dy, w4, arrived):
    copies = [
        pltpu.make_async_copy(source, target, arrived.at[k])
        for k, (source, target) in enumerate(((x_in, x), (w1_in, w1), (dy_in, dy), (w4_in, w4)))
    ]
    for copy in copies:
        copy.start()
    local, width, _ = w1.shape
    tokens = x.shape[0]
    halves = []
    for k in range(2):
        copies[2 * k].wait()
        copies[2 * k + 1].wait()
        tiles = []
        for b in range(local):
            cols = pl.ds(b * width, width)
            z = dot(w1[b], x[:, cols], TT) if k == 0 else dot(w4[b], dy[:, cols], NT)
            tiles.append(z.reshape(groups, width // groups, tokens))
        halves.append(swap_units(tiles))
    for q in range(local):
        both = jnp.concatenate([halves[0][q], halves[1][q]], axis=1)
        send[q * groups : (q + 1) * groups] = both.astype(BF)


def middle_kernel(groups, at, got, w2, w3, send, own, other, mixed, d_down, act, d_pre, grads):
    _, width, hidden = w2.shape
    tokens = got.shape[2]
    per = width // groups
    parts = hidden // width
    zl, block = at[0], at[1]
    for s in range(X_SIZE):
        cols = pl.ds(s * tokens, tokens)
        members = slice(s * groups, (s + 1) * groups)
        taken = got[members].astype(F32)
        mixed[:, cols] = taken[:, :per, :].reshape(width, tokens).astype(BF)
        d_down[:, cols] = taken[:, per:, :].reshape(width, tokens).astype(BF)
        h = dot(w2[block], mixed[:, cols], TN)
        squared = h * h
        half = 0.5 + 0.5 * jnp.tanh(h * (ROOT + (ROOT * CUBIC) * squared))
        acted = (h * half).astype(BF)
        gain = half + h * (half - half * half) * (2.0 * ROOT + (6.0 * ROOT * CUBIC) * squared)
        d_h = (dot(w3[block], d_down[:, cols], NN) * gain).astype(BF)
        down = dot(w3[block], acted, TN).reshape(groups, per, tokens)
        d_mixed = dot(w2[block], d_h, NN).reshape(groups, per, tokens)
        send[members] = jnp.concatenate([down, d_mixed], axis=1).astype(BF)
        act[:, cols] = acted
        d_pre[:, cols] = d_h
    second = dot(mixed[...], d_pre[...], NT).astype(BF)
    for j in range(parts):
        part = slice(j * width, (j + 1) * width)
        grads[0, part, :] = second[:, part]
    grads[1] = dot(act[...], d_down[...], NT).astype(BF)
    own[...] = grads[zl]
    other[...] = grads[1 - zl]


def pair_kernel(own, other, total):
    total[...] = (own[...].astype(F32) + other[...].astype(F32)).astype(BF)


def leave_kernel(scale, got, x, dy, *rest):
    *shares, back, d_first, grads, wide_sum = rest
    acc = shares[0][...].astype(F32)
    for share in shares[1:]:
        acc = acc + share[...].astype(F32)
    wide_sum[...] = (acc * scale).astype(BF)
    parts, width, _ = grads.shape
    local = parts // 2
    count, rows, tokens = got.shape
    groups, per = count // X_SIZE, rows // 2
    taken = [got[s * groups : (s + 1) * groups].astype(F32) for s in range(X_SIZE)]
    for k, out in enumerate((back, d_first)):
        tiles = swap_units([t[:, k * per : (k + 1) * per, :] for t in taken])
        for b in range(local):
            out[b * width : (b + 1) * width, :] = tiles[b].reshape(width, tokens).astype(BF)
    for b in range(local):
        held = pl.ds(b * width, width)
        grads[b] = dot(x[:, held], d_first[held, :], TT).astype(BF)
        grads[local + b] = dot(back[held, :], dy[:, held], NN).astype(BF)


def outputs_kernel(back, d_first, w1, w4, output, grad_tokens):
    local, width, _ = w1.shape
    for b in range(local):
        cols = pl.ds(b * width, width)
        output[:, cols] = dot(back[cols, :], w4[b], TN).astype(BF)
        grad_tokens[:, cols] = dot(d_first[cols, :], w1[b], TT).astype(BF)


def add_kernel(got, copies):
    acc = got[0].astype(F32)
    for k in range(1, got.shape[0]):
        acc = acc + got[k].astype(F32)
    total = acc.astype(BF)
    for k in range(copies.shape[0]):
        copies[k] = total


def add_copy_kernel(scale, got, wide_sum, copies):
    high = wide_sum.shape[0]
    acc = got[0].astype(F32)
    for k in range(1, got.shape[0]):
        acc = acc + got[k].astype(F32)
    total = (acc * scale).astype(BF)
    for k in range(copies.shape[0]):
        copies[k, :high, :] = wide_sum[...]
        copies[k, high:, :] = total


def unpack_kernel(got, first, second, third, fourth):
    local, width, hidden = second.shape
    for b in range(local):
        for j in range(hidden // width):
            part = slice(j * width, (j + 1) * width)
            second[b, :, part] = got[b, part, :]
        third[b] = got[local + b, :hidden, :]
        first[b] = got[b, hidden:, :]
        fourth[b] = got[local + b, hidden:, :]


def exchange(value, axes):
    return lax.all_to_all(value, axes, split_axis=0, concat_axis=0, tiled=True)


def body(all_tokens, tokens, w_first, w_second, w_third, w_fourth, upstream):
    count, wide = tokens.shape
    local, width, hidden = w_second.shape
    groups = lax.axis_size("hidden")
    near, middle = ("zl", "x"), ("x", "hidden")
    parts = Z_LOW * X_SIZE
    scale = float(all_tokens) ** -0.5
    rows = 2 * local * PAIR
    place = jnp.stack([lax.axis_index("zl"), lax.axis_index("x")]).astype(jnp.int32)
    entering = (tokens, w_first, upstream, w_fourth)
    (send,) = call(
        functools.partial(enter_kernel, groups),
        [shape(X_SIZE * groups, rows, count)],
        *entering,
        flops=4 * count * wide * width, vmem=60 << 20,
        in_specs=[pl.BlockSpec(memory_space=pltpu.HBM)] * 4,
        scratch_shapes=[pltpu.VMEM(a.shape, BF) for a in entering]
        + [pltpu.SemaphoreType.DMA((4,))],
    )
    got = exchange(send, middle)
    every = X_SIZE * count
    send, own, other = call(
        functools.partial(middle_kernel, groups),
        [shape(X_SIZE * groups, rows, count)] + [shape(hidden, width)] * 2,
        place, got, w_second, w_third,
        flops=12 * count * wide * hidden, transcendentals=count * local * hidden,
        in_specs=[pl.BlockSpec(memory_space=pltpu.SMEM)] + [pl.BlockSpec()] * 3,
        scratch_shapes=[pltpu.VMEM((width, every), BF)] * 2
        + [pltpu.VMEM((hidden, every), BF)] * 2
        + [pltpu.VMEM((2, hidden, width), BF)],
    )
    got = exchange(send, middle)
    far = lax.axis_size("far")
    other = lax.ppermute(other, "zl", [(0, 1), (1, 0)])
    (wide_sum,) = call(pair_kernel, [shape(hidden, width)], own, other, flops=hidden * width)
    shares = [wide_sum] + [
        lax.ppermute(wide_sum, "far", [(i, (i + k) % far) for i in range(far)])
        for k in range(1, far)
    ]
    back, d_first, grads, wide_sum = call(
        functools.partial(leave_kernel, scale),
        [
            shape(wide, count), shape(wide, count), shape(parts, width, width),
            shape(hidden, width),
        ],
        got, tokens, upstream, *shares,
        flops=8 * count * wide * width,
    )
    got = exchange(grads, near)
    output, grad_tokens = call(
        outputs_kernel, [shape(count, wide), shape(count, wide)],
        back, d_first, w_first, w_fourth,
        flops=4 * count * wide * width,
    )
    (copies,) = call(add_kernel, [shape(far, width, width)], got, flops=got.size)
    got = exchange(copies, "far")
    (copies,) = call(
        functools.partial(add_copy_kernel, scale),
        [shape(parts, hidden + width, width)], got, wide_sum, flops=got.size,
    )
    got = exchange(copies, near)
    first, second, third, fourth = call(
        unpack_kernel,
        [shape(*w.shape) for w in (w_first, w_second, w_third, w_fourth)],
        got,
    )
    return output, grad_tokens, first, second, third, fourth


def solution(mesh):
    seq, groups = mesh.shape["seq"], mesh.shape["hidden"]
    fine = Mesh(
        mesh.devices.reshape(seq // (Z_LOW * X_SIZE), Z_LOW, X_SIZE, groups),
        ("far", "zl", "x", "hidden"),
    )
    rows = P(("far", "zl", "x"), "hidden")
    weight = P("hidden", None, None)

    def run(tokens, w_first, w_second, w_third, w_fourth, upstream):
        return jax.shard_map(
            functools.partial(body, tokens.shape[0]),
            mesh=fine,
            in_specs=(rows, weight, weight, weight, weight, rows),
            out_specs=(rows, rows, weight, weight, weight, weight),
            check_vma=False,
        )(tokens, w_first, w_second, w_third, w_fourth, upstream)

    return run
```

time: 123 us -> 123 us (level)
  the two profiles are of different devices: /device:TPU:1 before, /device:TPU:8 now
where the time goes in v5:
time: 123 us
  starting transfers between devices  42.2 us (34%)
  waiting for transfers between devices  41.7 us (34%)
  blocking collectives  27.5 us (22%)
  Pallas kernels  10.3 us (8%)
    all_to_all x3, waiting for transfers between devices, exchange(): return lax.all_to_all(value, axes, split_axis=0, concat_axis=0, tiled=True)  31 us
    all_to_all x2, blocking collectives, exchange(): return lax.all_to_all(value, axes, split_axis=0, concat_axis=0, tiled=True)  27.5 us
    all_to_all x3, starting transfers between devices, exchange(): return lax.all_to_all(value, axes, split_axis=0, concat_axis=0, tiled=True)  20.9 us
    ppermute x3, starting transfers between devices, body(): lax.ppermute(wide_sum, 'far', [(i, (i + k) % far) for i in range(far)])  17 us
    pallas_call x8, Pallas kernels, call(): pl.pallas_call(kernel, out_shape=outs, compiler_params=pltpu.CompilerPara...  10.3 us
    ppermute x3, waiting for transfers between devices, body(): lax.ppermute(wide_sum, 'far', [(i, (i + k) % far) for i in range(far)])  6.89 us
    ppermute x1, starting transfers between devices, body(): other = lax.ppermute(other, 'zl', [(0, 1), (1, 0)])  4.29 us
    ppermute x1, waiting for transfers between devices, body(): other = lax.ppermute(other, 'zl', [(0, 1), (1, 0)])  3.79 us
  transfers between devices with their start and end apart: 7, of which 5 were waited for; matrix products, arithmetic and copies ran while one was open for 0% of the time, Pallas kernels for 1%

profile of v5, /device:TPU:8, one launch (start us, length us, event | category | flops | bytes accessed | tf_op | source)
XLA Modules:
  0.0 122.5 jit_solution(15749580262921838990)
XLA Ops:
  0.7 2.5 %shard_map.109 = bf16[64,16,256]{2,1,0:T(8,128)(2,1)} custom-call(bf16[256,512]{1,0:T(8,128)(2,1)} %x.1, bf16[4,128,128]{2,1,0:T(8,128)(2,1)} %w1.1, bf16[256,512]{1,0:T(8,128)(2,1)} %dy.1, bf16[4,128,128]{2,1,0:T(8,128)(2,1)} %w4.1), custom_call_target="tpu_custom_call" | custom-call | flops 67108864 | bytes 1310720 | tf_op jit(solution)/shard_map/pallas_call | solution.py:29
  3.1 10.6 %all-to-all-start = ((bf16[64,16,256]{2,1,0:T(8,128)(2,1)}), bf16[64,16,256]{2,1,0:T(8,128)(2,1)S(1)}, u32[]{:S(2)}, u32[]{:S(2)}) async-start(bf16[64,16,256]{2,1,0:T(8,128)(2,1)} %shard_map.109), calls=%async_computation | async-start | bytes 1048576 | tf_op jit(solution)/shard_map/all_to_all | solution.py:180
  13.7 0.1 pad_add_fusion.at
  13.8 17.0 %all-to-all-done.got = bf16[64,16,256]{2,1,0:T(8,128)(2,1)S(1)} async-done(((bf16[64,16,256]{2,1,0:T(8,128)(2,1)}), bf16[64,16,256]{2,1,0:T(8,128)(2,1)S(1)}, u32[]{:S(2)}, u32[]{:S(2)}) %all-to-all-start) | async-done | bytes 524320 | tf_op jit(solution)/shard_map/all_to_all | solution.py:180
  30.8 0.0 copy-done.4
  30.8 3.6 %shard_map.110 = (bf16[64,16,256]{2,1,0:T(8,128)(2,1)}, bf16[512,128]{1,0:T(8,128)(2,1)S(1)}, bf16[512,128]{1,0:T(8,128)(2,1)S(1)}) custom-call(s32[2]{0:T(128)S(1)} %pad_add_fusion.at, bf16[64,16,256]{2,1,0:T(8,128)(2,1)S(1)} %all-to-all-done.got, bf16[4,128,512]{2,1,0:T(8,128)(2,1)S(1)} %copy-done.4, bf16[4,512,128]{2,1,0:T(8,128)(2,1)S(1)} %copy-done.5), custom_call_target="tpu_custom_call" | custom-call | flops 805306368 | bytes 2359304 | tf_op jit(solution)/shard_map/pallas_call | solution.py:29
  34.5 6.6 %all-to-all-start.1 = ((bf16[64,16,256]{2,1,0:T(8,128)(2,1)}), bf16[64,16,256]{2,1,0:T(8,128)(2,1)S(1)}, u32[]{:S(2)}, u32[]{:S(2)}) async-start(bf16[64,16,256]{2,1,0:T(8,128)(2,1)} %get-tuple-element.19), calls=%async_computation.1 | async-start | bytes 1048576 | tf_op jit(solution)/shard_map/all_to_all | solution.py:180
  41.1 4.3 %collective-permute-start = (bf16[512,128]{1,0:T(8,128)(2,1)S(1)}, bf16[512,128]{1,0:T(8,128)(2,1)S(1)}, u32[]{:S(2)}, u32[]{:S(2)}) collective-permute-start(bf16[512,128]{1,0:T(8,128)(2,1)S(1)} %get-tuple-element.21), channel_id=1, source_target_pairs={{0,64},{64,0},{1,65},{65,1},{2,66},{66,2},{3,67},{67,3},{4,68},{68... | collective-permute-start | bytes 393224 | tf_op jit(solution)/shard_map/ppermute | solution.py:216
  45.4 3.8 %collective-permute-done.other = bf16[512,128]{1,0:T(8,128)(2,1)S(1)} collective-permute-done((bf16[512,128]{1,0:T(8,128)(2,1)S(1)}, bf16[512,128]{1,0:T(8,128)(2,1)S(1)}, u32[]{:S(2)}, u32[]{:S(2)}) %collective-permute-start) | collective-permute-done | bytes 131104 | tf_op jit(solution)/shard_map/ppermute | solution.py:216
  49.2 10.3 %collective-permute-start.3 = (bf16[512,128]{1,0:T(8,128)(2,1)S(1)}, bf16[512,128]{1,0:T(8,128)(2,1)S(1)}, u32[]{:S(2)}, u32[]{:S(2)}) collective-permute-start(bf16[512,128]{1,0:T(8,128)(2,1)S(1)} %shard_map.111.rest_0_), channel_id=1, source_target_pairs={{0,384},{128,0},{256,128},{384,256},{1,385},{129,1},{257,129},{385... | collective-permute-start | bytes 393224 | tf_op jit(solution)/shard_map/ppermute | solution.py:219
  59.5 1.9 %collective-permute-start.2 = (bf16[512,128]{1,0:T(8,128)(2,1)S(1)}, bf16[512,128]{1,0:T(8,128)(2,1)S(1)}, u32[]{:S(2)}, u32[]{:S(2)}) collective-permute-start(bf16[512,128]{1,0:T(8,128)(2,1)S(1)} %shard_map.111.rest_0_), channel_id=1, source_target_pairs={{0,256},{128,384},{256,0},{384,128},{1,257},{129,385},{257,1},{385... | collective-permute-start | bytes 393224 | tf_op jit(solution)/shard_map/ppermute | solution.py:219
  61.5 4.8 %collective-permute-start.1 = (bf16[512,128]{1,0:T(8,128)(2,1)S(1)}, bf16[512,128]{1,0:T(8,128)(2,1)S(1)}, u32[]{:S(2)}, u32[]{:S(2)}) collective-permute-start(bf16[512,128]{1,0:T(8,128)(2,1)S(1)} %shard_map.111.rest_0_), channel_id=1, source_target_pairs={{0,128},{128,256},{256,384},{384,0},{1,129},{129,257},{257,385},{3... | collective-permute-start | bytes 393224 | tf_op jit(solution)/shard_map/ppermute | solution.py:219
  66.3 4.0 %collective-permute-done.3.rest_3_ = bf16[512,128]{1,0:T(8,128)(2,1)S(1)} collective-permute-done((bf16[512,128]{1,0:T(8,128)(2,1)S(1)}, bf16[512,128]{1,0:T(8,128)(2,1)S(1)}, u32[]{:S(2)}, u32[]{:S(2)}) %collective-permute-start.3) | collective-permute-done | bytes 131104 | tf_op jit(solution)/shard_map/ppermute | solution.py:219
  70.2 2.9 %collective-permute-done.2.rest_2_ = bf16[512,128]{1,0:T(8,128)(2,1)S(1)} collective-permute-done((bf16[512,128]{1,0:T(8,128)(2,1)S(1)}, bf16[512,128]{1,0:T(8,128)(2,1)S(1)}, u32[]{:S(2)}, u32[]{:S(2)}) %collective-permute-start.2) | collective-permute-done | bytes 131104 | tf_op jit(solution)/shard_map/ppermute | solution.py:219
  73.2 0.0 collective-permute-done.1.rest_1_
  73.2 0.0 all-to-all-done.1.got
  73.2 0.5 shard_map.112
  73.7 14.7 %all_to_all.25.got = bf16[8,128,128]{2,1,0:T(8,128)(2,1)S(1)} all-to-all(bf16[8,128,128]{2,1,0:T(8,128)(2,1)S(1)} %get-tuple-element.26), channel_id=1, replica_groups=mesh['far'=4,'zl'=2,'x'=4,'hidden'=16] {'zl','x'}, dimensions={0} | all-to-all | bytes 524288 | tf_op jit(solution)/shard_map/all_to_all | solution.py:180
  88.4 12.8 %all_to_all.26.got = bf16[4,128,128]{2,1,0:T(8,128)(2,1)S(1)} all-to-all(bf16[4,128,128]{2,1,0:T(8,128)(2,1)S(1)} %shard_map.114), channel_id=1, replica_groups=mesh['far'=4,'zl'=2,'x'=4,'hidden'=16] {'far'}, dimensions={0} | all-to-all | bytes 262144 | tf_op jit(solution)/shard_map/all_to_all | solution.py:180
  101.2 1.3 %shard_map.115 = bf16[8,640,128]{2,1,0:T(8,128)(2,1)} custom-call(bf16[4,128,128]{2,1,0:T(8,128)(2,1)S(1)} %all_to_all.26.got, bf16[512,128]{1,0:T(8,128)(2,1)S(1)} %get-tuple-element.27.wide_sum), custom_call_target="tpu_custom_call" | custom-call | flops 65536 | bytes 1572864 | tf_op jit(solution)/shard_map/pallas_call | solution.py:29
  102.5 3.7 %all-to-all-start.4 = ((bf16[8,640,128]{2,1,0:T(8,128)(2,1)}), bf16[8,640,128]{2,1,0:T(8,128)(2,1)S(1)}, u32[]{:S(2)}, u32[]{:S(2)}) async-start(bf16[8,640,128]{2,1,0:T(8,128)(2,1)} %shard_map.115), calls=%async_computation.4 | async-start | bytes 2621440 | tf_op jit(solution)/shard_map/all_to_all | solution.py:180
  106.2 1.1 shard_map.113
  107.3 14.0 %all-to-all-done.4.got = bf16[8,640,128]{2,1,0:T(8,128)(2,1)S(1)} async-done(((bf16[8,640,128]{2,1,0:T(8,128)(2,1)}), bf16[8,640,128]{2,1,0:T(8,128)(2,1)S(1)}, u32[]{:S(2)}, u32[]{:S(2)}) %all-to-all-start.4) | async-done | bytes 1310752 | tf_op jit(solution)/shard_map/all_to_all | solution.py:180
  121.3 1.2 shard_map.116
  (13 shorter events, 0.1 us)
Async XLA Ops:
  0.6 30.2 %copy-start.5 = (bf16[4,512,128]{2,1,0:T(8,128)(2,1)S(1)}, bf16[4,512,128]{2,1,0:T(8,128)(2,1)}, u32[]{:S(2)}) copy-start(bf16[4,512,128]{2,1,0:T(8,128)(2,1)} %w3.1) | copy-start | bytes 1572868
  0.6 30.2 %copy-start.4 = (bf16[4,128,512]{2,1,0:T(8,128)(2,1)S(1)}, bf16[4,128,512]{2,1,0:T(8,128)(2,1)}, u32[]{:S(2)}) copy-start(bf16[4,128,512]{2,1,0:T(8,128)(2,1)} %w2.1) | copy-start | bytes 1572868
  3.1 27.7 %all-to-all-start = ((bf16[64,16,256]{2,1,0:T(8,128)(2,1)}), bf16[64,16,256]{2,1,0:T(8,128)(2,1)S(1)}, u32[]{:S(2)}, u32[]{:S(2)}) async-start(bf16[64,16,256]{2,1,0:T(8,128)(2,1)} %shard_map.109), calls=%async_computation | async-start | bytes 1048576 | tf_op jit(solution)/shard_map/all_to_all | solution.py:180
  34.5 38.7 %copy-start = (bf16[256,512]{1,0:T(8,128)(2,1)S(1)}, bf16[256,512]{1,0:T(8,128)(2,1)}, u32[]{:S(2)}) copy-start(bf16[256,512]{1,0:T(8,128)(2,1)} %x.1) | copy-start | bytes 786436
  34.5 38.7 %copy-start.1 = (bf16[256,512]{1,0:T(8,128)(2,1)S(1)}, bf16[256,512]{1,0:T(8,128)(2,1)}, u32[]{:S(2)}) copy-start(bf16[256,512]{1,0:T(8,128)(2,1)} %dy.1) | copy-start | bytes 786436
  34.5 38.7 %all-to-all-start.1 = ((bf16[64,16,256]{2,1,0:T(8,128)(2,1)}), bf16[64,16,256]{2,1,0:T(8,128)(2,1)S(1)}, u32[]{:S(2)}, u32[]{:S(2)}) async-start(bf16[64,16,256]{2,1,0:T(8,128)(2,1)} %get-tuple-element.19), calls=%async_computation.1 | async-start | bytes 1048576 | tf_op jit(solution)/shard_map/all_to_all | solution.py:180
  41.1 8.1 %collective-permute-start = (bf16[512,128]{1,0:T(8,128)(2,1)S(1)}, bf16[512,128]{1,0:T(8,128)(2,1)S(1)}, u32[]{:S(2)}, u32[]{:S(2)}) collective-permute-start(bf16[512,128]{1,0:T(8,128)(2,1)S(1)} %get-tuple-element.21), channel_id=1, source_target_pairs={{0,64},{64,0},{1,65},{65,1},{2,66},{66,2},{3,67},{67,3},{4,68},{68... | collective-permute-start | bytes 393224 | tf_op jit(solution)/shard_map/ppermute | solution.py:216
  49.2 21.0 %collective-permute-start.3 = (bf16[512,128]{1,0:T(8,128)(2,1)S(1)}, bf16[512,128]{1,0:T(8,128)(2,1)S(1)}, u32[]{:S(2)}, u32[]{:S(2)}) collective-permute-start(bf16[512,128]{1,0:T(8,128)(2,1)S(1)} %shard_map.111.rest_0_), channel_id=1, source_target_pairs={{0,384},{128,0},{256,128},{384,256},{1,385},{129,1},{257,129},{385... | collective-permute-start | bytes 393224 | tf_op jit(solution)/shard_map/ppermute | solution.py:219
  59.5 13.6 %collective-permute-start.2 = (bf16[512,128]{1,0:T(8,128)(2,1)S(1)}, bf16[512,128]{1,0:T(8,128)(2,1)S(1)}, u32[]{:S(2)}, u32[]{:S(2)}) collective-permute-start(bf16[512,128]{1,0:T(8,128)(2,1)S(1)} %shard_map.111.rest_0_), channel_id=1, source_target_pairs={{0,256},{128,384},{256,0},{384,128},{1,257},{129,385},{257,1},{385... | collective-permute-start | bytes 393224 | tf_op jit(solution)/shard_map/ppermute | solution.py:219
  61.5 11.7 %collective-permute-start.1 = (bf16[512,128]{1,0:T(8,128)(2,1)S(1)}, bf16[512,128]{1,0:T(8,128)(2,1)S(1)}, u32[]{:S(2)}, u32[]{:S(2)}) collective-permute-start(bf16[512,128]{1,0:T(8,128)(2,1)S(1)} %shard_map.111.rest_0_), channel_id=1, source_target_pairs={{0,128},{128,256},{256,384},{384,0},{1,129},{129,257},{257,385},{3... | collective-permute-start | bytes 393224 | tf_op jit(solution)/shard_map/ppermute | solution.py:219
  102.5 3.7 %copy-start.2 = (bf16[4,128,128]{2,1,0:T(8,128)(2,1)S(1)}, bf16[4,128,128]{2,1,0:T(8,128)(2,1)}, u32[]{:S(2)}) copy-start(bf16[4,128,128]{2,1,0:T(8,128)(2,1)} %w1.1) | copy-start | bytes 393220
  102.5 3.7 %copy-start.3 = (bf16[4,128,128]{2,1,0:T(8,128)(2,1)S(1)}, bf16[4,128,128]{2,1,0:T(8,128)(2,1)}, u32[]{:S(2)}) copy-start(bf16[4,128,128]{2,1,0:T(8,128)(2,1)} %w4.1) | copy-start | bytes 393220
  102.5 18.9 %all-to-all-start.4 = ((bf16[8,640,128]{2,1,0:T(8,128)(2,1)}), bf16[8,640,128]{2,1,0:T(8,128)(2,1)S(1)}, u32[]{:S(2)}, u32[]{:S(2)}) async-start(bf16[8,640,128]{2,1,0:T(8,128)(2,1)} %shard_map.115), calls=%async_computation.4 | async-start | bytes 2621440 | tf_op jit(solution)/shard_map/all_to_all | solution.py:180

commit v6 on v4

--- a/solution.py
+++ b/solution.py
@@ -145,31 +145,27 @@
     base = at[0] * mine
     collect(got, 0, local, mixed)
     collect(got, 1, local, d_down)
-    for zl in range(Z_LOW):
-        cols = pl.ds(zl * tokens, tokens)
-        downs, d_mixeds = [], []
-        for b in range(mine):
-            held = pl.ds(b * width, width)
-            h = dot(w2[base + b], mixed[held, cols], TN)
-            squared = h * h
-            half = 0.5 + 0.5 * jnp.tanh(h * (ROOT + (ROOT * CUBIC) * squared))
-            acted = (h * half).astype(BF)
-            gain = half + h * (half - half * half) * (2.0 * ROOT + (6.0 * ROOT * CUBIC) * squared)
-            d_act = dot(w3[base + b], d_down[held, cols], NN)
-            d_h = (d_act * gain).astype(BF)
-            downs.append(dot(w3[base + b], acted, TN))
-            d_mixeds.append(dot(w2[base + b], d_h, NN))
-            act[b, :, cols] = acted
-            d_pre[b, :, cols] = d_h
-        send[zl * groups : (zl + 1) * groups, :rows, :] = stack(*downs).astype(BF)
-        send[zl * groups : (zl + 1) * groups, rows:, :] = stack(*d_mixeds).astype(BF)
+    downs, d_mixeds = [], []
     for b in range(mine):
         held = pl.ds(b * width, width)
+        h = dot(w2[base + b], mixed[held, :], TN)
+        squared = h * h
+        half = 0.5 + 0.5 * jnp.tanh(h * (ROOT + (ROOT * CUBIC) * squared))
+        act[b] = (h * half).astype(BF)
+        gain = half + h * (half - half * half) * (2.0 * ROOT + (6.0 * ROOT * CUBIC) * squared)
+        d_pre[b] = (dot(w3[base + b], d_down[held, :], NN) * gain).astype(BF)
+        downs.append(dot(w3[base + b], act[b], TN))
+        d_mixeds.append(dot(w2[base + b], d_pre[b], NN))
         second = dot(mixed[held, :], d_pre[b], NT).astype(BF)
         for j in range(parts):
             part = slice(j * width, (j + 1) * width)
             grads[b, part, :] = second[:, part]
         grads[mine + b] = dot(act[b], d_down[held, :], NT).astype(BF)
+    for zl in range(Z_LOW):
+        cols = slice(zl * tokens, (zl + 1) * tokens)
+        members = slice(zl * groups, (zl + 1) * groups)
+        send[members, :rows, :] = stack(*[z[:, cols] for z in downs]).astype(BF)
+        send[members, rows:, :] = stack(*[z[:, cols] for z in d_mixeds]).astype(BF)
     for k in range(X_SIZE):
         shares[k][...] = grads[(at[1] + k) % X_SIZE]
 
@@ -286,6 +282,7 @@
         back, d_first, w_first, w_fourth,
         flops=4 * count * wide * width,
     )
+    got, output, grad_tokens = lax.optimization_barrier((got, output, grad_tokens))
     (total,) = call(
         add_kernel, [shape(hidden + width, width)], got, wide_sum, flops=4 * hidden * width
     )

time: 111 us -> 111 us (level)
  waiting for transfers between devices: 36.3 us -> 30.1 us
  blocking collectives: 34.4 us -> 39.8 us
    all_to_all x3, waiting for transfers between devices: 32.8 us -> 26.5 us  [exchange(): return lax.all_to_all(value, axes, split_axis=0, concat_axis=0, tiled=True)]
    all_to_all x1, blocking collectives: 11.3 us -> 16.7 us  [exchange(): return lax.all_to_all(value, axes, split_axis=0, concat_axis=0, tiled=True)]
where the time goes in v6:
time: 111 us; the launch traced here: 110 us
  blocking collectives  39.8 us (36%)
  waiting for transfers between devices  30.1 us (27%)
  starting transfers between devices  29.8 us (27%)
  Pallas kernels  9.58 us (9%)
    all_to_all x3, waiting for transfers between devices, exchange(): return lax.all_to_all(value, axes, split_axis=0, concat_axis=0, tiled=True)  26.5 us
    all_gather x1, blocking collectives, body(): got = lax.all_gather(total, 'far', axis=0, tiled=False)  23.1 us
    all_to_all x3, starting transfers between devices, exchange(): return lax.all_to_all(value, axes, split_axis=0, concat_axis=0, tiled=True)  18.3 us
    all_to_all x1, blocking collectives, exchange(): return lax.all_to_all(value, axes, split_axis=0, concat_axis=0, tiled=True)  16.7 us
    ppermute x3, starting transfers between devices, body(): lax.ppermute(share, 'x', [(i, (i + k) % X_SIZE) for i in range(X_SIZE)])  11.5 us
    pallas_call x7, Pallas kernels, call(): pl.pallas_call(kernel, out_shape=outs, compiler_params=pltpu.CompilerPara...  9.58 us
    ppermute x3, waiting for transfers between devices, body(): lax.ppermute(share, 'x', [(i, (i + k) % X_SIZE) for i in range(X_SIZE)])  3.53 us
  transfers between devices with their start and end apart: 6, of which 5 were waited for; matrix products, arithmetic and copies ran while one was open for 0% of the time, Pallas kernels for 1%

profile of v6, /device:TPU:8, one launch (start us, length us, event | category | flops | bytes accessed | tf_op | source)
XLA Modules:
  0.0 110.1 jit_solution(5715178103094493610)
XLA Ops:
  0.7 2.4 %shard_map.109 = bf16[32,32,256]{2,1,0:T(8,128)(2,1)} custom-call(bf16[256,512]{1,0:T(8,128)(2,1)} %x.1, bf16[4,128,128]{2,1,0:T(8,128)(2,1)} %w1.1, bf16[256,512]{1,0:T(8,128)(2,1)} %dy.1, bf16[4,128,128]{2,1,0:T(8,128)(2,1)} %w4.1), custom_call_target="tpu_custom_call" | custom-call | flops 67108864 | bytes 1310720 | tf_op jit(solution)/shard_map/pallas_call | solution.py:29
  3.1 9.5 %all-to-all-start = ((bf16[32,32,256]{2,1,0:T(8,128)(2,1)}), bf16[32,32,256]{2,1,0:T(8,128)(2,1)S(1)}, u32[]{:S(2)}, u32[]{:S(2)}) async-start(bf16[32,32,256]{2,1,0:T(8,128)(2,1)} %shard_map.109), calls=%async_computation | async-start | bytes 1048576 | tf_op jit(solution)/shard_map/all_to_all | solution.py:230
  12.6 0.1 pad_add_fusion.at
  12.7 17.7 %all-to-all-done.got = bf16[32,32,256]{2,1,0:T(8,128)(2,1)S(1)} async-done(((bf16[32,32,256]{2,1,0:T(8,128)(2,1)}), bf16[32,32,256]{2,1,0:T(8,128)(2,1)S(1)}, u32[]{:S(2)}, u32[]{:S(2)}) %all-to-all-start) | async-done | bytes 524320 | tf_op jit(solution)/shard_map/all_to_all | solution.py:230
  30.4 3.4 %shard_map.110 = (bf16[32,32,256]{2,1,0:T(8,128)(2,1)}, bf16[512,128]{1,0:T(8,128)(2,1)S(1)}, bf16[512,128]{1,0:T(8,128)(2,1)S(1)}, bf16[512,128]{1,0:T(8,128)(2,1)S(1)}, bf16[512,128]{1,0:T(8,128)(2,1)S(1)}) custom-call(s32[2]{0:T(128)S(1)} %pad_add_fusion.at, bf16[32,32,256]{2,1,0:T(8,128)(2,1)S(1)} %all-to-all-done.got, ...), custom_call_target="tpu_custom_call" | custom-call | flops 805306368 | bytes 2621448 | tf_op jit(solution)/shard_map/pallas_call | solution.py:29
  33.8 4.5 %all-to-all-start.1 = ((bf16[32,32,256]{2,1,0:T(8,128)(2,1)}), bf16[32,32,256]{2,1,0:T(8,128)(2,1)S(1)}, u32[]{:S(2)}, u32[]{:S(2)}) async-start(bf16[32,32,256]{2,1,0:T(8,128)(2,1)} %get-tuple-element.24), calls=%async_computation.1 | async-start | bytes 1048576 | tf_op jit(solution)/shard_map/all_to_all | solution.py:230
  38.2 0.0 copy-start.2
  38.3 0.0 copy-start.3
  38.3 3.5 %collective-permute-start = (bf16[512,128]{1,0:T(8,128)(2,1)S(1)}, bf16[512,128]{1,0:T(8,128)(2,1)S(1)}, u32[]{:S(2)}, u32[]{:S(2)}) collective-permute-start(bf16[512,128]{1,0:T(8,128)(2,1)S(1)} %get-tuple-element.26), channel_id=1, source_target_pairs={{0,16},{16,32},{32,48},{48,0},{1,17},{17,33},{33,49},{49,1},{2,18}... | collective-permute-start | bytes 393224 | tf_op jit(solution)/shard_map/ppermute | solution.py:267
  41.8 4.6 %collective-permute-start.1 = (bf16[512,128]{1,0:T(8,128)(2,1)S(1)}, bf16[512,128]{1,0:T(8,128)(2,1)S(1)}, u32[]{:S(2)}, u32[]{:S(2)}) collective-permute-start(bf16[512,128]{1,0:T(8,128)(2,1)S(1)} %get-tuple-element.27), channel_id=1, source_target_pairs={{0,32},{16,48},{32,0},{48,16},{1,33},{17,49},{33,1},{49,17},{2,34}... | collective-permute-start | bytes 393224 | tf_op jit(solution)/shard_map/ppermute | solution.py:267
  46.5 3.3 %collective-permute-start.2 = (bf16[512,128]{1,0:T(8,128)(2,1)S(1)}, bf16[512,128]{1,0:T(8,128)(2,1)S(1)}, u32[]{:S(2)}, u32[]{:S(2)}) collective-permute-start(bf16[512,128]{1,0:T(8,128)(2,1)S(1)} %get-tuple-element.28), channel_id=1, source_target_pairs={{0,48},{16,0},{32,16},{48,32},{1,49},{17,1},{33,17},{49,33},{2,50}... | collective-permute-start | bytes 393224 | tf_op jit(solution)/shard_map/ppermute | solution.py:267
  49.8 0.0 collective-permute-done.rest_1_
  49.8 1.0 collective-permute-done.1.rest_2_
  50.8 2.5 %collective-permute-done.2.rest_3_ = bf16[512,128]{1,0:T(8,128)(2,1)S(1)} collective-permute-done((bf16[512,128]{1,0:T(8,128)(2,1)S(1)}, bf16[512,128]{1,0:T(8,128)(2,1)S(1)}, u32[]{:S(2)}, u32[]{:S(2)}) %collective-permute-start.2) | collective-permute-done | bytes 131104 | tf_op jit(solution)/shard_map/ppermute | solution.py:267
  53.3 2.8 %all-to-all-done.1.got = bf16[32,32,256]{2,1,0:T(8,128)(2,1)S(1)} async-done(((bf16[32,32,256]{2,1,0:T(8,128)(2,1)}), bf16[32,32,256]{2,1,0:T(8,128)(2,1)S(1)}, u32[]{:S(2)}, u32[]{:S(2)}) %all-to-all-start.1) | async-done | bytes 524320 | tf_op jit(solution)/shard_map/all_to_all | solution.py:230
  56.1 0.0 copy-done
  56.1 1.3 %shard_map.111 = (bf16[512,256]{1,0:T(8,128)(2,1)S(1)}, bf16[512,256]{1,0:T(8,128)(2,1)S(1)}, bf16[8,128,128]{2,1,0:T(8,128)(2,1)}, bf16[512,128]{1,0:T(8,128)(2,1)S(1)}) custom-call(bf16[32,32,256]{2,1,0:T(8,128)(2,1)S(1)} %all-to-all-done.1.got, bf16[256,512]{1,0:T(8,128)(2,1)S(1)} %copy-done, bf16[256,512]{1,0:T(8,128)(2,1)S(1)} %copy-done.1, ...), custom_call_target="tpu_custom_call" | custom-call | flops 134217728 | bytes 2490368 | tf_op jit(solution)/shard_map/pallas_call | solution.py:29
  57.4 4.3 %all-to-all-start.2 = ((bf16[8,128,128]{2,1,0:T(8,128)(2,1)}), bf16[8,128,128]{2,1,0:T(8,128)(2,1)S(1)}, u32[]{:S(2)}, u32[]{:S(2)}) async-start(bf16[8,128,128]{2,1,0:T(8,128)(2,1)} %get-tuple-element.29), calls=%async_computation.2 | async-start | bytes 524288 | tf_op jit(solution)/shard_map/all_to_all | solution.py:230
  61.7 1.1 %shard_map.112 = (bf16[256,512]{1,0:T(8,128)(2,1)}, bf16[256,512]{1,0:T(8,128)(2,1)}) custom-call(bf16[512,256]{1,0:T(8,128)(2,1)S(1)} %get-tuple-element.30.back, bf16[512,256]{1,0:T(8,128)(2,1)S(1)} %get-tuple-element.31.d_first, bf16[4,128,128]{2,1,0:T(8,128)(2,1)S(1)} %copy-done.2, bf16[4,128,128]{2,1,0:T(8,128)(2,1)S(1)} %copy-done.3), custom_call_target="tpu_custom_call" | custom-call | flops 67108864 | bytes 1310720 | tf_op jit(solution)/shard_map/pallas_call | solution.py:29
  62.9 6.1 %all-to-all-done.2.got = bf16[8,128,128]{2,1,0:T(8,128)(2,1)S(1)} async-done(((bf16[8,128,128]{2,1,0:T(8,128)(2,1)}), bf16[8,128,128]{2,1,0:T(8,128)(2,1)S(1)}, u32[]{:S(2)}, u32[]{:S(2)}) %all-to-all-start.2) | async-done | bytes 262176 | tf_op jit(solution)/shard_map/all_to_all | solution.py:230
  69.0 23.1 %all-gather = bf16[2560,128]{1,0:T(8,128)(2,1)S(1)} all-gather(bf16[640,128]{1,0:T(8,128)(2,1)S(1)} %shard_map.113), channel_id=2, replica_groups=mesh['far'=4,'zl'=2,'x'=4,'hidden'=16] {'far'}, dimensions={0}, use_global_device_ids=true | all-gather | bytes 819200 | tf_op jit(solution)/shard_map/all_gather | solution.py:289
  92.1 0.1 shard_map.114
  92.2 16.7 %all_to_all.20.got = bf16[8,640,128]{2,1,0:T(8,128)(2,1)S(1)} all-to-all(bf16[8,640,128]{2,1,0:T(8,128)(2,1)S(1)} %shard_map.114), channel_id=1, replica_groups=mesh['far'=4,'zl'=2,'x'=4,'hidden'=16] {'zl','x'}, dimensions={0} | all-to-all | bytes 2621440 | tf_op jit(solution)/shard_map/all_to_all | solution.py:230
  108.9 1.2 %shard_map.115 = (bf16[4,128,128]{2,1,0:T(8,128)(2,1)}, bf16[4,128,512]{2,1,0:T(8,128)(2,1)}, bf16[4,512,128]{2,1,0:T(8,128)(2,1)}, bf16[4,128,128]{2,1,0:T(8,128)(2,1)}) custom-call(bf16[8,640,128]{2,1,0:T(8,128)(2,1)S(1)} %all_to_all.20.got), custom_call_target="tpu_custom_call" | custom-call | bytes 2621440 | tf_op jit(solution)/shard_map/pallas_call | solution.py:29
  (10 shorter events, 0.1 us)
Async XLA Ops:
  0.6 29.7 %copy-start.5 = (bf16[4,512,128]{2,1,0:T(8,128)(2,1)S(1)}, bf16[4,512,128]{2,1,0:T(8,128)(2,1)}, u32[]{:S(2)}) copy-start(bf16[4,512,128]{2,1,0:T(8,128)(2,1)} %w3.1) | copy-start | bytes 1572868
  0.6 29.7 %copy-start.4 = (bf16[4,128,512]{2,1,0:T(8,128)(2,1)S(1)}, bf16[4,128,512]{2,1,0:T(8,128)(2,1)}, u32[]{:S(2)}) copy-start(bf16[4,128,512]{2,1,0:T(8,128)(2,1)} %w2.1) | copy-start | bytes 1572868
  3.1 27.3 %all-to-all-start = ((bf16[32,32,256]{2,1,0:T(8,128)(2,1)}), bf16[32,32,256]{2,1,0:T(8,128)(2,1)S(1)}, u32[]{:S(2)}, u32[]{:S(2)}) async-start(bf16[32,32,256]{2,1,0:T(8,128)(2,1)} %shard_map.109), calls=%async_computation | async-start | bytes 1048576 | tf_op jit(solution)/shard_map/all_to_all | solution.py:230
  12.7 43.4 %copy-start = (bf16[256,512]{1,0:T(8,128)(2,1)S(1)}, bf16[256,512]{1,0:T(8,128)(2,1)}, u32[]{:S(2)}) copy-start(bf16[256,512]{1,0:T(8,128)(2,1)} %x.1) | copy-start | bytes 786436
  12.7 43.4 %copy-start.1 = (bf16[256,512]{1,0:T(8,128)(2,1)S(1)}, bf16[256,512]{1,0:T(8,128)(2,1)}, u32[]{:S(2)}) copy-start(bf16[256,512]{1,0:T(8,128)(2,1)} %dy.1) | copy-start | bytes 786436
  33.8 22.3 %all-to-all-start.1 = ((bf16[32,32,256]{2,1,0:T(8,128)(2,1)}), bf16[32,32,256]{2,1,0:T(8,128)(2,1)S(1)}, u32[]{:S(2)}, u32[]{:S(2)}) async-start(bf16[32,32,256]{2,1,0:T(8,128)(2,1)} %get-tuple-element.24), calls=%async_computation.1 | async-start | bytes 1048576 | tf_op jit(solution)/shard_map/all_to_all | solution.py:230
  38.2 23.5 %copy-start.2 = (bf16[4,128,128]{2,1,0:T(8,128)(2,1)S(1)}, bf16[4,128,128]{2,1,0:T(8,128)(2,1)}, u32[]{:S(2)}) copy-start(bf16[4,128,128]{2,1,0:T(8,128)(2,1)} %w1.1) | copy-start | bytes 393220
  38.3 23.5 %copy-start.3 = (bf16[4,128,128]{2,1,0:T(8,128)(2,1)S(1)}, bf16[4,128,128]{2,1,0:T(8,128)(2,1)}, u32[]{:S(2)}) copy-start(bf16[4,128,128]{2,1,0:T(8,128)(2,1)} %w4.1) | copy-start | bytes 393220
  38.3 11.5 %collective-permute-start = (bf16[512,128]{1,0:T(8,128)(2,1)S(1)}, bf16[512,128]{1,0:T(8,128)(2,1)S(1)}, u32[]{:S(2)}, u32[]{:S(2)}) collective-permute-start(bf16[512,128]{1,0:T(8,128)(2,1)S(1)} %get-tuple-element.26), channel_id=1, source_target_pairs={{0,16},{16,32},{32,48},{48,0},{1,17},{17,33},{33,49},{49,1},{2,18}... | collective-permute-start | bytes 393224 | tf_op jit(solution)/shard_map/ppermute | solution.py:267
  41.8 9.0 %collective-permute-start.1 = (bf16[512,128]{1,0:T(8,128)(2,1)S(1)}, bf16[512,128]{1,0:T(8,128)(2,1)S(1)}, u32[]{:S(2)}, u32[]{:S(2)}) collective-permute-start(bf16[512,128]{1,0:T(8,128)(2,1)S(1)} %get-tuple-element.27), channel_id=1, source_target_pairs={{0,32},{16,48},{32,0},{48,16},{1,33},{17,49},{33,1},{49,17},{2,34}... | collective-permute-start | bytes 393224 | tf_op jit(solution)/shard_map/ppermute | solution.py:267
  46.5 6.9 %collective-permute-start.2 = (bf16[512,128]{1,0:T(8,128)(2,1)S(1)}, bf16[512,128]{1,0:T(8,128)(2,1)S(1)}, u32[]{:S(2)}, u32[]{:S(2)}) collective-permute-start(bf16[512,128]{1,0:T(8,128)(2,1)S(1)} %get-tuple-element.28), channel_id=1, source_target_pairs={{0,48},{16,0},{32,16},{48,32},{1,49},{17,1},{33,17},{49,33},{2,50}... | collective-permute-start | bytes 393224 | tf_op jit(solution)/shard_map/ppermute | solution.py:267
  57.4 11.5 %all-to-all-start.2 = ((bf16[8,128,128]{2,1,0:T(8,128)(2,1)}), bf16[8,128,128]{2,1,0:T(8,128)(2,1)S(1)}, u32[]{:S(2)}, u32[]{:S(2)}) async-start(bf16[8,128,128]{2,1,0:T(8,128)(2,1)} %get-tuple-element.29), calls=%async_computation.2 | async-start | bytes 524288 | tf_op jit(solution)/shard_map/all_to_all | solution.py:230

commit v7 on v6

--- a/solution.py
+++ b/solution.py
@@ -136,7 +136,7 @@
 
 
 def middle_kernel(groups, at, got, w2, w3, send, *rest):
-    shares, (mixed, d_down, act, d_pre, grads) = rest[:X_SIZE], rest[X_SIZE:]
+    shares, (mixed, d_down, act, d_pre, grads, ready, left) = rest[:X_SIZE], rest[X_SIZE:]
     local, width, hidden = w2.shape
     mine = local // Z_LOW
     tokens = got.shape[2]
@@ -145,7 +145,6 @@
     base = at[0] * mine
     collect(got, 0, local, mixed)
     collect(got, 1, local, d_down)
-    downs, d_mixeds = [], []
     for b in range(mine):
         held = pl.ds(b * width, width)
         h = dot(w2[base + b], mixed[held, :], TN)
@@ -154,36 +153,57 @@
         act[b] = (h * half).astype(BF)
         gain = half + h * (half - half * half) * (2.0 * ROOT + (6.0 * ROOT * CUBIC) * squared)
         d_pre[b] = (dot(w3[base + b], d_down[held, :], NN) * gain).astype(BF)
-        downs.append(dot(w3[base + b], act[b], TN))
-        d_mixeds.append(dot(w2[base + b], d_pre[b], NN))
+    leaving = []
+    for k, (w, value, dims) in enumerate(((w3, act, TN), (w2, d_pre, NN))):
+        results = [dot(w[base + b], value[b], dims) for b in range(mine)]
+        part = slice(k * rows, (k + 1) * rows)
+        for zl in range(Z_LOW):
+            cols = slice(zl * tokens, (zl + 1) * tokens)
+            members = slice(zl * groups, (zl + 1) * groups)
+            ready[members, part, :] = stack(*[z[:, cols] for z in results]).astype(BF)
+        part = pl.ds(k * rows, rows)
+        copy = pltpu.make_async_copy(ready.at[:, part, :], send.at[:, part, :], left.at[k])
+        copy.start()
+        leaving.append(copy)
+    for b in range(mine):
+        held = pl.ds(b * width, width)
         second = dot(mixed[held, :], d_pre[b], NT).astype(BF)
         for j in range(parts):
             part = slice(j * width, (j + 1) * width)
             grads[b, part, :] = second[:, part]
         grads[mine + b] = dot(act[b], d_down[held, :], NT).astype(BF)
-    for zl in range(Z_LOW):
-        cols = slice(zl * tokens, (zl + 1) * tokens)
-        members = slice(zl * groups, (zl + 1) * groups)
-        send[members, :rows, :] = stack(*[z[:, cols] for z in downs]).astype(BF)
-        send[members, rows:, :] = stack(*[z[:, cols] for z in d_mixeds]).astype(BF)
     for k in range(X_SIZE):
         shares[k][...] = grads[(at[1] + k) % X_SIZE]
+    for copy in leaving:
+        copy.wait()
 
 
 def leave_kernel(got, x, dy, *rest):
-    *shares, back, d_first, grads, wide_sum = rest
+    *shares, back, d_first, grads, wide_sum, ready, left = rest
+    parts, width, _ = ready.shape
+    local = parts // 2
+    leaving = []
+
+    def leave(k, value):
+        ready[k] = value.astype(BF)
+        copy = pltpu.make_async_copy(ready.at[k], grads.at[k], left.at[k])
+        copy.start()
+        leaving.append(copy)
+
+    collect_back(got, 0, local, back)
+    for b in range(local):
+        rows = pl.ds(b * width, width)
+        leave(local + b, dot(back[rows, :], dy[:, rows], NN))
+    collect_back(got, 1, local, d_first)
+    for b in range(local):
+        rows = pl.ds(b * width, width)
+        leave(b, dot(x[:, rows], d_first[rows, :], TT))
     acc = shares[0][...].astype(F32)
     for share in shares[1:]:
         acc = acc + share[...].astype(F32)
     wide_sum[...] = acc.astype(BF)
-    parts, width, _ = grads.shape
-    local = parts // 2
-    collect_back(got, 0, local, back)
-    collect_back(got, 1, local, d_first)
-    for b in range(local):
-        rows = pl.ds(b * width, width)
-        grads[b] = dot(x[:, rows], d_first[rows, :], TT).astype(BF)
-        grads[local + b] = dot(back[rows, :], dy[:, rows], NN).astype(BF)
+    for copy in leaving:
+        copy.wait()
 
 
 def outputs_kernel(back, d_first, w1, w4, output, grad_tokens):
@@ -260,7 +280,9 @@
         in_specs=[pl.BlockSpec(memory_space=pltpu.SMEM)] + [pl.BlockSpec()] * 3,
         scratch_shapes=[pltpu.VMEM((mine * width, both), BF)] * 2
         + [pltpu.VMEM((mine, hidden, both), BF)] * 2
-        + [pltpu.VMEM((X_SIZE, hidden, width), BF)],
+        + [pltpu.VMEM((X_SIZE, hidden, width), BF), pltpu.VMEM(got.shape, BF)]
+        + [pltpu.SemaphoreType.DMA((2,))],
+        out_specs=[pl.BlockSpec(memory_space=pl.ANY)] + [pl.BlockSpec()] * X_SIZE,
     )
     got = exchange(send, middle)
     shares = [
@@ -275,6 +297,12 @@
         ],
         got, tokens, upstream, *shares,
         flops=8 * count * wide * width,
+        out_specs=[
+            pl.BlockSpec(), pl.BlockSpec(), pl.BlockSpec(memory_space=pl.ANY), pl.BlockSpec(),
+        ],
+        scratch_shapes=[
+            pltpu.VMEM((parts, width, width), BF), pltpu.SemaphoreType.DMA((parts,)),
+        ],
     )
     got = exchange(grads, near)
     output, grad_tokens = call(

time: 111 us -> 110 us (level)
  no operation moved by 1% of the time
where the time goes in v7:
time: 110 us
  blocking collectives  39.8 us (36%)
  waiting for transfers between devices  30.1 us (27%)
  starting transfers between devices  29.8 us (27%)
  Pallas kernels  9.34 us (8%)
    all_to_all x3, waiting for transfers between devices, exchange(): return lax.all_to_all(value, axes, split_axis=0, concat_axis=0, tiled=True)  26.5 us
    all_gather x1, blocking collectives, body(): got = lax.all_gather(total, 'far', axis=0, tiled=False)  23 us
    all_to_all x3, starting transfers between devices, exchange(): return lax.all_to_all(value, axes, split_axis=0, concat_axis=0, tiled=True)  18.3 us
    all_to_all x1, blocking collectives, exchange(): return lax.all_to_all(value, axes, split_axis=0, concat_axis=0, tiled=True)  16.8 us
    ppermute x3, starting transfers between devices, body(): lax.ppermute(share, 'x', [(i, (i + k) % X_SIZE) for i in range(X_SIZE)])  11.5 us
    pallas_call x7, Pallas kernels, call(): pl.pallas_call(kernel, out_shape=outs, compiler_params=pltpu.CompilerPara...  9.34 us
    ppermute x3, waiting for transfers between devices, body(): lax.ppermute(share, 'x', [(i, (i + k) % X_SIZE) for i in range(X_SIZE)])  3.53 us
  transfers between devices with their start and end apart: 6, of which 5 were waited for; matrix products, arithmetic and copies ran while one was open for 0% of the time, Pallas kernels for 1%

profile of v7, /device:TPU:8, one launch (start us, length us, event | category | flops | bytes accessed | tf_op | source)
XLA Modules:
  0.0 109.9 jit_solution(3657691607160704430)
XLA Ops:
  0.7 2.4 %shard_map.109 = bf16[32,32,256]{2,1,0:T(8,128)(2,1)} custom-call(bf16[256,512]{1,0:T(8,128)(2,1)} %x.1, bf16[4,128,128]{2,1,0:T(8,128)(2,1)} %w1.1, bf16[256,512]{1,0:T(8,128)(2,1)} %dy.1, bf16[4,128,128]{2,1,0:T(8,128)(2,1)} %w4.1), custom_call_target="tpu_custom_call" | custom-call | flops 67108864 | bytes 1310720 | tf_op jit(solution)/shard_map/pallas_call | solution.py:29
  3.1 9.5 %all-to-all-start = ((bf16[32,32,256]{2,1,0:T(8,128)(2,1)}), bf16[32,32,256]{2,1,0:T(8,128)(2,1)S(1)}, u32[]{:S(2)}, u32[]{:S(2)}) async-start(bf16[32,32,256]{2,1,0:T(8,128)(2,1)} %shard_map.109), calls=%async_computation | async-start | bytes 1048576 | tf_op jit(solution)/shard_map/all_to_all | solution.py:250
  12.6 0.1 pad_add_fusion.at
  12.7 17.7 %all-to-all-done.got = bf16[32,32,256]{2,1,0:T(8,128)(2,1)S(1)} async-done(((bf16[32,32,256]{2,1,0:T(8,128)(2,1)}), bf16[32,32,256]{2,1,0:T(8,128)(2,1)S(1)}, u32[]{:S(2)}, u32[]{:S(2)}) %all-to-all-start) | async-done | bytes 524320 | tf_op jit(solution)/shard_map/all_to_all | solution.py:250
  30.4 3.1 %shard_map.110 = (bf16[32,32,256]{2,1,0:T(8,128)(2,1)}, bf16[512,128]{1,0:T(8,128)(2,1)S(1)}, bf16[512,128]{1,0:T(8,128)(2,1)S(1)}, bf16[512,128]{1,0:T(8,128)(2,1)S(1)}, bf16[512,128]{1,0:T(8,128)(2,1)S(1)}) custom-call(s32[2]{0:T(128)S(1)} %pad_add_fusion.at, bf16[32,32,256]{2,1,0:T(8,128)(2,1)S(1)} %all-to-all-done.got, ...), custom_call_target="tpu_custom_call" | custom-call | flops 805306368 | bytes 2621448 | tf_op jit(solution)/shard_map/pallas_call | solution.py:29
  33.5 4.5 %all-to-all-start.1 = ((bf16[32,32,256]{2,1,0:T(8,128)(2,1)}), bf16[32,32,256]{2,1,0:T(8,128)(2,1)S(1)}, u32[]{:S(2)}, u32[]{:S(2)}) async-start(bf16[32,32,256]{2,1,0:T(8,128)(2,1)} %get-tuple-element.24), calls=%async_computation.1 | async-start | bytes 1048576 | tf_op jit(solution)/shard_map/all_to_all | solution.py:250
  38.0 0.0 copy-start.2
  38.0 0.0 copy-start.3
  38.0 3.5 %collective-permute-start = (bf16[512,128]{1,0:T(8,128)(2,1)S(1)}, bf16[512,128]{1,0:T(8,128)(2,1)S(1)}, u32[]{:S(2)}, u32[]{:S(2)}) collective-permute-start(bf16[512,128]{1,0:T(8,128)(2,1)S(1)} %get-tuple-element.26), channel_id=1, source_target_pairs={{0,16},{16,32},{32,48},{48,0},{1,17},{17,33},{33,49},{49,1},{2,18}... | collective-permute-start | bytes 393224 | tf_op jit(solution)/shard_map/ppermute | solution.py:289
  41.6 4.6 %collective-permute-start.1 = (bf16[512,128]{1,0:T(8,128)(2,1)S(1)}, bf16[512,128]{1,0:T(8,128)(2,1)S(1)}, u32[]{:S(2)}, u32[]{:S(2)}) collective-permute-start(bf16[512,128]{1,0:T(8,128)(2,1)S(1)} %get-tuple-element.27), channel_id=1, source_target_pairs={{0,32},{16,48},{32,0},{48,16},{1,33},{17,49},{33,1},{49,17},{2,34}... | collective-permute-start | bytes 393224 | tf_op jit(solution)/shard_map/ppermute | solution.py:289
  46.2 3.3 %collective-permute-start.2 = (bf16[512,128]{1,0:T(8,128)(2,1)S(1)}, bf16[512,128]{1,0:T(8,128)(2,1)S(1)}, u32[]{:S(2)}, u32[]{:S(2)}) collective-permute-start(bf16[512,128]{1,0:T(8,128)(2,1)S(1)} %get-tuple-element.28), channel_id=1, source_target_pairs={{0,48},{16,0},{32,16},{48,32},{1,49},{17,1},{33,17},{49,33},{2,50}... | collective-permute-start | bytes 393224 | tf_op jit(solution)/shard_map/ppermute | solution.py:289
  49.5 0.0 collective-permute-done.rest_1_
  49.6 1.0 collective-permute-done.1.rest_2_
  50.6 2.5 %collective-permute-done.2.rest_3_ = bf16[512,128]{1,0:T(8,128)(2,1)S(1)} collective-permute-done((bf16[512,128]{1,0:T(8,128)(2,1)S(1)}, bf16[512,128]{1,0:T(8,128)(2,1)S(1)}, u32[]{:S(2)}, u32[]{:S(2)}) %collective-permute-start.2) | collective-permute-done | bytes 131104 | tf_op jit(solution)/shard_map/ppermute | solution.py:289
  53.1 2.8 %all-to-all-done.1.got = bf16[32,32,256]{2,1,0:T(8,128)(2,1)S(1)} async-done(((bf16[32,32,256]{2,1,0:T(8,128)(2,1)}), bf16[32,32,256]{2,1,0:T(8,128)(2,1)S(1)}, u32[]{:S(2)}, u32[]{:S(2)}) %all-to-all-start.1) | async-done | bytes 524320 | tf_op jit(solution)/shard_map/all_to_all | solution.py:250
  55.9 1.4 %shard_map.111 = (bf16[512,256]{1,0:T(8,128)(2,1)S(1)}, bf16[512,256]{1,0:T(8,128)(2,1)S(1)}, bf16[8,128,128]{2,1,0:T(8,128)(2,1)}, bf16[512,128]{1,0:T(8,128)(2,1)S(1)}) custom-call(bf16[32,32,256]{2,1,0:T(8,128)(2,1)S(1)} %all-to-all-done.1.got, bf16[256,512]{1,0:T(8,128)(2,1)S(1)} %copy-done, bf16[256,512]{1,0:T(8,128)(2,1)S(1)} %copy-done.1, ...), custom_call_target="tpu_custom_call" | custom-call | flops 134217728 | bytes 2490368 | tf_op jit(solution)/shard_map/pallas_call | solution.py:29
  57.2 4.3 %all-to-all-start.2 = ((bf16[8,128,128]{2,1,0:T(8,128)(2,1)}), bf16[8,128,128]{2,1,0:T(8,128)(2,1)S(1)}, u32[]{:S(2)}, u32[]{:S(2)}) async-start(bf16[8,128,128]{2,1,0:T(8,128)(2,1)} %get-tuple-element.29), calls=%async_computation.2 | async-start | bytes 524288 | tf_op jit(solution)/shard_map/all_to_all | solution.py:250
  61.5 0.0 copy-done.3
  61.5 1.1 %shard_map.112 = (bf16[256,512]{1,0:T(8,128)(2,1)}, bf16[256,512]{1,0:T(8,128)(2,1)}) custom-call(bf16[512,256]{1,0:T(8,128)(2,1)S(1)} %get-tuple-element.30.back, bf16[512,256]{1,0:T(8,128)(2,1)S(1)} %get-tuple-element.31.d_first, bf16[4,128,128]{2,1,0:T(8,128)(2,1)S(1)} %copy-done.2, bf16[4,128,128]{2,1,0:T(8,128)(2,1)S(1)} %copy-done.3), custom_call_target="tpu_custom_call" | custom-call | flops 67108864 | bytes 1310720 | tf_op jit(solution)/shard_map/pallas_call | solution.py:29
  62.7 6.1 %all-to-all-done.2.got = bf16[8,128,128]{2,1,0:T(8,128)(2,1)S(1)} async-done(((bf16[8,128,128]{2,1,0:T(8,128)(2,1)}), bf16[8,128,128]{2,1,0:T(8,128)(2,1)S(1)}, u32[]{:S(2)}, u32[]{:S(2)}) %all-to-all-start.2) | async-done | bytes 262176 | tf_op jit(solution)/shard_map/all_to_all | solution.py:250
  68.8 23.0 %all-gather = bf16[2560,128]{1,0:T(8,128)(2,1)S(1)} all-gather(bf16[640,128]{1,0:T(8,128)(2,1)S(1)} %shard_map.113), channel_id=2, replica_groups=mesh['far'=4,'zl'=2,'x'=4,'hidden'=16] {'far'}, dimensions={0}, use_global_device_ids=true | all-gather | bytes 819200 | tf_op jit(solution)/shard_map/all_gather | solution.py:317
  91.8 0.1 shard_map.114
  91.9 16.8 %all_to_all.20.got = bf16[8,640,128]{2,1,0:T(8,128)(2,1)S(1)} all-to-all(bf16[8,640,128]{2,1,0:T(8,128)(2,1)S(1)} %shard_map.114), channel_id=1, replica_groups=mesh['far'=4,'zl'=2,'x'=4,'hidden'=16] {'zl','x'}, dimensions={0} | all-to-all | bytes 2621440 | tf_op jit(solution)/shard_map/all_to_all | solution.py:250
  108.7 1.2 %shard_map.115 = (bf16[4,128,128]{2,1,0:T(8,128)(2,1)}, bf16[4,128,512]{2,1,0:T(8,128)(2,1)}, bf16[4,512,128]{2,1,0:T(8,128)(2,1)}, bf16[4,128,128]{2,1,0:T(8,128)(2,1)}) custom-call(bf16[8,640,128]{2,1,0:T(8,128)(2,1)S(1)} %all_to_all.20.got), custom_call_target="tpu_custom_call" | custom-call | bytes 2621440 | tf_op jit(solution)/shard_map/pallas_call | solution.py:29
  (10 shorter events, 0.1 us)
Async XLA Ops:
  0.6 29.7 %copy-start.5 = (bf16[4,512,128]{2,1,0:T(8,128)(2,1)S(1)}, bf16[4,512,128]{2,1,0:T(8,128)(2,1)}, u32[]{:S(2)}) copy-start(bf16[4,512,128]{2,1,0:T(8,128)(2,1)} %w3.1) | copy-start | bytes 1572868
  0.6 29.7 %copy-start.4 = (bf16[4,128,512]{2,1,0:T(8,128)(2,1)S(1)}, bf16[4,128,512]{2,1,0:T(8,128)(2,1)}, u32[]{:S(2)}) copy-start(bf16[4,128,512]{2,1,0:T(8,128)(2,1)} %w2.1) | copy-start | bytes 1572868
  3.1 27.3 %all-to-all-start = ((bf16[32,32,256]{2,1,0:T(8,128)(2,1)}), bf16[32,32,256]{2,1,0:T(8,128)(2,1)S(1)}, u32[]{:S(2)}, u32[]{:S(2)}) async-start(bf16[32,32,256]{2,1,0:T(8,128)(2,1)} %shard_map.109), calls=%async_computation | async-start | bytes 1048576 | tf_op jit(solution)/shard_map/all_to_all | solution.py:250
  12.7 43.2 %copy-start = (bf16[256,512]{1,0:T(8,128)(2,1)S(1)}, bf16[256,512]{1,0:T(8,128)(2,1)}, u32[]{:S(2)}) copy-start(bf16[256,512]{1,0:T(8,128)(2,1)} %x.1) | copy-start | bytes 786436
  12.7 43.2 %copy-start.1 = (bf16[256,512]{1,0:T(8,128)(2,1)S(1)}, bf16[256,512]{1,0:T(8,128)(2,1)}, u32[]{:S(2)}) copy-start(bf16[256,512]{1,0:T(8,128)(2,1)} %dy.1) | copy-start | bytes 786436
  33.5 22.4 %all-to-all-start.1 = ((bf16[32,32,256]{2,1,0:T(8,128)(2,1)}), bf16[32,32,256]{2,1,0:T(8,128)(2,1)S(1)}, u32[]{:S(2)}, u32[]{:S(2)}) async-start(bf16[32,32,256]{2,1,0:T(8,128)(2,1)} %get-tuple-element.24), calls=%async_computation.1 | async-start | bytes 1048576 | tf_op jit(solution)/shard_map/all_to_all | solution.py:250
  38.0 23.5 %copy-start.2 = (bf16[4,128,128]{2,1,0:T(8,128)(2,1)S(1)}, bf16[4,128,128]{2,1,0:T(8,128)(2,1)}, u32[]{:S(2)}) copy-start(bf16[4,128,128]{2,1,0:T(8,128)(2,1)} %w1.1) | copy-start | bytes 393220
  38.0 23.5 %copy-start.3 = (bf16[4,128,128]{2,1,0:T(8,128)(2,1)S(1)}, bf16[4,128,128]{2,1,0:T(8,128)(2,1)}, u32[]{:S(2)}) copy-start(bf16[4,128,128]{2,1,0:T(8,128)(2,1)} %w4.1) | copy-start | bytes 393220
  38.0 11.5 %collective-permute-start = (bf16[512,128]{1,0:T(8,128)(2,1)S(1)}, bf16[512,128]{1,0:T(8,128)(2,1)S(1)}, u32[]{:S(2)}, u32[]{:S(2)}) collective-permute-start(bf16[512,128]{1,0:T(8,128)(2,1)S(1)} %get-tuple-element.26), channel_id=1, source_target_pairs={{0,16},{16,32},{32,48},{48,0},{1,17},{17,33},{33,49},{49,1},{2,18}... | collective-permute-start | bytes 393224 | tf_op jit(solution)/shard_map/ppermute | solution.py:289
  41.6 9.0 %collective-permute-start.1 = (bf16[512,128]{1,0:T(8,128)(2,1)S(1)}, bf16[512,128]{1,0:T(8,128)(2,1)S(1)}, u32[]{:S(2)}, u32[]{:S(2)}) collective-permute-start(bf16[512,128]{1,0:T(8,128)(2,1)S(1)} %get-tuple-element.27), channel_id=1, source_target_pairs={{0,32},{16,48},{32,0},{48,16},{1,33},{17,49},{33,1},{49,17},{2,34}... | collective-permute-start | bytes 393224 | tf_op jit(solution)/shard_map/ppermute | solution.py:289
  46.2 6.9 %collective-permute-start.2 = (bf16[512,128]{1,0:T(8,128)(2,1)S(1)}, bf16[512,128]{1,0:T(8,128)(2,1)S(1)}, u32[]{:S(2)}, u32[]{:S(2)}) collective-permute-start(bf16[512,128]{1,0:T(8,128)(2,1)S(1)} %get-tuple-element.28), channel_id=1, source_target_pairs={{0,48},{16,0},{32,16},{48,32},{1,49},{17,1},{33,17},{49,33},{2,50}... | collective-permute-start | bytes 393224 | tf_op jit(solution)/shard_map/ppermute | solution.py:289
  57.2 11.5 %all-to-all-start.2 = ((bf16[8,128,128]{2,1,0:T(8,128)(2,1)}), bf16[8,128,128]{2,1,0:T(8,128)(2,1)S(1)}, u32[]{:S(2)}, u32[]{:S(2)}) async-start(bf16[8,128,128]{2,1,0:T(8,128)(2,1)} %get-tuple-element.29), calls=%async_computation.2 | async-start | bytes 524288 | tf_op jit(solution)/shard_map/all_to_all | solution.py:250

commit v8 on v7

--- a/solution.py
+++ b/solution.py
@@ -135,14 +135,15 @@
             out[to : to + some * per, :] = moved[b * some * per : (b + 1) * some * per, :]
 
 
-def middle_kernel(groups, at, got, w2, w3, send, *rest):
+def middle_kernel(groups, got, w2, w3, send, *rest):
     shares, (mixed, d_down, act, d_pre, grads, ready, left) = rest[:X_SIZE], rest[X_SIZE:]
     local, width, hidden = w2.shape
     mine = local // Z_LOW
     tokens = got.shape[2]
     rows = send.shape[1] // 2
     parts = hidden // width
-    base = at[0] * mine
+    base = lax.axis_index("zl") * mine
+    x_index = lax.axis_index("x")
     collect(got, 0, local, mixed)
     collect(got, 1, local, d_down)
     for b in range(mine):
@@ -173,7 +174,7 @@
             grads[b, part, :] = second[:, part]
         grads[mine + b] = dot(act[b], d_down[held, :], NT).astype(BF)
     for k in range(X_SIZE):
-        shares[k][...] = grads[(at[1] + k) % X_SIZE]
+        shares[k][...] = grads[(x_index + k) % X_SIZE]
     for copy in leaving:
         copy.wait()
 
@@ -259,7 +260,6 @@
     mine = local // Z_LOW
     scale = float(all_tokens) ** -0.5
     rows = 2 * local * mine * PAIR
-    place = jnp.stack([lax.axis_index("zl"), lax.axis_index("x")]).astype(jnp.int32)
     entering = (tokens, w_first, upstream, w_fourth)
     (send,) = call(
         functools.partial(enter_kernel, groups),
@@ -275,9 +275,8 @@
     send, *shares = call(
         functools.partial(middle_kernel, groups),
         [shape(Z_LOW * groups, rows, count)] + [shape(hidden, width)] * X_SIZE,
-        place, got, w_second, w_third,
+        got, w_second, w_third,
         flops=12 * count * wide * hidden, transcendentals=count * local * hidden,
-        in_specs=[pl.BlockSpec(memory_space=pltpu.SMEM)] + [pl.BlockSpec()] * 3,
         scratch_shapes=[pltpu.VMEM((mine * width, both), BF)] * 2
         + [pltpu.VMEM((mine, hidden, both), BF)] * 2
         + [pltpu.VMEM((X_SIZE, hidden, width), BF), pltpu.VMEM(got.shape, BF)]

time: 110 us -> 110 us (level)
  blocking collectives: 39.8 us -> 67.1 us
  waiting for transfers between devices: 30.1 us -> 12.4 us
  starting transfers between devices: 29.8 us -> 20.3 us
    all_to_all x1 -> x2, blocking collectives: 16.8 us -> 44 us  [exchange(): return lax.all_to_all(value, axes, split_axis=0, concat_axis=0, tiled=True)]
    all_to_all x3 -> x2, waiting for transfers between devices: 26.5 us -> 8.87 us  [exchange(): return lax.all_to_all(value, axes, split_axis=0, concat_axis=0, tiled=True)]
    all_to_all x3 -> x2, starting transfers between devices: 18.3 us -> 8.79 us  [exchange(): return lax.all_to_all(value, axes, split_axis=0, concat_axis=0, tiled=True)]
  transfers between devices with their start and end apart: 6 -> 5, of which waited for: 5 -> 4; matrix products, arithmetic and copies ran while one was open for 0% -> 0% of each run, Pallas kernels for 1% -> 1%
where the time goes in v8:
time: 110 us; the launch traced here: 109 us
  blocking collectives  67.1 us (61%)
  starting transfers between devices  20.3 us (18%)
  waiting for transfers between devices  12.4 us (11%)
  Pallas kernels  8.8 us (8%)
    all_to_all x2, blocking collectives, exchange(): return lax.all_to_all(value, axes, split_axis=0, concat_axis=0, tiled=True)  44 us
    all_gather x1, blocking collectives, body(): got = lax.all_gather(total, 'far', axis=0, tiled=False)  23.1 us
    ppermute x3, starting transfers between devices, body(): lax.ppermute(share, 'x', [(i, (i + k) % X_SIZE) for i in range(X_SIZE)])  11.5 us
    all_to_all x2, waiting for transfers between devices, exchange(): return lax.all_to_all(value, axes, split_axis=0, concat_axis=0, tiled=True)  8.87 us
    pallas_call x7, Pallas kernels, call(): pl.pallas_call(kernel, out_shape=outs, compiler_params=pltpu.CompilerPara...  8.8 us
    all_to_all x2, starting transfers between devices, exchange(): return lax.all_to_all(value, axes, split_axis=0, concat_axis=0, tiled=True)  8.79 us
    ppermute x3, waiting for transfers between devices, body(): lax.ppermute(share, 'x', [(i, (i + k) % X_SIZE) for i in range(X_SIZE)])  3.53 us
  transfers between devices with their start and end apart: 5, of which 4 were waited for; matrix products, arithmetic and copies ran while one was open for 0% of the time, Pallas kernels for 1%

profile of v8, /device:TPU:8, one launch (start us, length us, event | category | flops | bytes accessed | tf_op | source)
XLA Modules:
  0.0 109.3 jit_solution(2610743040375229466)
XLA Ops:
  0.6 0.0 copy-start.5
  0.7 2.4 %shard_map.109 = bf16[32,32,256]{2,1,0:T(8,128)(2,1)} custom-call(bf16[256,512]{1,0:T(8,128)(2,1)} %x.1, bf16[4,128,128]{2,1,0:T(8,128)(2,1)} %w1.1, bf16[256,512]{1,0:T(8,128)(2,1)} %dy.1, bf16[4,128,128]{2,1,0:T(8,128)(2,1)} %w4.1), custom_call_target="tpu_custom_call" | custom-call | flops 67108864 | bytes 1310720 | tf_op jit(solution)/shard_map/pallas_call | solution.py:29
  3.1 27.3 %all_to_all.20.got = bf16[32,32,256]{2,1,0:T(8,128)(2,1)S(1)} all-to-all(bf16[32,32,256]{2,1,0:T(8,128)(2,1)} %shard_map.109), channel_id=1, replica_groups=mesh['far'=4,'zl'=2,'x'=4,'hidden'=16] {'zl','hidden'}, dimensions={0} | all-to-all | bytes 1048576 | tf_op jit(solution)/shard_map/all_to_all | solution.py:251
  30.3 0.0 copy-done.4
  30.3 2.6 %shard_map.110 = (bf16[32,32,256]{2,1,0:T(8,128)(2,1)}, bf16[512,128]{1,0:T(8,128)(2,1)S(1)}, bf16[512,128]{1,0:T(8,128)(2,1)S(1)}, bf16[512,128]{1,0:T(8,128)(2,1)S(1)}, bf16[512,128]{1,0:T(8,128)(2,1)S(1)}) custom-call(bf16[32,32,256]{2,1,0:T(8,128)(2,1)S(1)} %all_to_all.20.got, bf16[4,128,512]{2,1,0:T(8,128)(2,1)S(1)} %copy-done.4, ...), custom_call_target="tpu_custom_call" | custom-call | flops 805306368 | bytes 2621440 | tf_op jit(solution)/shard_map/pallas_call | solution.py:29
  33.0 4.5 %all-to-all-start.1 = ((bf16[32,32,256]{2,1,0:T(8,128)(2,1)}), bf16[32,32,256]{2,1,0:T(8,128)(2,1)S(1)}, u32[]{:S(2)}, u32[]{:S(2)}) async-start(bf16[32,32,256]{2,1,0:T(8,128)(2,1)} %get-tuple-element.24), calls=%async_computation.1 | async-start | bytes 1048576 | tf_op jit(solution)/shard_map/all_to_all | solution.py:251
  37.5 0.0 copy-start.2
  37.5 0.0 copy-start.3
  37.5 3.5 %collective-permute-start = (bf16[512,128]{1,0:T(8,128)(2,1)S(1)}, bf16[512,128]{1,0:T(8,128)(2,1)S(1)}, u32[]{:S(2)}, u32[]{:S(2)}) collective-permute-start(bf16[512,128]{1,0:T(8,128)(2,1)S(1)} %get-tuple-element.26), channel_id=1, source_target_pairs={{0,16},{16,32},{32,48},{48,0},{1,17},{17,33},{33,49},{49,1},{2,18}... | collective-permute-start | bytes 393224 | tf_op jit(solution)/shard_map/ppermute | solution.py:288
  41.0 4.6 %collective-permute-start.1 = (bf16[512,128]{1,0:T(8,128)(2,1)S(1)}, bf16[512,128]{1,0:T(8,128)(2,1)S(1)}, u32[]{:S(2)}, u32[]{:S(2)}) collective-permute-start(bf16[512,128]{1,0:T(8,128)(2,1)S(1)} %get-tuple-element.27), channel_id=1, source_target_pairs={{0,32},{16,48},{32,0},{48,16},{1,33},{17,49},{33,1},{49,17},{2,34}... | collective-permute-start | bytes 393224 | tf_op jit(solution)/shard_map/ppermute | solution.py:288
  45.7 3.3 %collective-permute-start.2 = (bf16[512,128]{1,0:T(8,128)(2,1)S(1)}, bf16[512,128]{1,0:T(8,128)(2,1)S(1)}, u32[]{:S(2)}, u32[]{:S(2)}) collective-permute-start(bf16[512,128]{1,0:T(8,128)(2,1)S(1)} %get-tuple-element.28), channel_id=1, source_target_pairs={{0,48},{16,0},{32,16},{48,32},{1,49},{17,1},{33,17},{49,33},{2,50}... | collective-permute-start | bytes 393224 | tf_op jit(solution)/shard_map/ppermute | solution.py:288
  49.0 0.0 collective-permute-done.rest_1_
  49.0 1.0 collective-permute-done.1.rest_2_
  50.1 2.5 %collective-permute-done.2.rest_3_ = bf16[512,128]{1,0:T(8,128)(2,1)S(1)} collective-permute-done((bf16[512,128]{1,0:T(8,128)(2,1)S(1)}, bf16[512,128]{1,0:T(8,128)(2,1)S(1)}, u32[]{:S(2)}, u32[]{:S(2)}) %collective-permute-start.2) | collective-permute-done | bytes 131104 | tf_op jit(solution)/shard_map/ppermute | solution.py:288
  52.5 2.8 %all-to-all-done.1.got = bf16[32,32,256]{2,1,0:T(8,128)(2,1)S(1)} async-done(((bf16[32,32,256]{2,1,0:T(8,128)(2,1)}), bf16[32,32,256]{2,1,0:T(8,128)(2,1)S(1)}, u32[]{:S(2)}, u32[]{:S(2)}) %all-to-all-start.1) | async-done | bytes 524320 | tf_op jit(solution)/shard_map/all_to_all | solution.py:251
  55.3 0.0 copy-done.1
  55.3 1.4 %shard_map.111 = (bf16[512,256]{1,0:T(8,128)(2,1)S(1)}, bf16[512,256]{1,0:T(8,128)(2,1)S(1)}, bf16[8,128,128]{2,1,0:T(8,128)(2,1)}, bf16[512,128]{1,0:T(8,128)(2,1)S(1)}) custom-call(bf16[32,32,256]{2,1,0:T(8,128)(2,1)S(1)} %all-to-all-done.1.got, bf16[256,512]{1,0:T(8,128)(2,1)S(1)} %copy-done, bf16[256,512]{1,0:T(8,128)(2,1)S(1)} %copy-done.1, ...), custom_call_target="tpu_custom_call" | custom-call | flops 134217728 | bytes 2490368 | tf_op jit(solution)/shard_map/pallas_call | solution.py:29
  56.7 4.3 %all-to-all-start.2 = ((bf16[8,128,128]{2,1,0:T(8,128)(2,1)}), bf16[8,128,128]{2,1,0:T(8,128)(2,1)S(1)}, u32[]{:S(2)}, u32[]{:S(2)}) async-start(bf16[8,128,128]{2,1,0:T(8,128)(2,1)} %get-tuple-element.29), calls=%async_computation.2 | async-start | bytes 524288 | tf_op jit(solution)/shard_map/all_to_all | solution.py:251
  61.0 1.1 %shard_map.112 = (bf16[256,512]{1,0:T(8,128)(2,1)}, bf16[256,512]{1,0:T(8,128)(2,1)}) custom-call(bf16[512,256]{1,0:T(8,128)(2,1)S(1)} %get-tuple-element.30.back, bf16[512,256]{1,0:T(8,128)(2,1)S(1)} %get-tuple-element.31.d_first, bf16[4,128,128]{2,1,0:T(8,128)(2,1)S(1)} %copy-done.2, bf16[4,128,128]{2,1,0:T(8,128)(2,1)S(1)} %copy-done.3), custom_call_target="tpu_custom_call" | custom-call | flops 67108864 | bytes 1310720 | tf_op jit(solution)/shard_map/pallas_call | solution.py:29
  62.1 6.1 %all-to-all-done.2.got = bf16[8,128,128]{2,1,0:T(8,128)(2,1)S(1)} async-done(((bf16[8,128,128]{2,1,0:T(8,128)(2,1)}), bf16[8,128,128]{2,1,0:T(8,128)(2,1)S(1)}, u32[]{:S(2)}, u32[]{:S(2)}) %all-to-all-start.2) | async-done | bytes 262176 | tf_op jit(solution)/shard_map/all_to_all | solution.py:251
  68.3 23.1 %all-gather = bf16[2560,128]{1,0:T(8,128)(2,1)S(1)} all-gather(bf16[640,128]{1,0:T(8,128)(2,1)S(1)} %shard_map.113), channel_id=2, replica_groups=mesh['far'=4,'zl'=2,'x'=4,'hidden'=16] {'far'}, dimensions={0}, use_global_device_ids=true | all-gather | bytes 819200 | tf_op jit(solution)/shard_map/all_gather | solution.py:316
  91.3 0.1 shard_map.114
  91.4 16.7 %all_to_all.21.got = bf16[8,640,128]{2,1,0:T(8,128)(2,1)S(1)} all-to-all(bf16[8,640,128]{2,1,0:T(8,128)(2,1)S(1)} %shard_map.114), channel_id=1, replica_groups=mesh['far'=4,'zl'=2,'x'=4,'hidden'=16] {'zl','x'}, dimensions={0} | all-to-all | bytes 2621440 | tf_op jit(solution)/shard_map/all_to_all | solution.py:251
  108.1 1.2 %shard_map.115 = (bf16[4,128,128]{2,1,0:T(8,128)(2,1)}, bf16[4,128,512]{2,1,0:T(8,128)(2,1)}, bf16[4,512,128]{2,1,0:T(8,128)(2,1)}, bf16[4,128,128]{2,1,0:T(8,128)(2,1)}) custom-call(bf16[8,640,128]{2,1,0:T(8,128)(2,1)S(1)} %all_to_all.21.got), custom_call_target="tpu_custom_call" | custom-call | bytes 2621440 | tf_op jit(solution)/shard_map/pallas_call | solution.py:29
  (8 shorter events, 0.1 us)
Async XLA Ops:
  0.6 29.7 %copy-start.5 = (bf16[4,512,128]{2,1,0:T(8,128)(2,1)S(1)}, bf16[4,512,128]{2,1,0:T(8,128)(2,1)}, u32[]{:S(2)}) copy-start(bf16[4,512,128]{2,1,0:T(8,128)(2,1)} %w3.1) | copy-start | bytes 1572868
  0.6 29.7 %copy-start.4 = (bf16[4,128,512]{2,1,0:T(8,128)(2,1)S(1)}, bf16[4,128,512]{2,1,0:T(8,128)(2,1)}, u32[]{:S(2)}) copy-start(bf16[4,128,512]{2,1,0:T(8,128)(2,1)} %w2.1) | copy-start | bytes 1572868
  30.3 25.0 %copy-start = (bf16[256,512]{1,0:T(8,128)(2,1)S(1)}, bf16[256,512]{1,0:T(8,128)(2,1)}, u32[]{:S(2)}) copy-start(bf16[256,512]{1,0:T(8,128)(2,1)} %x.1) | copy-start | bytes 786436
  30.3 25.0 %copy-start.1 = (bf16[256,512]{1,0:T(8,128)(2,1)S(1)}, bf16[256,512]{1,0:T(8,128)(2,1)}, u32[]{:S(2)}) copy-start(bf16[256,512]{1,0:T(8,128)(2,1)} %dy.1) | copy-start | bytes 786436
  33.0 22.4 %all-to-all-start.1 = ((bf16[32,32,256]{2,1,0:T(8,128)(2,1)}), bf16[32,32,256]{2,1,0:T(8,128)(2,1)S(1)}, u32[]{:S(2)}, u32[]{:S(2)}) async-start(bf16[32,32,256]{2,1,0:T(8,128)(2,1)} %get-tuple-element.24), calls=%async_computation.1 | async-start | bytes 1048576 | tf_op jit(solution)/shard_map/all_to_all | solution.py:251
  37.5 23.5 %copy-start.2 = (bf16[4,128,128]{2,1,0:T(8,128)(2,1)S(1)}, bf16[4,128,128]{2,1,0:T(8,128)(2,1)}, u32[]{:S(2)}) copy-start(bf16[4,128,128]{2,1,0:T(8,128)(2,1)} %w1.1) | copy-start | bytes 393220
  37.5 23.5 %copy-start.3 = (bf16[4,128,128]{2,1,0:T(8,128)(2,1)S(1)}, bf16[4,128,128]{2,1,0:T(8,128)(2,1)}, u32[]{:S(2)}) copy-start(bf16[4,128,128]{2,1,0:T(8,128)(2,1)} %w4.1) | copy-start | bytes 393220
  37.5 11.5 %collective-permute-start = (bf16[512,128]{1,0:T(8,128)(2,1)S(1)}, bf16[512,128]{1,0:T(8,128)(2,1)S(1)}, u32[]{:S(2)}, u32[]{:S(2)}) collective-permute-start(bf16[512,128]{1,0:T(8,128)(2,1)S(1)} %get-tuple-element.26), channel_id=1, source_target_pairs={{0,16},{16,32},{32,48},{48,0},{1,17},{17,33},{33,49},{49,1},{2,18}... | collective-permute-start | bytes 393224 | tf_op jit(solution)/shard_map/ppermute | solution.py:288
  41.0 9.0 %collective-permute-start.1 = (bf16[512,128]{1,0:T(8,128)(2,1)S(1)}, bf16[512,128]{1,0:T(8,128)(2,1)S(1)}, u32[]{:S(2)}, u32[]{:S(2)}) collective-permute-start(bf16[512,128]{1,0:T(8,128)(2,1)S(1)} %get-tuple-element.27), channel_id=1, source_target_pairs={{0,32},{16,48},{32,0},{48,16},{1,33},{17,49},{33,1},{49,17},{2,34}... | collective-permute-start | bytes 393224 | tf_op jit(solution)/shard_map/ppermute | solution.py:288
  45.7 6.9 %collective-permute-start.2 = (bf16[512,128]{1,0:T(8,128)(2,1)S(1)}, bf16[512,128]{1,0:T(8,128)(2,1)S(1)}, u32[]{:S(2)}, u32[]{:S(2)}) collective-permute-start(bf16[512,128]{1,0:T(8,128)(2,1)S(1)} %get-tuple-element.28), channel_id=1, source_target_pairs={{0,48},{16,0},{32,16},{48,32},{1,49},{17,1},{33,17},{49,33},{2,50}... | collective-permute-start | bytes 393224 | tf_op jit(solution)/shard_map/ppermute | solution.py:288
  56.7 11.5 %all-to-all-start.2 = ((bf16[8,128,128]{2,1,0:T(8,128)(2,1)}), bf16[8,128,128]{2,1,0:T(8,128)(2,1)S(1)}, u32[]{:S(2)}, u32[]{:S(2)}) async-start(bf16[8,128,128]{2,1,0:T(8,128)(2,1)} %get-tuple-element.29), calls=%async_computation.2 | async-start | bytes 524288 | tf_op jit(solution)/shard_map/all_to_all | solution.py:251

commit v9 on v8

--- a/solution.py
+++ b/solution.py
@@ -48,7 +48,7 @@
     return jnp.concatenate([low.reshape(split), high.reshape(split)], axis=1)
 
 
-def enter_kernel(groups, x_in, w1_in, dy_in, w4_in, send, x, w1, dy, w4, arrived):
+def enter_kernel(groups, x_in, w1_in, dy_in, w4_in, out, x, w1, dy, w4, send, arrived, left):
     copies = [
         pltpu.make_async_copy(source, target, arrived.at[k])
         for k, (source, target) in enumerate(((x_in, x), (w1_in, w1), (dy_in, dy), (w4_in, w4)))
@@ -59,6 +59,7 @@
     tokens = x.shape[0]
     per = width // groups
     rows = local * per // Z_LOW
+    leaving = []
     first_half = lax.broadcasted_iota(jnp.int32, (groups, per, tokens), 1) < per // 2
     for k in range(2):
         copies[2 * k].wait()
@@ -79,6 +80,12 @@
         for zl in range(Z_LOW):
             filled = jnp.concatenate(to_zl[zl], axis=1).astype(BF)
             send[zl * groups : (zl + 1) * groups, k * rows : (k + 1) * rows, :] = filled
+        part = pl.ds(k * rows, rows)
+        copy = pltpu.make_async_copy(send.at[:, part, :], out.at[:, part, :], left.at[k])
+        copy.start()
+        leaving.append(copy)
+    for copy in leaving:
+        copy.wait()
 
 
 def one_hot(source):
@@ -267,8 +274,10 @@
         *entering,
         flops=4 * count * wide * width, vmem=60 << 20,
         in_specs=[pl.BlockSpec(memory_space=pltpu.HBM)] * 4,
+        out_specs=[pl.BlockSpec(memory_space=pl.ANY)],
         scratch_shapes=[pltpu.VMEM(a.shape, BF) for a in entering]
-        + [pltpu.SemaphoreType.DMA((4,))],
+        + [pltpu.VMEM((Z_LOW * groups, rows, count), BF)]
+        + [pltpu.SemaphoreType.DMA((4,)), pltpu.SemaphoreType.DMA((2,))],
     )
     got = exchange(send, middle)
     both = Z_LOW * count

time: 110 us -> 110 us (level)
  no operation moved by 1% of the time
where the time goes in v9:
time: 110 us; the launch traced here: 109 us
  blocking collectives  67.1 us (61%)
  starting transfers between devices  20.3 us (18%)
  waiting for transfers between devices  12.4 us (11%)
  Pallas kernels  8.73 us (8%)
    all_to_all x2, blocking collectives, exchange(): return lax.all_to_all(value, axes, split_axis=0, concat_axis=0, tiled=True)  44 us
    all_gather x1, blocking collectives, body(): got = lax.all_gather(total, 'far', axis=0, tiled=False)  23.1 us
    ppermute x3, starting transfers between devices, body(): lax.ppermute(share, 'x', [(i, (i + k) % X_SIZE) for i in range(X_SIZE)])  11.5 us
    all_to_all x2, waiting for transfers between devices, exchange(): return lax.all_to_all(value, axes, split_axis=0, concat_axis=0, tiled=True)  8.88 us
    all_to_all x2, starting transfers between devices, exchange(): return lax.all_to_all(value, axes, split_axis=0, concat_axis=0, tiled=True)  8.79 us
    pallas_call x7, Pallas kernels, call(): pl.pallas_call(kernel, out_shape=outs, compiler_params=pltpu.CompilerPara...  8.73 us
    ppermute x3, waiting for transfers between devices, body(): lax.ppermute(share, 'x', [(i, (i + k) % X_SIZE) for i in range(X_SIZE)])  3.52 us
  transfers between devices with their start and end apart: 5, of which 4 were waited for; matrix products, arithmetic and copies ran while one was open for 0% of the time, Pallas kernels for 1%

profile of v9, /device:TPU:8, one launch (start us, length us, event | category | flops | bytes accessed | tf_op | source)
XLA Modules:
  0.0 109.3 jit_solution(3708698560335128172)
XLA Ops:
  0.6 0.0 copy-start.5
  0.7 2.3 %shard_map.109 = bf16[32,32,256]{2,1,0:T(8,128)(2,1)} custom-call(bf16[256,512]{1,0:T(8,128)(2,1)} %x.1, bf16[4,128,128]{2,1,0:T(8,128)(2,1)} %w1.1, bf16[256,512]{1,0:T(8,128)(2,1)} %dy.1, bf16[4,128,128]{2,1,0:T(8,128)(2,1)} %w4.1), custom_call_target="tpu_custom_call" | custom-call | flops 67108864 | bytes 1310720 | tf_op jit(solution)/shard_map/pallas_call | solution.py:29
  3.0 27.3 %all_to_all.20.got = bf16[32,32,256]{2,1,0:T(8,128)(2,1)S(1)} all-to-all(bf16[32,32,256]{2,1,0:T(8,128)(2,1)} %shard_map.109), channel_id=1, replica_groups=mesh['far'=4,'zl'=2,'x'=4,'hidden'=16] {'zl','hidden'}, dimensions={0} | all-to-all | bytes 1048576 | tf_op jit(solution)/shard_map/all_to_all | solution.py:258
  30.3 2.6 %shard_map.110 = (bf16[32,32,256]{2,1,0:T(8,128)(2,1)}, bf16[512,128]{1,0:T(8,128)(2,1)S(1)}, bf16[512,128]{1,0:T(8,128)(2,1)S(1)}, bf16[512,128]{1,0:T(8,128)(2,1)S(1)}, bf16[512,128]{1,0:T(8,128)(2,1)S(1)}) custom-call(bf16[32,32,256]{2,1,0:T(8,128)(2,1)S(1)} %all_to_all.20.got, bf16[4,128,512]{2,1,0:T(8,128)(2,1)S(1)} %copy-done.4, ...), custom_call_target="tpu_custom_call" | custom-call | flops 805306368 | bytes 2621440 | tf_op jit(solution)/shard_map/pallas_call | solution.py:29
  32.9 4.5 %all-to-all-start.1 = ((bf16[32,32,256]{2,1,0:T(8,128)(2,1)}), bf16[32,32,256]{2,1,0:T(8,128)(2,1)S(1)}, u32[]{:S(2)}, u32[]{:S(2)}) async-start(bf16[32,32,256]{2,1,0:T(8,128)(2,1)} %get-tuple-element.24), calls=%async_computation.1 | async-start | bytes 1048576 | tf_op jit(solution)/shard_map/all_to_all | solution.py:258
  37.4 0.0 copy-start.2
  37.4 0.0 copy-start.3
  37.4 3.5 %collective-permute-start = (bf16[512,128]{1,0:T(8,128)(2,1)S(1)}, bf16[512,128]{1,0:T(8,128)(2,1)S(1)}, u32[]{:S(2)}, u32[]{:S(2)}) collective-permute-start(bf16[512,128]{1,0:T(8,128)(2,1)S(1)} %get-tuple-element.26), channel_id=1, source_target_pairs={{0,16},{16,32},{32,48},{48,0},{1,17},{17,33},{33,49},{49,1},{2,18}... | collective-permute-start | bytes 393224 | tf_op jit(solution)/shard_map/ppermute | solution.py:297
  40.9 4.6 %collective-permute-start.1 = (bf16[512,128]{1,0:T(8,128)(2,1)S(1)}, bf16[512,128]{1,0:T(8,128)(2,1)S(1)}, u32[]{:S(2)}, u32[]{:S(2)}) collective-permute-start(bf16[512,128]{1,0:T(8,128)(2,1)S(1)} %get-tuple-element.27), channel_id=1, source_target_pairs={{0,32},{16,48},{32,0},{48,16},{1,33},{17,49},{33,1},{49,17},{2,34}... | collective-permute-start | bytes 393224 | tf_op jit(solution)/shard_map/ppermute | solution.py:297
  45.6 3.4 %collective-permute-start.2 = (bf16[512,128]{1,0:T(8,128)(2,1)S(1)}, bf16[512,128]{1,0:T(8,128)(2,1)S(1)}, u32[]{:S(2)}, u32[]{:S(2)}) collective-permute-start(bf16[512,128]{1,0:T(8,128)(2,1)S(1)} %get-tuple-element.28), channel_id=1, source_target_pairs={{0,48},{16,0},{32,16},{48,32},{1,49},{17,1},{33,17},{49,33},{2,50}... | collective-permute-start | bytes 393224 | tf_op jit(solution)/shard_map/ppermute | solution.py:297
  48.9 0.0 collective-permute-done.rest_1_
  48.9 1.0 collective-permute-done.1.rest_2_
  50.0 2.5 %collective-permute-done.2.rest_3_ = bf16[512,128]{1,0:T(8,128)(2,1)S(1)} collective-permute-done((bf16[512,128]{1,0:T(8,128)(2,1)S(1)}, bf16[512,128]{1,0:T(8,128)(2,1)S(1)}, u32[]{:S(2)}, u32[]{:S(2)}) %collective-permute-start.2) | collective-permute-done | bytes 131104 | tf_op jit(solution)/shard_map/ppermute | solution.py:297
  52.5 2.8 %all-to-all-done.1.got = bf16[32,32,256]{2,1,0:T(8,128)(2,1)S(1)} async-done(((bf16[32,32,256]{2,1,0:T(8,128)(2,1)}), bf16[32,32,256]{2,1,0:T(8,128)(2,1)S(1)}, u32[]{:S(2)}, u32[]{:S(2)}) %all-to-all-start.1) | async-done | bytes 524320 | tf_op jit(solution)/shard_map/all_to_all | solution.py:258
  55.3 1.4 %shard_map.111 = (bf16[512,256]{1,0:T(8,128)(2,1)S(1)}, bf16[512,256]{1,0:T(8,128)(2,1)S(1)}, bf16[8,128,128]{2,1,0:T(8,128)(2,1)}, bf16[512,128]{1,0:T(8,128)(2,1)S(1)}) custom-call(bf16[32,32,256]{2,1,0:T(8,128)(2,1)S(1)} %all-to-all-done.1.got, bf16[256,512]{1,0:T(8,128)(2,1)S(1)} %copy-done, bf16[256,512]{1,0:T(8,128)(2,1)S(1)} %copy-done.1, ...), custom_call_target="tpu_custom_call" | custom-call | flops 134217728 | bytes 2490368 | tf_op jit(solution)/shard_map/pallas_call | solution.py:29
  56.6 4.3 %all-to-all-start.2 = ((bf16[8,128,128]{2,1,0:T(8,128)(2,1)}), bf16[8,128,128]{2,1,0:T(8,128)(2,1)S(1)}, u32[]{:S(2)}, u32[]{:S(2)}) async-start(bf16[8,128,128]{2,1,0:T(8,128)(2,1)} %get-tuple-element.29), calls=%async_computation.2 | async-start | bytes 524288 | tf_op jit(solution)/shard_map/all_to_all | solution.py:258
  60.9 0.0 copy-done.2
  60.9 0.0 copy-done.3
  60.9 1.1 %shard_map.112 = (bf16[256,512]{1,0:T(8,128)(2,1)}, bf16[256,512]{1,0:T(8,128)(2,1)}) custom-call(bf16[512,256]{1,0:T(8,128)(2,1)S(1)} %get-tuple-element.30.back, bf16[512,256]{1,0:T(8,128)(2,1)S(1)} %get-tuple-element.31.d_first, bf16[4,128,128]{2,1,0:T(8,128)(2,1)S(1)} %copy-done.2, bf16[4,128,128]{2,1,0:T(8,128)(2,1)S(1)} %copy-done.3), custom_call_target="tpu_custom_call" | custom-call | flops 67108864 | bytes 1310720 | tf_op jit(solution)/shard_map/pallas_call | solution.py:29
  62.0 6.1 %all-to-all-done.2.got = bf16[8,128,128]{2,1,0:T(8,128)(2,1)S(1)} async-done(((bf16[8,128,128]{2,1,0:T(8,128)(2,1)}), bf16[8,128,128]{2,1,0:T(8,128)(2,1)S(1)}, u32[]{:S(2)}, u32[]{:S(2)}) %all-to-all-start.2) | async-done | bytes 262176 | tf_op jit(solution)/shard_map/all_to_all | solution.py:258
  68.2 23.1 %all-gather = bf16[2560,128]{1,0:T(8,128)(2,1)S(1)} all-gather(bf16[640,128]{1,0:T(8,128)(2,1)S(1)} %shard_map.113), channel_id=2, replica_groups=mesh['far'=4,'zl'=2,'x'=4,'hidden'=16] {'far'}, dimensions={0}, use_global_device_ids=true | all-gather | bytes 819200 | tf_op jit(solution)/shard_map/all_gather | solution.py:325
  91.3 0.1 shard_map.114
  91.4 16.7 %all_to_all.21.got = bf16[8,640,128]{2,1,0:T(8,128)(2,1)S(1)} all-to-all(bf16[8,640,128]{2,1,0:T(8,128)(2,1)S(1)} %shard_map.114), channel_id=1, replica_groups=mesh['far'=4,'zl'=2,'x'=4,'hidden'=16] {'zl','x'}, dimensions={0} | all-to-all | bytes 2621440 | tf_op jit(solution)/shard_map/all_to_all | solution.py:258
  108.1 1.2 %shard_map.115 = (bf16[4,128,128]{2,1,0:T(8,128)(2,1)}, bf16[4,128,512]{2,1,0:T(8,128)(2,1)}, bf16[4,512,128]{2,1,0:T(8,128)(2,1)}, bf16[4,128,128]{2,1,0:T(8,128)(2,1)}) custom-call(bf16[8,640,128]{2,1,0:T(8,128)(2,1)S(1)} %all_to_all.21.got), custom_call_target="tpu_custom_call" | custom-call | bytes 2621440 | tf_op jit(solution)/shard_map/pallas_call | solution.py:29
  (8 shorter events, 0.1 us)
Async XLA Ops:
  0.6 29.6 %copy-start.5 = (bf16[4,512,128]{2,1,0:T(8,128)(2,1)S(1)}, bf16[4,512,128]{2,1,0:T(8,128)(2,1)}, u32[]{:S(2)}) copy-start(bf16[4,512,128]{2,1,0:T(8,128)(2,1)} %w3.1) | copy-start | bytes 1572868
  0.6 29.6 %copy-start.4 = (bf16[4,128,512]{2,1,0:T(8,128)(2,1)S(1)}, bf16[4,128,512]{2,1,0:T(8,128)(2,1)}, u32[]{:S(2)}) copy-start(bf16[4,128,512]{2,1,0:T(8,128)(2,1)} %w2.1) | copy-start | bytes 1572868
  30.3 25.0 %copy-start = (bf16[256,512]{1,0:T(8,128)(2,1)S(1)}, bf16[256,512]{1,0:T(8,128)(2,1)}, u32[]{:S(2)}) copy-start(bf16[256,512]{1,0:T(8,128)(2,1)} %x.1) | copy-start | bytes 786436
  30.3 25.0 %copy-start.1 = (bf16[256,512]{1,0:T(8,128)(2,1)S(1)}, bf16[256,512]{1,0:T(8,128)(2,1)}, u32[]{:S(2)}) copy-start(bf16[256,512]{1,0:T(8,128)(2,1)} %dy.1) | copy-start | bytes 786436
  32.9 22.4 %all-to-all-start.1 = ((bf16[32,32,256]{2,1,0:T(8,128)(2,1)}), bf16[32,32,256]{2,1,0:T(8,128)(2,1)S(1)}, u32[]{:S(2)}, u32[]{:S(2)}) async-start(bf16[32,32,256]{2,1,0:T(8,128)(2,1)} %get-tuple-element.24), calls=%async_computation.1 | async-start | bytes 1048576 | tf_op jit(solution)/shard_map/all_to_all | solution.py:258
  37.4 23.5 %copy-start.2 = (bf16[4,128,128]{2,1,0:T(8,128)(2,1)S(1)}, bf16[4,128,128]{2,1,0:T(8,128)(2,1)}, u32[]{:S(2)}) copy-start(bf16[4,128,128]{2,1,0:T(8,128)(2,1)} %w1.1) | copy-start | bytes 393220
  37.4 23.5 %copy-start.3 = (bf16[4,128,128]{2,1,0:T(8,128)(2,1)S(1)}, bf16[4,128,128]{2,1,0:T(8,128)(2,1)}, u32[]{:S(2)}) copy-start(bf16[4,128,128]{2,1,0:T(8,128)(2,1)} %w4.1) | copy-start | bytes 393220
  37.4 11.5 %collective-permute-start = (bf16[512,128]{1,0:T(8,128)(2,1)S(1)}, bf16[512,128]{1,0:T(8,128)(2,1)S(1)}, u32[]{:S(2)}, u32[]{:S(2)}) collective-permute-start(bf16[512,128]{1,0:T(8,128)(2,1)S(1)} %get-tuple-element.26), channel_id=1, source_target_pairs={{0,16},{16,32},{32,48},{48,0},{1,17},{17,33},{33,49},{49,1},{2,18}... | collective-permute-start | bytes 393224 | tf_op jit(solution)/shard_map/ppermute | solution.py:297
  40.9 9.0 %collective-permute-start.1 = (bf16[512,128]{1,0:T(8,128)(2,1)S(1)}, bf16[512,128]{1,0:T(8,128)(2,1)S(1)}, u32[]{:S(2)}, u32[]{:S(2)}) collective-permute-start(bf16[512,128]{1,0:T(8,128)(2,1)S(1)} %get-tuple-element.27), channel_id=1, source_target_pairs={{0,32},{16,48},{32,0},{48,16},{1,33},{17,49},{33,1},{49,17},{2,34}... | collective-permute-start | bytes 393224 | tf_op jit(solution)/shard_map/ppermute | solution.py:297
  45.6 6.9 %collective-permute-start.2 = (bf16[512,128]{1,0:T(8,128)(2,1)S(1)}, bf16[512,128]{1,0:T(8,128)(2,1)S(1)}, u32[]{:S(2)}, u32[]{:S(2)}) collective-permute-start(bf16[512,128]{1,0:T(8,128)(2,1)S(1)} %get-tuple-element.28), channel_id=1, source_target_pairs={{0,48},{16,0},{32,16},{48,32},{1,49},{17,1},{33,17},{49,33},{2,50}... | collective-permute-start | bytes 393224 | tf_op jit(solution)/shard_map/ppermute | solution.py:297
  56.6 11.5 %all-to-all-start.2 = ((bf16[8,128,128]{2,1,0:T(8,128)(2,1)}), bf16[8,128,128]{2,1,0:T(8,128)(2,1)S(1)}, u32[]{:S(2)}, u32[]{:S(2)}) async-start(bf16[8,128,128]{2,1,0:T(8,128)(2,1)} %get-tuple-element.29), calls=%async_computation.2 | async-start | bytes 524288 | tf_op jit(solution)/shard_map/all_to_all | solution.py:258

commit v10 on v9

--- a/solution.py
+++ b/solution.py
@@ -293,9 +293,9 @@
         out_specs=[pl.BlockSpec(memory_space=pl.ANY)] + [pl.BlockSpec()] * X_SIZE,
     )
     got = exchange(send, middle)
-    shares = [
-        share if k == 0 else lax.ppermute(share, "x", [(i, (i + k) % X_SIZE) for i in range(X_SIZE)])
-        for k, share in enumerate(shares)
+    shares = shares[:1] + [
+        lax.ppermute(shares[k], "x", [(i, (i + k) % X_SIZE) for i in range(X_SIZE)])
+        for k in (2, 1, 3)
     ]
     back, d_first, grads, wide_sum = call(
         leave_kernel,

time: 110 us -> 110 us (level)
  no operation moved by 1% of the time
where the time goes in v10:
time: 110 us; the launch traced here: 109 us
  blocking collectives  67.1 us (61%)
  starting transfers between devices  20.9 us (19%)
  waiting for transfers between devices  11.8 us (11%)
  Pallas kernels  8.73 us (8%)
    all_to_all x2, blocking collectives, exchange(): return lax.all_to_all(value, axes, split_axis=0, concat_axis=0, tiled=True)  44 us
    all_gather x1, blocking collectives, body(): got = lax.all_gather(total, 'far', axis=0, tiled=False)  23.1 us
    ppermute x3, starting transfers between devices, body(): lax.ppermute(shares[k], 'x', [(i, (i + k) % X_SIZE) for i in range(X_SIZE)])  12.1 us
    all_to_all x2, waiting for transfers between devices, exchange(): return lax.all_to_all(value, axes, split_axis=0, concat_axis=0, tiled=True)  9.3 us
    all_to_all x2, starting transfers between devices, exchange(): return lax.all_to_all(value, axes, split_axis=0, concat_axis=0, tiled=True)  8.79 us
    pallas_call x7, Pallas kernels, call(): pl.pallas_call(kernel, out_shape=outs, compiler_params=pltpu.CompilerPara...  8.73 us
    ppermute x3, waiting for transfers between devices, body(): lax.ppermute(shares[k], 'x', [(i, (i + k) % X_SIZE) for i in range(X_SIZE)])  2.49 us
  transfers between devices with their start and end apart: 5, of which 4 were waited for; matrix products, arithmetic and copies ran while one was open for 0% of the time, Pallas kernels for 1%

profile of v10, /device:TPU:8, one launch (start us, length us, event | category | flops | bytes accessed | tf_op | source)
XLA Modules:
  0.0 109.3 jit_solution(12972927633957670497)
XLA Ops:
  0.6 0.0 copy-start.5
  0.7 2.3 %shard_map.109 = bf16[32,32,256]{2,1,0:T(8,128)(2,1)} custom-call(bf16[256,512]{1,0:T(8,128)(2,1)} %x.1, bf16[4,128,128]{2,1,0:T(8,128)(2,1)} %w1.1, bf16[256,512]{1,0:T(8,128)(2,1)} %dy.1, bf16[4,128,128]{2,1,0:T(8,128)(2,1)} %w4.1), custom_call_target="tpu_custom_call" | custom-call | flops 67108864 | bytes 1310720 | tf_op jit(solution)/shard_map/pallas_call | solution.py:29
  3.0 27.3 %all_to_all.20.got = bf16[32,32,256]{2,1,0:T(8,128)(2,1)S(1)} all-to-all(bf16[32,32,256]{2,1,0:T(8,128)(2,1)} %shard_map.109), channel_id=1, replica_groups=mesh['far'=4,'zl'=2,'x'=4,'hidden'=16] {'zl','hidden'}, dimensions={0} | all-to-all | bytes 1048576 | tf_op jit(solution)/shard_map/all_to_all | solution.py:258
  30.3 2.6 %shard_map.110 = (bf16[32,32,256]{2,1,0:T(8,128)(2,1)}, bf16[512,128]{1,0:T(8,128)(2,1)S(1)}, bf16[512,128]{1,0:T(8,128)(2,1)S(1)}, bf16[512,128]{1,0:T(8,128)(2,1)S(1)}, bf16[512,128]{1,0:T(8,128)(2,1)S(1)}) custom-call(bf16[32,32,256]{2,1,0:T(8,128)(2,1)S(1)} %all_to_all.20.got, bf16[4,128,512]{2,1,0:T(8,128)(2,1)S(1)} %copy-done.4, ...), custom_call_target="tpu_custom_call" | custom-call | flops 805306368 | bytes 2621440 | tf_op jit(solution)/shard_map/pallas_call | solution.py:29
  32.9 4.5 %all-to-all-start.1 = ((bf16[32,32,256]{2,1,0:T(8,128)(2,1)}), bf16[32,32,256]{2,1,0:T(8,128)(2,1)S(1)}, u32[]{:S(2)}, u32[]{:S(2)}) async-start(bf16[32,32,256]{2,1,0:T(8,128)(2,1)} %get-tuple-element.24), calls=%async_computation.1 | async-start | bytes 1048576 | tf_op jit(solution)/shard_map/all_to_all | solution.py:258
  37.4 0.0 copy-start.2
  37.4 0.0 copy-start.3
  37.4 5.1 %collective-permute-start = (bf16[512,128]{1,0:T(8,128)(2,1)S(1)}, bf16[512,128]{1,0:T(8,128)(2,1)S(1)}, u32[]{:S(2)}, u32[]{:S(2)}) collective-permute-start(bf16[512,128]{1,0:T(8,128)(2,1)S(1)} %get-tuple-element.26), channel_id=1, source_target_pairs={{0,32},{16,48},{32,0},{48,16},{1,33},{17,49},{33,1},{49,17},{2,34}... | collective-permute-start | bytes 393224 | tf_op jit(solution)/shard_map/ppermute | solution.py:297
  42.5 2.5 %collective-permute-start.1 = (bf16[512,128]{1,0:T(8,128)(2,1)S(1)}, bf16[512,128]{1,0:T(8,128)(2,1)S(1)}, u32[]{:S(2)}, u32[]{:S(2)}) collective-permute-start(bf16[512,128]{1,0:T(8,128)(2,1)S(1)} %get-tuple-element.27), channel_id=1, source_target_pairs={{0,16},{16,32},{32,48},{48,0},{1,17},{17,33},{33,49},{49,1},{2,18}... | collective-permute-start | bytes 393224 | tf_op jit(solution)/shard_map/ppermute | solution.py:297
  45.0 4.6 %collective-permute-start.2 = (bf16[512,128]{1,0:T(8,128)(2,1)S(1)}, bf16[512,128]{1,0:T(8,128)(2,1)S(1)}, u32[]{:S(2)}, u32[]{:S(2)}) collective-permute-start(bf16[512,128]{1,0:T(8,128)(2,1)S(1)} %get-tuple-element.28), channel_id=1, source_target_pairs={{0,48},{16,0},{32,16},{48,32},{1,49},{17,1},{33,17},{49,33},{2,50}... | collective-permute-start | bytes 393224 | tf_op jit(solution)/shard_map/ppermute | solution.py:297
  49.5 0.0 collective-permute-done.rest_1_
  49.6 1.3 %collective-permute-done.1.rest_2_ = bf16[512,128]{1,0:T(8,128)(2,1)S(1)} collective-permute-done((bf16[512,128]{1,0:T(8,128)(2,1)S(1)}, bf16[512,128]{1,0:T(8,128)(2,1)S(1)}, u32[]{:S(2)}, u32[]{:S(2)}) %collective-permute-start.1) | collective-permute-done | bytes 131104 | tf_op jit(solution)/shard_map/ppermute | solution.py:297
  50.9 1.2 %collective-permute-done.2.rest_3_ = bf16[512,128]{1,0:T(8,128)(2,1)S(1)} collective-permute-done((bf16[512,128]{1,0:T(8,128)(2,1)S(1)}, bf16[512,128]{1,0:T(8,128)(2,1)S(1)}, u32[]{:S(2)}, u32[]{:S(2)}) %collective-permute-start.2) | collective-permute-done | bytes 131104 | tf_op jit(solution)/shard_map/ppermute | solution.py:297
  52.0 3.2 %all-to-all-done.1.got = bf16[32,32,256]{2,1,0:T(8,128)(2,1)S(1)} async-done(((bf16[32,32,256]{2,1,0:T(8,128)(2,1)}), bf16[32,32,256]{2,1,0:T(8,128)(2,1)S(1)}, u32[]{:S(2)}, u32[]{:S(2)}) %all-to-all-start.1) | async-done | bytes 524320 | tf_op jit(solution)/shard_map/all_to_all | solution.py:258
  55.3 0.0 copy-done
  55.3 1.4 %shard_map.111 = (bf16[512,256]{1,0:T(8,128)(2,1)S(1)}, bf16[512,256]{1,0:T(8,128)(2,1)S(1)}, bf16[8,128,128]{2,1,0:T(8,128)(2,1)}, bf16[512,128]{1,0:T(8,128)(2,1)S(1)}) custom-call(bf16[32,32,256]{2,1,0:T(8,128)(2,1)S(1)} %all-to-all-done.1.got, bf16[256,512]{1,0:T(8,128)(2,1)S(1)} %copy-done, bf16[256,512]{1,0:T(8,128)(2,1)S(1)} %copy-done.1, ...), custom_call_target="tpu_custom_call" | custom-call | flops 134217728 | bytes 2490368 | tf_op jit(solution)/shard_map/pallas_call | solution.py:29
  56.6 4.3 %all-to-all-start.2 = ((bf16[8,128,128]{2,1,0:T(8,128)(2,1)}), bf16[8,128,128]{2,1,0:T(8,128)(2,1)S(1)}, u32[]{:S(2)}, u32[]{:S(2)}) async-start(bf16[8,128,128]{2,1,0:T(8,128)(2,1)} %get-tuple-element.29), calls=%async_computation.2 | async-start | bytes 524288 | tf_op jit(solution)/shard_map/all_to_all | solution.py:258
  60.9 0.0 copy-done.3
  60.9 1.1 %shard_map.112 = (bf16[256,512]{1,0:T(8,128)(2,1)}, bf16[256,512]{1,0:T(8,128)(2,1)}) custom-call(bf16[512,256]{1,0:T(8,128)(2,1)S(1)} %get-tuple-element.30.back, bf16[512,256]{1,0:T(8,128)(2,1)S(1)} %get-tuple-element.31.d_first, bf16[4,128,128]{2,1,0:T(8,128)(2,1)S(1)} %copy-done.2, bf16[4,128,128]{2,1,0:T(8,128)(2,1)S(1)} %copy-done.3), custom_call_target="tpu_custom_call" | custom-call | flops 67108864 | bytes 1310720 | tf_op jit(solution)/shard_map/pallas_call | solution.py:29
  62.0 6.1 %all-to-all-done.2.got = bf16[8,128,128]{2,1,0:T(8,128)(2,1)S(1)} async-done(((bf16[8,128,128]{2,1,0:T(8,128)(2,1)}), bf16[8,128,128]{2,1,0:T(8,128)(2,1)S(1)}, u32[]{:S(2)}, u32[]{:S(2)}) %all-to-all-start.2) | async-done | bytes 262176 | tf_op jit(solution)/shard_map/all_to_all | solution.py:258
  68.2 23.1 %all-gather = bf16[2560,128]{1,0:T(8,128)(2,1)S(1)} all-gather(bf16[640,128]{1,0:T(8,128)(2,1)S(1)} %shard_map.113), channel_id=2, replica_groups=mesh['far'=4,'zl'=2,'x'=4,'hidden'=16] {'far'}, dimensions={0}, use_global_device_ids=true | all-gather | bytes 819200 | tf_op jit(solution)/shard_map/all_gather | solution.py:325
  91.3 0.1 shard_map.114
  91.4 16.7 %all_to_all.21.got = bf16[8,640,128]{2,1,0:T(8,128)(2,1)S(1)} all-to-all(bf16[8,640,128]{2,1,0:T(8,128)(2,1)S(1)} %shard_map.114), channel_id=1, replica_groups=mesh['far'=4,'zl'=2,'x'=4,'hidden'=16] {'zl','x'}, dimensions={0} | all-to-all | bytes 2621440 | tf_op jit(solution)/shard_map/all_to_all | solution.py:258
  108.1 1.2 %shard_map.115 = (bf16[4,128,128]{2,1,0:T(8,128)(2,1)}, bf16[4,128,512]{2,1,0:T(8,128)(2,1)}, bf16[4,512,128]{2,1,0:T(8,128)(2,1)}, bf16[4,128,128]{2,1,0:T(8,128)(2,1)}) custom-call(bf16[8,640,128]{2,1,0:T(8,128)(2,1)S(1)} %all_to_all.21.got), custom_call_target="tpu_custom_call" | custom-call | bytes 2621440 | tf_op jit(solution)/shard_map/pallas_call | solution.py:29
  (8 shorter events, 0.1 us)
Async XLA Ops:
  0.6 29.6 %copy-start.5 = (bf16[4,512,128]{2,1,0:T(8,128)(2,1)S(1)}, bf16[4,512,128]{2,1,0:T(8,128)(2,1)}, u32[]{:S(2)}) copy-start(bf16[4,512,128]{2,1,0:T(8,128)(2,1)} %w3.1) | copy-start | bytes 1572868
  0.6 29.6 %copy-start.4 = (bf16[4,128,512]{2,1,0:T(8,128)(2,1)S(1)}, bf16[4,128,512]{2,1,0:T(8,128)(2,1)}, u32[]{:S(2)}) copy-start(bf16[4,128,512]{2,1,0:T(8,128)(2,1)} %w2.1) | copy-start | bytes 1572868
  30.3 25.0 %copy-start = (bf16[256,512]{1,0:T(8,128)(2,1)S(1)}, bf16[256,512]{1,0:T(8,128)(2,1)}, u32[]{:S(2)}) copy-start(bf16[256,512]{1,0:T(8,128)(2,1)} %x.1) | copy-start | bytes 786436
  30.3 25.0 %copy-start.1 = (bf16[256,512]{1,0:T(8,128)(2,1)S(1)}, bf16[256,512]{1,0:T(8,128)(2,1)}, u32[]{:S(2)}) copy-start(bf16[256,512]{1,0:T(8,128)(2,1)} %dy.1) | copy-start | bytes 786436
  32.9 22.4 %all-to-all-start.1 = ((bf16[32,32,256]{2,1,0:T(8,128)(2,1)}), bf16[32,32,256]{2,1,0:T(8,128)(2,1)S(1)}, u32[]{:S(2)}, u32[]{:S(2)}) async-start(bf16[32,32,256]{2,1,0:T(8,128)(2,1)} %get-tuple-element.24), calls=%async_computation.1 | async-start | bytes 1048576 | tf_op jit(solution)/shard_map/all_to_all | solution.py:258
  37.4 23.5 %copy-start.2 = (bf16[4,128,128]{2,1,0:T(8,128)(2,1)S(1)}, bf16[4,128,128]{2,1,0:T(8,128)(2,1)}, u32[]{:S(2)}) copy-start(bf16[4,128,128]{2,1,0:T(8,128)(2,1)} %w1.1) | copy-start | bytes 393220
  37.4 23.5 %copy-start.3 = (bf16[4,128,128]{2,1,0:T(8,128)(2,1)S(1)}, bf16[4,128,128]{2,1,0:T(8,128)(2,1)}, u32[]{:S(2)}) copy-start(bf16[4,128,128]{2,1,0:T(8,128)(2,1)} %w4.1) | copy-start | bytes 393220
  37.4 12.1 %collective-permute-start = (bf16[512,128]{1,0:T(8,128)(2,1)S(1)}, bf16[512,128]{1,0:T(8,128)(2,1)S(1)}, u32[]{:S(2)}, u32[]{:S(2)}) collective-permute-start(bf16[512,128]{1,0:T(8,128)(2,1)S(1)} %get-tuple-element.26), channel_id=1, source_target_pairs={{0,32},{16,48},{32,0},{48,16},{1,33},{17,49},{33,1},{49,17},{2,34}... | collective-permute-start | bytes 393224 | tf_op jit(solution)/shard_map/ppermute | solution.py:297
  42.5 8.4 %collective-permute-start.1 = (bf16[512,128]{1,0:T(8,128)(2,1)S(1)}, bf16[512,128]{1,0:T(8,128)(2,1)S(1)}, u32[]{:S(2)}, u32[]{:S(2)}) collective-permute-start(bf16[512,128]{1,0:T(8,128)(2,1)S(1)} %get-tuple-element.27), channel_id=1, source_target_pairs={{0,16},{16,32},{32,48},{48,0},{1,17},{17,33},{33,49},{49,1},{2,18}... | collective-permute-start | bytes 393224 | tf_op jit(solution)/shard_map/ppermute | solution.py:297
  45.0 7.1 %collective-permute-start.2 = (bf16[512,128]{1,0:T(8,128)(2,1)S(1)}, bf16[512,128]{1,0:T(8,128)(2,1)S(1)}, u32[]{:S(2)}, u32[]{:S(2)}) collective-permute-start(bf16[512,128]{1,0:T(8,128)(2,1)S(1)} %get-tuple-element.28), channel_id=1, source_target_pairs={{0,48},{16,0},{32,16},{48,32},{1,49},{17,1},{33,17},{49,33},{2,50}... | collective-permute-start | bytes 393224 | tf_op jit(solution)/shard_map/ppermute | solution.py:297
  56.6 11.5 %all-to-all-start.2 = ((bf16[8,128,128]{2,1,0:T(8,128)(2,1)}), bf16[8,128,128]{2,1,0:T(8,128)(2,1)S(1)}, u32[]{:S(2)}, u32[]{:S(2)}) async-start(bf16[8,128,128]{2,1,0:T(8,128)(2,1)} %get-tuple-element.29), calls=%async_computation.2 | async-start | bytes 524288 | tf_op jit(solution)/shard_map/all_to_all | solution.py:258
